TPU v7x, 32 devices: a whole 2x2x4 slice. The times are simulated.
32 devices in a mesh: dp: 4 (over x, core), mp: 8 (over z, y).
Axes of the slice: x: 2, y: 2, z: 4, core: 2. Of those that a mesh axis runs over, the one named last changes fastest.
Arguments:
- hidden: bfloat16 [2048, 5120], P('dp', 'mp'), may hold values from -6 to 6
- mod_table: bfloat16 [50, 2, 5120], P(None, None, 'mp'), may hold values from -3 to 3
- timestep: int32 [4], P('dp'), may hold values from 0 to 49
- head_weight: bfloat16 [5120, 64], P('mp'), may hold values from -0.078125 to 0.078125
- conv_in: bfloat16 [16, 27, 384], replicated, may hold values from -0.3125 to 0.3125
- conv_mid: bfloat16 [384, 27, 384], P('dp'), may hold values from -0.0625 to 0.0625
- patch_weight: bfloat16 [384, 1024], replicated, may hold values from -0.3125 to 0.3125
- text_emb: float32 [4, 1024], P('dp'), may hold values from -6 to 6
Outputs:
- reward: float32 [4], P('dp')
- head_grad: float32 [5120, 64], P('mp')
- hidden_grad: bfloat16 [2048, 5120], P('dp', 'mp')
Inputs may be any that keep to these rules, and one draw needn't show every extreme that they name: One timestep index a video.
All inputs are finite; a program needn't handle non-finite values.
Results may differ from a plain program's by a relative error of at most 0.029.
Values may be sent and summed in bfloat16 or wider, within the bound.
No kernel may reach another device: no remote copies, remote signals or barrier semaphores. Data moves between devices by JAX's collectives and lax.ppermute only.
A program may use at most 64 MiB of HBM per device.

v0:
```python
import jax
import jax.numpy as jnp
from jax import lax
from jax.sharding import PartitionSpec as P

LW = 64
LT = 2


def with_halo(block, sides, width):
    for axis, dim in sides:
        count = lax.axis_size(axis)
        forward = [(i, i + 1) for i in range(count - 1)]
        backward = [(target, source) for source, target in forward]
        low = lax.ppermute(
            lax.slice_in_dim(block, block.shape[dim] - width, None, axis=dim), axis, forward
        )
        high = lax.ppermute(lax.slice_in_dim(block, 0, width, axis=dim), axis, backward)
        block = jnp.concatenate([low, block, high], axis=dim)
    return block


def silu_slope(value):
    gate = jax.nn.sigmoid(value)
    return gate * (1.0 + value * (1.0 - gate))


def scoring(pooled, video_text, patch_weight):
    embedded = jnp.dot(pooled, patch_weight.astype(jnp.float32), precision=lax.Precision.HIGHEST)
    embed_length = jnp.sqrt(jnp.sum(embedded * embedded, axis=1) + 1e-06)
    text_length = jnp.sqrt(jnp.sum(video_text * video_text) + 1e-06)
    cosine = jnp.dot(embedded, video_text, precision=lax.Precision.HIGHEST) / (
        embed_length * text_length
    )
    return 100.0 * jnp.mean(cosine)


def make_views(rimmed, rows, reverse_time):
    time_pad = (0, 2) if reverse_time else (2, 0)
    padded = jnp.pad(rimmed, (time_pad, (0, 0), (1, 1), (0, 0)))
    frames, cols = (rimmed.shape[0], rimmed.shape[2])
    views = []
    for tap_index in range(27):
        step_time, step_rows, step_cols = (tap_index // 9, tap_index // 3 % 3, tap_index % 3)
        views.append(
            padded[
                step_time : step_time + frames,
                step_rows : step_rows + rows,
                step_cols : step_cols + cols,
            ]
        )
    return views


def backward_views(field):
    rimmed = with_halo(field, (("mp", 1),), 1)
    return make_views(rimmed, field.shape[1], True)


def forward_views(field):
    rimmed = with_halo(field, (("mp", 1),), 1)
    return make_views(rimmed, field.shape[1], False)


def forward_full(views, weight):
    summed = jnp.zeros(views[0].shape[:3] + (weight.shape[2],), jnp.float32)
    for tap_index in range(27):
        summed = summed + jnp.einsum(
            "thwi,io->thwo",
            views[tap_index],
            weight[:, tap_index, :],
            preferred_element_type=jnp.float32,
        )
    return summed


def backward_full(views, weight):
    summed = jnp.zeros(views[0].shape[:3] + (weight.shape[0],), jnp.float32)
    for tap_index in range(27):
        summed = summed + jnp.einsum(
            "thwo,io->thwi",
            views[tap_index],
            weight[:, 26 - tap_index, :],
            preferred_element_type=jnp.float32,
        )
    return summed


def body(hidden, mod_table, timestep, head_weight, conv_in, conv_mid, patch_weight, text_emb):
    steps_total = mod_table.shape[0]
    selector = (jnp.arange(steps_total, dtype=jnp.int32) == timestep[0]).astype(jnp.float32)
    modulation = jnp.einsum(
        "s,skd->kd", selector, mod_table.astype(jnp.float32), precision=lax.Precision.HIGHEST
    )
    gain = 1.0 + modulation[1]
    modulated = (hidden.astype(jnp.float32) * gain + modulation[0]).astype(jnp.bfloat16)
    head_terms = jnp.dot(modulated, head_weight, preferred_element_type=jnp.float32)
    features = head_weight.shape[1]
    channels = features // 4
    video_tokens = hidden.shape[0]
    pair_cols = LW // 2
    pair_rows = video_tokens // (LT * pair_cols)
    latent_grid = head_terms.reshape(LT, pair_rows, pair_cols, features)
    narrow = lax.psum_scatter(
        latent_grid.astype(jnp.bfloat16), "mp", scatter_dimension=2, tiled=True
    )
    tile_rows = lax.all_to_all(narrow, "mp", split_axis=1, concat_axis=2, tiled=True)
    local_pairs = tile_rows.shape[1]
    local_rows = 2 * local_pairs
    latent = (
        tile_rows.reshape(LT, local_pairs, pair_cols, 2, 2, channels)
        .transpose(0, 1, 3, 2, 4, 5)
        .reshape(LT, local_rows, LW, channels)
    )
    pre_first = forward_full(forward_views(latent), conv_in)
    act_first = jax.nn.silu(pre_first).astype(jnp.bfloat16)
    mid_views = forward_views(act_first)
    gathered = lax.all_gather(conv_mid, "dp", axis=0, tiled=True)
    pre_second = forward_full(mid_views, gathered)
    decoded = jax.nn.silu(pre_second).astype(jnp.bfloat16)
    frame_sums = jnp.sum(decoded, axis=(1, 2), dtype=jnp.float32)
    cell_count = 2 * pair_rows * LW
    pooled = lax.psum(frame_sums, "mp") / cell_count
    video_text = text_emb[0]
    reward, pullback = jax.vjp(lambda pool_in: scoring(pool_in, video_text, patch_weight), pooled)
    pool_grad = pullback(jnp.ones((), jnp.float32))[0]
    grad_second = (pool_grad[:, None, None, :] / cell_count * silu_slope(pre_second)).astype(
        jnp.bfloat16
    )
    second_views = backward_views(grad_second)
    grad_act = backward_full(second_views, gathered)
    grad_first = (grad_act * silu_slope(pre_first)).astype(jnp.bfloat16)
    latent_grad = backward_full(backward_views(grad_first), conv_in).astype(jnp.bfloat16)
    full_grad = lax.all_gather(latent_grad, "mp", axis=1, tiled=True)
    token_grad = (
        full_grad.reshape(LT, pair_rows, 2, pair_cols, 2, channels)
        .transpose(0, 1, 3, 2, 4, 5)
        .reshape(video_tokens, features)
    )
    hidden_grad = (
        jnp.dot(token_grad, head_weight.T, preferred_element_type=jnp.float32) * gain
    ).astype(jnp.bfloat16)
    head_local = jnp.einsum("sd,sf->df", modulated, token_grad, preferred_element_type=jnp.float32)
    head_grad = lax.psum(head_local.astype(jnp.bfloat16), "dp").astype(jnp.float32)
    return (reward.reshape(1), head_grad, hidden_grad)


def solution(mesh):
    in_specs = (
        P("dp", "mp"),
        P(None, None, "mp"),
        P("dp"),
        P("mp", None),
        P(),
        P("dp", None, None),
        P(),
        P("dp", None),
    )
    out_specs = (P("dp"), P("mp", None), P("dp", "mp"))
    return jax.shard_map(body, mesh=mesh, in_specs=in_specs, out_specs=out_specs, check_vma=False)
```

profile of v0, /device:TPU:0, one launch (start us, length us, event | category | flops | bytes accessed | tf_op | source)
XLA Modules:
  0.0 261.6 jit_solution(13927650747533604210)
XLA Ops:
  8.8 1.1 fusion.124
  9.9 1.4 convolution_convert_fusion.1
  11.4 0.7 copy.23
  12.2 0.5 all-gather.2.cloned.1.call-update
  12.8 0.9 fusion.260
  13.6 0.9 convolution_add_fusion.21
  14.5 0.9 convolution_add_fusion.20
  15.4 0.9 convolution_add_fusion.19
  16.3 0.9 convolution_add_fusion.18
  17.2 0.9 convolution_add_fusion.17
  18.5 57.8 %reduce-scatter.2.cloned.1.call-done = bf16[2,8,4,64]{3,1,0,2:T(8,128)(2,1)} async-done(((bf16[2,8,32,64]{3,1,0,2:T(8,128)(2,1)}), bf16[2,8,4,64]{3,1,0,2:T(8,128)(2,1)}) %reduce-scatter.2.cloned.1.call-update) | async-done | bytes 8208 | tf_op jit(solution)/shard_map/reduce_scatter | solution.py:104
  76.3 0.7 copy.97
  77.1 0.7 reshape.94
  77.7 3.6 %all-to-all-start = ((bf16[8,2,256]{2,1,0:T(2,128)(2,1)}), bf16[8,2,256]{2,1,0:T(2,128)(2,1)S(1)}, u32[]{:S(2)}, u32[]{:S(2)}) async-start(bf16[8,2,256]{2,1,0:T(2,128)(2,1)} %reshape.94), calls=%async_computation.1 | async-start | bytes 16384 | tf_op jit(solution)/shard_map/all_to_all | solution.py:107
  81.6 6.3 %all-to-all-done = bf16[8,2,256]{2,1,0:T(2,128)(2,1)S(1)} async-done(((bf16[8,2,256]{2,1,0:T(2,128)(2,1)}), bf16[8,2,256]{2,1,0:T(2,128)(2,1)S(1)}, u32[]{:S(2)}, u32[]{:S(2)}) %all-to-all-start) | async-done | bytes 8224 | tf_op jit(solution)/shard_map/all_to_all | solution.py:107
  88.2 2.4 collective-permute-start
  90.7 1.3 collective-permute-start.1
  92.2 4.1 %collective-permute-done.1 = bf16[2,1,64,16]{2,3,1,0:T(8,128)(2,1)S(1)} collective-permute-done((bf16[2,1,64,16]{2,3,1,0:T(8,128)(2,1)S(1)}, bf16[2,1,64,16]{2,3,1,0:T(8,128)(2,1)S(1)}, u32[]{:S(2)}, u32[]{:S(2)}) %collective-permute-start.1) | collective-permute-done | bytes 4128 | tf_op jit(solution)/shard_map/ppermute | solution.py:18
  97.4 0.3 convolution_add_fusion.12
  98.6 0.3 convolution_add_fusion.8
  99.2 0.3 convolution_add_fusion.6
  99.5 0.3 convolution_add_fusion.5
  101.2 4.3 %collective-permute-start.2 = (bf16[2,1,64,384]{3,2,1,0:T(8,128)(2,1)S(1)}, bf16[2,1,64,384]{3,2,1,0:T(8,128)(2,1)S(1)}, u32[]{:S(2)}, u32[]{:S(2)}) collective-permute-start(bf16[2,1,64,384]{3,2,1,0:T(8,128)(2,1)S(1)} %get-tuple-element.9), channel_id=1, source_target_pairs={{0,1},{1,2},{2,3},{3,4},{4,5},{5,6},{6,7},{8,9},{9,10},{10,11},{11... | collective-permute-start | bytes 294920 | tf_op jit(solution)/shard_map/ppermute | solution.py:15
  105.5 1.3 collective-permute-start.3
  106.8 0.6 multiply_reduce_fusion.1
  108.1 3.9 %collective-permute-done.3 = bf16[2,1,64,384]{3,2,1,0:T(8,128)(2,1)S(1)} collective-permute-done((bf16[2,1,64,384]{3,2,1,0:T(8,128)(2,1)S(1)}, bf16[2,1,64,384]{3,2,1,0:T(8,128)(2,1)S(1)}, u32[]{:S(2)}, u32[]{:S(2)}) %collective-permute-start.3) | collective-permute-done | bytes 98336 | tf_op jit(solution)/shard_map/ppermute | solution.py:18
  112.2 1.4 fusion.65
  113.6 1.5 fusion.68
  115.1 1.2 fusion.69
  116.4 1.2 fusion.73
  117.6 1.2 convolution_add_fusion.66
  118.8 1.2 convolution_add_fusion.65
  120.1 1.2 convolution_add_fusion.64
  121.3 1.2 convolution_add_fusion.63
  122.6 1.2 convolution_add_fusion.62
  128.5 0.4 convert_reduce_fusion
  128.9 18.2 %psum.14 = f32[2,384]{1,0:T(2,128)S(1)} all-reduce(f32[2,384]{1,0:T(2,128)S(1)} %get-tuple-element.18), channel_id=1, replica_groups=mesh['dp'=4,'mp'=8] {'mp'}, use_global_device_ids=true, to_apply=%region_2.3 | all-reduce | flops 768 | bytes 6144 | tf_op jit(solution)/shard_map/psum | solution.py:123
  147.1 0.5 multiply_reduce_fusion
  147.7 0.8 divide_multiply_fusion
  148.5 0.7 convolution_multiply_fusion.1
  149.4 2.8 %collective-permute-start.4 = (bf16[2,1,64,384]{3,2,1,0:T(8,128)(2,1)S(1)}, bf16[2,1,64,384]{3,2,1,0:T(8,128)(2,1)S(1)}, u32[]{:S(2)}, u32[]{:S(2)}) collective-permute-start(bf16[2,1,64,384]{3,2,1,0:T(8,128)(2,1)S(1)} %get-tuple-element.7), channel_id=1, source_target_pairs={{0,1},{1,2},{2,3},{3,4},{4,5},{5,6},{6,7},{8,9},{9,10},{10,11},{11... | collective-permute-start | bytes 294920 | tf_op jit(solution)/shard_map/ppermute | solution.py:15
  152.2 1.5 collective-permute-start.5
  153.7 0.7 collective-permute-done.4
  154.4 4.3 %collective-permute-done.5 = bf16[2,1,64,384]{3,2,1,0:T(8,128)(2,1)S(1)} collective-permute-done((bf16[2,1,64,384]{3,2,1,0:T(8,128)(2,1)S(1)}, bf16[2,1,64,384]{3,2,1,0:T(8,128)(2,1)S(1)}, u32[]{:S(2)}, u32[]{:S(2)}) %collective-permute-start.5) | collective-permute-done | bytes 98336 | tf_op jit(solution)/shard_map/ppermute | solution.py:18
  158.9 1.3 fusion.70
  160.1 1.3 fusion.71
  161.4 1.2 fusion.72
  162.7 1.3 fusion.67
  163.9 1.2 fusion.66
  165.2 1.4 fusion.21
  166.6 1.3 convolution_add_fusion.45
  167.9 1.3 convolution_add_fusion.44
  169.1 1.3 convolution_add_fusion.43
  170.4 1.3 fusion.23
  176.5 0.3 fusion.26
  176.8 2.8 %collective-permute-start.6 = (bf16[2,1,64,384]{3,2,1,0:T(8,128)(2,1)S(1)}, bf16[2,1,64,384]{3,2,1,0:T(8,128)(2,1)S(1)}, u32[]{:S(2)}, u32[]{:S(2)}) collective-permute-start(bf16[2,1,64,384]{3,2,1,0:T(8,128)(2,1)S(1)} %get-tuple-element.5), channel_id=1, source_target_pairs={{0,1},{1,2},{2,3},{3,4},{4,5},{5,6},{6,7},{8,9},{9,10},{10,11},{11... | collective-permute-start | bytes 294920 | tf_op jit(solution)/shard_map/ppermute | solution.py:15
  179.7 1.3 collective-permute-start.7
  181.9 4.5 %collective-permute-done.7 = bf16[2,1,64,384]{3,2,1,0:T(8,128)(2,1)S(1)} collective-permute-done((bf16[2,1,64,384]{3,2,1,0:T(8,128)(2,1)S(1)}, bf16[2,1,64,384]{3,2,1,0:T(8,128)(2,1)S(1)}, u32[]{:S(2)}, u32[]{:S(2)}) %collective-permute-start.7) | collective-permute-done | bytes 98336 | tf_op jit(solution)/shard_map/ppermute | solution.py:18
  191.7 30.6 %all_gather.7 = bf16[2,16,64,16]{2,3,1,0:T(8,128)(2,1)S(1)} all-gather(bf16[2,2,64,16]{2,3,1,0:T(8,128)(2,1)S(1)} %fusion.31), channel_id=1, replica_groups=mesh['dp'=4,'mp'=8] {'mp'}, dimensions={1}, use_global_device_ids=true | all-gather | bytes 73728 | tf_op jit(solution)/shard_map/all_gather | solution.py:134
  222.5 0.5 copy.34
  223.3 0.9 convolution_convert_fusion
  224.2 1.2 fusion.13
  225.4 26.1 %all-reduce.6.cloned.1.call-done = bf16[640,64]{0,1:T(8,128)(2,1)} async-done(((bf16[640,64]{0,1:T(8,128)(2,1)}), bf16[640,64]{0,1:T(8,128)(2,1)}) %all-reduce.6.cloned.1.call-update) | async-done | bytes 81936 | tf_op jit(solution)/shard_map/psum | solution.py:144
  251.5 1.6 convert_element_type.60
  (122 shorter events, 20.9 us)
Async XLA Ops:
  8.0 139.1 %copy-start = (bf16[384,1024]{1,0:T(8,128)(2,1)S(1)}, bf16[384,1024]{1,0:T(8,128)(2,1)}, u32[]{:S(2)}) copy-start(bf16[384,1024]{1,0:T(8,128)(2,1)} %param.14) | copy-start | bytes 2359300
  8.0 10.1 %copy-start.2 = (bf16[16,27,384]{2,0,1:T(8,128)(2,1)S(1)}, bf16[16,27,384]{2,0,1:T(8,128)(2,1)}, u32[]{:S(2)}) copy-start(bf16[16,27,384]{2,0,1:T(8,128)(2,1)} %param.12) | copy-start | bytes 995332
  8.0 68.3 %reduce-scatter.2.cloned.1.call-start = ((), (), s32[]{:S(2)}) async-start(), calls=%async_computation.3 | async-start | bytes 147456 | tf_op jit(solution)/shard_map/reduce_scatter | solution.py:104
  12.2 100.0 %all-gather.2.cloned.1.call-start = ((), (), s32[]{:S(2)}) async-start(), calls=%async_computation.2 | async-start | bytes 9953280 | tf_op jit(solution)/shard_map/all_gather | solution.py:118
  77.7 10.1 %all-to-all-start = ((bf16[8,2,256]{2,1,0:T(2,128)(2,1)}), bf16[8,2,256]{2,1,0:T(2,128)(2,1)S(1)}, u32[]{:S(2)}, u32[]{:S(2)}) async-start(bf16[8,2,256]{2,1,0:T(2,128)(2,1)} %reshape.94), calls=%async_computation.1 | async-start | bytes 16384 | tf_op jit(solution)/shard_map/all_to_all | solution.py:107
  81.4 170.1 %all-reduce.6.cloned.1.call-start = ((), (), s32[]{:S(2)}) async-start(), calls=%async_computation.4 | async-start | bytes 163840 | tf_op jit(solution)/shard_map/psum | solution.py:144
  88.2 18.6 %copy-start.4 = (f32[1,1024]{1,0:T(1,128)S(1)}, f32[1,1024]{1,0:T(1,128)}, u32[]{:S(2)}) copy-start(f32[1,1024]{1,0:T(1,128)} %param.15) | copy-start | bytes 12292
  88.2 3.9 %collective-permute-start = (bf16[2,1,64,16]{2,3,1,0:T(8,128)(2,1)S(1)}, bf16[2,1,64,16]{2,3,1,0:T(8,128)(2,1)S(1)}, u32[]{:S(2)}, u32[]{:S(2)}) collective-permute-start(bf16[2,1,64,16]{2,3,1,0:T(8,128)(2,1)S(1)} %get-tuple-element.11), channel_id=1, source_target_pairs={{0,1},{1,2},{2,3},{3,4},{4,5},{5,6},{6,7},{8,9},{9,10},{10,11},{11... | collective-permute-start | bytes 12296 | tf_op jit(solution)/shard_map/ppermute | solution.py:15
  90.7 5.5 %collective-permute-start.1 = (bf16[2,1,64,16]{2,3,1,0:T(8,128)(2,1)S(1)}, bf16[2,1,64,16]{2,3,1,0:T(8,128)(2,1)S(1)}, u32[]{:S(2)}, u32[]{:S(2)}) collective-permute-start(bf16[2,1,64,16]{2,3,1,0:T(8,128)(2,1)S(1)} %get-tuple-element.12), channel_id=1, source_target_pairs={{1,0},{2,1},{3,2},{4,3},{5,4},{6,5},{7,6},{9,8},{10,9},{11,10},{12... | collective-permute-start | bytes 12296 | tf_op jit(solution)/shard_map/ppermute | solution.py:18
  101.2 6.9 %collective-permute-start.2 = (bf16[2,1,64,384]{3,2,1,0:T(8,128)(2,1)S(1)}, bf16[2,1,64,384]{3,2,1,0:T(8,128)(2,1)S(1)}, u32[]{:S(2)}, u32[]{:S(2)}) collective-permute-start(bf16[2,1,64,384]{3,2,1,0:T(8,128)(2,1)S(1)} %get-tuple-element.9), channel_id=1, source_target_pairs={{0,1},{1,2},{2,3},{3,4},{4,5},{5,6},{6,7},{8,9},{9,10},{10,11},{11... | collective-permute-start | bytes 294920 | tf_op jit(solution)/shard_map/ppermute | solution.py:15
  105.5 6.5 %collective-permute-start.3 = (bf16[2,1,64,384]{3,2,1,0:T(8,128)(2,1)S(1)}, bf16[2,1,64,384]{3,2,1,0:T(8,128)(2,1)S(1)}, u32[]{:S(2)}, u32[]{:S(2)}) collective-permute-start(bf16[2,1,64,384]{3,2,1,0:T(8,128)(2,1)S(1)} %get-tuple-element.10), channel_id=1, source_target_pairs={{1,0},{2,1},{3,2},{4,3},{5,4},{6,5},{7,6},{9,8},{10,9},{11,10},{12... | collective-permute-start | bytes 294920 | tf_op jit(solution)/shard_map/ppermute | solution.py:18
  112.2 11.6 %copy-start.1 = (bf16[384,27,384]{2,0,1:T(8,128)(2,1)S(1)}, bf16[384,27,384]{2,0,1:T(8,128)(2,1)}, u32[]{:S(2)}) copy-start(bf16[384,27,384]{2,0,1:T(8,128)(2,1)} %all-gather.2.cloned.1.call-done) | copy-start | bytes 23887876
  147.7 24.0 %slice-start = ((s8[7962624]{0:T(1024)(128)(4,1)}), s8[3768320]{0:T(1024)(128)(4,1)S(1)}, s32[]{:S(2)}) async-start(s8[7962624]{0:T(1024)(128)(4,1)} %bitcast.496), calls=%async_computation.5 | async-start | bytes 7536640
  149.4 5.0 %collective-permute-start.4 = (bf16[2,1,64,384]{3,2,1,0:T(8,128)(2,1)S(1)}, bf16[2,1,64,384]{3,2,1,0:T(8,128)(2,1)S(1)}, u32[]{:S(2)}, u32[]{:S(2)}) collective-permute-start(bf16[2,1,64,384]{3,2,1,0:T(8,128)(2,1)S(1)} %get-tuple-element.7), channel_id=1, source_target_pairs={{0,1},{1,2},{2,3},{3,4},{4,5},{5,6},{6,7},{8,9},{9,10},{10,11},{11... | collective-permute-start | bytes 294920 | tf_op jit(solution)/shard_map/ppermute | solution.py:15
  152.2 6.5 %collective-permute-start.5 = (bf16[2,1,64,384]{3,2,1,0:T(8,128)(2,1)S(1)}, bf16[2,1,64,384]{3,2,1,0:T(8,128)(2,1)S(1)}, u32[]{:S(2)}, u32[]{:S(2)}) collective-permute-start(bf16[2,1,64,384]{3,2,1,0:T(8,128)(2,1)S(1)} %get-tuple-element.8), channel_id=1, source_target_pairs={{1,0},{2,1},{3,2},{4,3},{5,4},{6,5},{7,6},{9,8},{10,9},{11,10},{12... | collective-permute-start | bytes 294920 | tf_op jit(solution)/shard_map/ppermute | solution.py:18
  165.2 6.5 %slice-start.1 = ((s8[7962624]{0:T(1024)(128)(4,1)}), s8[4194304]{0:T(1024)(128)(4,1)S(1)}, s32[]{:S(2)}) async-start(s8[7962624]{0:T(1024)(128)(4,1)} %bitcast.496), calls=%async_computation.6 | async-start | bytes 8388608
  175.9 47.4 %copy-start.5 = (bf16[512,640]{1,0:T(8,128)(2,1)S(1)}, bf16[512,640]{1,0:T(8,128)(2,1)}, u32[]{:S(2)}) copy-start(bf16[512,640]{1,0:T(8,128)(2,1)} %param.8) | copy-start | bytes 1966084
  176.2 48.1 %copy-start.3 = (bf16[640,64]{0,1:T(8,128)(2,1)S(1)}, bf16[640,64]{0,1:T(8,128)(2,1)}, u32[]{:S(2)}) copy-start(bf16[640,64]{0,1:T(8,128)(2,1)} %param.11) | copy-start | bytes 245764
  176.8 5.0 %collective-permute-start.6 = (bf16[2,1,64,384]{3,2,1,0:T(8,128)(2,1)S(1)}, bf16[2,1,64,384]{3,2,1,0:T(8,128)(2,1)S(1)}, u32[]{:S(2)}, u32[]{:S(2)}) collective-permute-start(bf16[2,1,64,384]{3,2,1,0:T(8,128)(2,1)S(1)} %get-tuple-element.5), channel_id=1, source_target_pairs={{0,1},{1,2},{2,3},{3,4},{4,5},{5,6},{6,7},{8,9},{9,10},{10,11},{11... | collective-permute-start | bytes 294920 | tf_op jit(solution)/shard_map/ppermute | solution.py:15
  179.7 6.7 %collective-permute-start.7 = (bf16[2,1,64,384]{3,2,1,0:T(8,128)(2,1)S(1)}, bf16[2,1,64,384]{3,2,1,0:T(8,128)(2,1)S(1)}, u32[]{:S(2)}, u32[]{:S(2)}) collective-permute-start(bf16[2,1,64,384]{3,2,1,0:T(8,128)(2,1)S(1)} %get-tuple-element.6), channel_id=1, source_target_pairs={{1,0},{2,1},{3,2},{4,3},{5,4},{6,5},{7,6},{9,8},{10,9},{11,10},{12... | collective-permute-start | bytes 294920 | tf_op jit(solution)/shard_map/ppermute | solution.py:18
Sparse Core Ops, SparseCore 0:
  12.7 63.5 reduce-scatter.1
Sparse Core Ops, SparseCore 1:
  14.2 58.4 all-gather.1
  224.3 27.1 all-reduce.5
where the time goes:
time: 263 us; the launch traced here: 262 us
  waiting for transfers between devices  109 us (41%)
  matrix products  56.7 us (22%)
  blocking collectives  48.8 us (19%)
  starting transfers between devices  21.4 us (8%)
  between operations  19.6 us (7%)
  local copies, waits for them, and re-layouts  3.66 us (1%)
  other arithmetic  2.92 us (1%)
    reduce_scatter x1, waiting for transfers between devices, body(): lax.psum_scatter(latent_grid.astype(jnp.bfloat16), 'mp', scatter_dimensio...  57.8 us
    all_gather x1, blocking collectives, body(): full_grad = lax.all_gather(latent_grad, 'mp', axis=1, tiled=True)  30.6 us
    dot_general x54, matrix products, forward_full(): jnp.einsum('thwi,io->thwo', views[tap_index], weight[:, tap_index, :], pr...  27.2 us
    psum x1, waiting for transfers between devices, body(): lax.psum(head_local.astype(jnp.bfloat16), 'dp').astype(jnp.float32)  26.1 us
    dot_general x54, matrix products, backward_full(): jnp.einsum('thwo,io->thwi', views[tap_index], weight[:, 26 - tap_index, :...  22.8 us
    psum x1, blocking collectives, body(): pooled = lax.psum(frame_sums, 'mp') / cell_count  18.2 us
    ppermute x4, waiting for transfers between devices, with_halo(): lax.ppermute(lax.slice_in_dim(block, 0, width, axis=dim), axis, backward)  16.8 us
    ppermute x4, starting transfers between devices, with_halo(): lax.ppermute(lax.slice_in_dim(block, block.shape[dim] - width, None, axis...  12.3 us
  transfers between devices with their start and end apart: 12, of which 9 were waited for; matrix products, arithmetic and copies ran while one was open for 6% of the time, Pallas kernels for 0%

commit v1 on v0

v1 whole, which is shorter than its diff:
```python
import functools

import jax
import jax.numpy as jnp
import numpy as np
from jax import lax
from jax.experimental import pallas as pl
from jax.experimental.pallas import tpu as pltpu
from jax.sharding import PartitionSpec as P

LW = 64
LT = 2
DEEP = 256
TILE = 128
PAIR_COLS = LW // 2
BF = jnp.bfloat16
F32 = jnp.float32
MIB = 1024 * 1024


def params(mib):
    return pltpu.CompilerParams(vmem_limit_bytes=mib * MIB)


def sigmoid(value):
    return 1.0 / (1.0 + jnp.exp(-value))


def dot(left, right):
    return jnp.dot(left, right, preferred_element_type=F32)


def dot_nt(left, right):
    return lax.dot_general(left, right, (((1,), (1,)), ((), ())), preferred_element_type=F32)


def selection(channels):
    pick = np.zeros((3, 3, 2, 2, channels, 4, 4, channels), np.float32)
    for pair_row in range(3):
        for row in range(2):
            patch_row = 2 * (pair_row - 1) + row + 1
            for pair_col in range(3):
                for col in range(2):
                    patch_col = 2 * (pair_col - 1) + col + 1
                    if 0 <= patch_row < 4 and 0 <= patch_col < 4:
                        for k in range(channels):
                            pick[pair_row, pair_col, row, col, k, patch_row, patch_col, k] = 1.0
    return pick.reshape(36 * channels, 16 * channels).astype(BF)


def pack_kernel(taps_hbm, packed_ref, taps, sem):
    count = taps.shape[0]
    copy = pltpu.make_async_copy(taps_hbm.at[pl.ds(taps_hbm.shape[0] - count, count)], taps, sem)
    copy.start()
    copy.wait()
    odd = lax.axis_index("mp") % 2
    lane = lax.broadcasted_iota(jnp.int32, (taps.shape[1], TILE), 1)
    for side in range(2):

        @pl.when(odd == side)
        def _():
            for pair in range(count // 2):
                first, second = taps[2 * pair], taps[2 * pair + 1]
                packed_ref[pair, :, :TILE] = first[:, side * TILE : (side + 1) * TILE]
                packed_ref[pair, :, TILE : 2 * TILE] = second[:, side * TILE : (side + 1) * TILE]
                left, right = first[:, 2 * TILE :].astype(F32), second[:, 2 * TILE :].astype(F32)
                if side == 0:
                    right = pltpu.roll(right, TILE // 2, 1)
                else:
                    left = pltpu.roll(left, TILE // 2, 1)
                packed_ref[pair, :, 2 * TILE :] = jnp.where(lane < TILE // 2, left, right).astype(BF)


def head_kernel(
    parts, step_hbm, hidden_hbm, mod_hbm, head_hbm, modulated_ref, gain_ref, send_ref, step_ref, hidden_ref, mod_ref,
    head_ref, sems
):
    copies = [
        pltpu.make_async_copy(hidden_hbm, hidden_ref, sems.at[0]),
        pltpu.make_async_copy(mod_hbm, mod_ref, sems.at[1]),
        pltpu.make_async_copy(head_hbm, head_ref, sems.at[2]),
        pltpu.make_async_copy(step_hbm, step_ref, sems.at[3]),
    ]
    for copy in copies:
        copy.start()
    for copy in copies:
        copy.wait()
    mod = mod_ref[step_ref[0]].astype(F32)
    gain = 1.0 + mod[1:2]
    modulated = (hidden_ref[...].astype(F32) * gain + mod[0:1]).astype(BF)
    modulated_ref[...] = modulated
    gain_ref[...] = gain
    terms = dot_nt(modulated, head_ref[...])
    half = terms.shape[0] // 2
    wide = jnp.concatenate([terms[:half], terms[half:]], axis=1)
    n = PAIR_COLS
    blank = jnp.zeros((n, wide.shape[1]), F32)
    lower = lax.broadcasted_iota(jnp.int32, blank.shape, 1) // (wide.shape[1] // 4) % 2 == 1

    def pair_row(i):
        return blank if i < 0 or i >= parts else wide[i * n : (i + 1) * n]

    for part in range(0, parts, 2):
        outer = jnp.where(lower, pair_row(part - 2), pair_row(part + 3))
        rows = [pair_row(part + i) for i in range(-1, 3)] + [outer]
        block = jnp.concatenate(rows, axis=0).astype(BF)
        send_ref[part] = block
        send_ref[part + 1] = block


def build_patch_weights(conv_ref, patch_w):
    channels, width = conv_ref.shape[1], conv_ref.shape[2]
    patch_w[...] = jnp.zeros_like(patch_w)
    for a in range(2):
        for b in range(3):
            for c in range(3):
                tap = conv_ref[9 * a + 3 * b + c]
                for r in range(2):
                    for s in range(2):
                        row = ((r + b) * 4 + s + c) * channels
                        col = (2 * r + s) * width
                        patch_w[a, row : row + channels, col : col + width] = tap


def weight_copies(refs, weights, sems):
    rows = refs[0].shape[1]
    return [
        pltpu.make_async_copy(ref, weights.at[:, pl.ds(i * rows, rows), :], sems.at[i]) for i, ref in enumerate(refs)
    ]


def tap_weights(refs, tap):
    pair, side = tap // 2, tap % 2
    blocks = []
    for ref in refs:
        half = ref[pair, :, 2 * TILE :]
        lane = lax.broadcasted_iota(jnp.int32, half.shape, 1)
        half = jnp.where((lane < TILE // 2) == (side == 0), half, jnp.zeros_like(half))
        blocks.append(jnp.concatenate([ref[pair, :, side * TILE : (side + 1) * TILE], half], axis=1))
    filled = sum(block.shape[0] for block in blocks)
    return jnp.concatenate(blocks + [jnp.zeros((DEEP - filled, 2 * TILE), BF)], axis=0)


def store_views(views, t, row, even, odd, odd_down, even_up):
    n, deep = PAIR_COLS, even.shape[1]
    for c, (at_even, at_odd) in enumerate(((odd_down, even), (even, odd), (odd, even_up))):
        views[t, row, 0:n, c * deep : (c + 1) * deep] = at_even
        views[t, row, n : 2 * n, c * deep : (c + 1) * deep] = at_odd


def shift_down(value):
    place = lax.broadcasted_iota(jnp.int32, value.shape, 0) % PAIR_COLS
    return jnp.where(place == 0, 0.0, pltpu.roll(value, 1, 0))


def shift_up(value):
    place = lax.broadcasted_iota(jnp.int32, value.shape, 0) % PAIR_COLS
    return jnp.where(place == PAIR_COLS - 1, 0.0, pltpu.roll(value, value.shape[0] - 1, 0))


def near_kernel(parts, blocks, info_ref, recv_ref, conv_ref, pick_ref, *refs):
    acc, far_views, slope_ref, weights, patch_w, views, sems = refs[blocks:]
    copies = weight_copies(refs[:blocks], weights, sems)
    for copy in copies:
        copy.start()
    n = PAIR_COLS
    width = conv_ref.shape[2]
    build_patch_weights(conv_ref, patch_w)

    latent = recv_ref[0].astype(F32)
    for part in range(1, parts):
        latent = latent + recv_ref[part].astype(F32)
    latent = latent.astype(BF).astype(F32)
    left, right = shift_down(latent), shift_up(latent)
    half = latent.shape[1] // 2
    stacked = []
    for t in range(LT):
        lanes = slice(t * half, (t + 1) * half)
        cols = jnp.concatenate([left[:, lanes], latent[:, lanes], right[:, lanes]], axis=1)
        above = jnp.concatenate([cols[4 * n :], cols[: 3 * n]], axis=0)
        stacked.append(jnp.concatenate([above, cols[: 4 * n], cols[n:]], axis=1))
    patches = dot(jnp.concatenate(stacked, axis=0).astype(BF), pick_ref[...]).astype(BF)

    top_scale, bottom_scale = edge_scales(parts, info_ref[0])
    group = lax.broadcasted_iota(jnp.int32, (8 * n, 1), 0) // n % 4
    scale = jnp.where(group == 0, top_scale, jnp.where(group == 3, bottom_scale, 1.0))
    for r in range(2):
        lanes = slice(2 * r * width, (2 * r + 2) * width)
        pre = dot(patches, patch_w[1, :, lanes])
        late = dot(patches[: 4 * n], patch_w[0, :, lanes])
        pre = jnp.concatenate([pre[: 4 * n], pre[4 * n :] + late], axis=0)
        gate = sigmoid(pre)
        act = pre * gate * scale
        even, odd = act[:, :width], act[:, width:]
        odd_down, even_up = shift_down(odd).astype(BF), shift_up(even).astype(BF)
        even, odd = even.astype(BF), odd.astype(BF)
        for t in range(LT):
            for g in range(4):
                at = slice((4 * t + g) * n, (4 * t + g + 1) * n)
                for target, lanes in ((views, slice(0, DEEP)), (far_views, slice(DEEP, 2 * DEEP))):
                    store_views(
                        target, t, 2 * g + r, even[at, lanes], odd[at, lanes], odd_down[at, lanes], even_up[at, lanes]
                    )
            for g in (1, 2):
                at = slice((4 * t + g) * n, (4 * t + g + 1) * n)
                own, own_gate = pre[at], gate[at]
                slope = own_gate * (1.0 + own * (1.0 - own_gate))
                base = (4 * t + 2 * (g - 1) + r) * 2 * n
                slope_ref[base : base + n, :] = slope[:, :width]
                slope_ref[base + n : base + 2 * n, :] = slope[:, width:]

    for copy in copies:
        copy.wait()
    add_taps(views, [weights], acc, None)


def edge_scales(parts, mp_index):
    place = mp_index // 2
    return jnp.where(place == 0, 0.0, 1.0).astype(F32), jnp.where(place == parts // 2 - 1, 0.0, 1.0).astype(F32)


def add_taps(views, refs, acc, base):
    half_rows = acc.shape[0] // 2
    rows = half_rows // (2 * PAIR_COLS)
    for b in range(3):
        field = views[:, b : b + rows].reshape(2 * half_rows, 3 * DEEP)
        now = dot(field, jnp.concatenate([tap_weights(refs, 9 + 3 * b + c) for c in range(3)], axis=0))
        late = dot(field[:half_rows], jnp.concatenate([tap_weights(refs, 3 * b + c) for c in range(3)], axis=0))
        so_far = acc if b else base
        if so_far is None:
            acc[:half_rows] = now[:half_rows]
            acc[half_rows:] = now[half_rows:] + late
        else:
            acc[:half_rows] = so_far[:half_rows] + now[:half_rows]
            acc[half_rows:] = so_far[half_rows:] + (now[half_rows:] + late)


def far_kernel(parts, info_ref, near_ref, views, *refs):
    sums_ref, slope_ref, acc = refs[-3:]
    add_taps(views, refs[:-3], acc, near_ref)
    n = PAIR_COLS
    top_scale, bottom_scale = edge_scales(parts, info_ref[0])
    tiles = []
    for t in range(LT):
        for row in range(6):
            part = acc[(6 * t + row) * 2 * n : (6 * t + row + 1) * 2 * n]
            half = part[:, TILE:]
            pre = jnp.concatenate([part[:, :TILE], half + pltpu.roll(half, TILE // 2, 1)], axis=1)
            gate = sigmoid(pre)
            slope = gate * (1.0 + pre * (1.0 - gate))
            if row == 0:
                slope = slope * top_scale
            elif row == 5:
                slope = slope * bottom_scale
            else:
                part_sum = jnp.sum(pre * gate, axis=0, keepdims=True)
                total = part_sum if row == 1 else total + part_sum
            slope_ref[t, row] = slope.astype(BF)
        tiles += [total[:, :TILE], total[:, TILE:]]
    sums = jnp.concatenate(tiles + [jnp.zeros((8 - len(tiles), TILE), F32)], axis=0)
    for part in range(parts):
        sums_ref[part] = sums


def three_terms(value):
    high = value.astype(BF)
    rest = value - high.astype(F32)
    middle = rest.astype(BF)
    low = (rest - middle.astype(F32)).astype(BF)
    return jnp.concatenate([high, middle, low], axis=0)


def backward_kernel(
    parts, cells, info_ref, sums_ref, patch_ref, text_ref, second_ref, slope_ref, pick_ref, patch_w, near_w, *refs
):
    far_refs = refs[:-4]
    reward_ref, send_ref, views, acc = refs[-4:]
    n = PAIR_COLS
    lane = lax.broadcasted_iota(jnp.int32, (8, TILE), 1)

    by_side = []
    for side in range(2):
        total = sums_ref[side]
        for part in range(side + 2, parts, 2):
            total = total + sums_ref[part]
        by_side.append(total)
    rows = []
    for t in range(LT):
        even, odd = [total[2 * t : 2 * t + 2] for total in by_side]
        mixed = jnp.where(lane[:1] < TILE // 2, even[1:2], odd[1:2])
        rows.append(jnp.concatenate([even[0:1], odd[0:1], mixed], axis=1))
    pooled = jnp.concatenate(rows + [jnp.zeros((8 - LT, 3 * TILE), F32)], axis=0) / cells
    products = dot(three_terms(pooled), patch_ref[...])
    embedded = products[0:8] + products[8:16] + products[16:24]
    text = text_ref[...]
    text_length = jnp.sqrt(jnp.sum(text * text, axis=1, keepdims=True) + 1e-06)
    embed_square = jnp.sum(embedded * embedded, axis=1, keepdims=True) + 1e-06
    embed_length = jnp.sqrt(embed_square)
    along = jnp.sum(embedded * text, axis=1, keepdims=True)
    cosine = along / (embed_length * text_length)
    share = 100.0 / LT
    reward_ref[0] = share * (cosine[0, 0] + cosine[1, 0])
    embed_grad = share * (text / (embed_length * text_length) - cosine * embedded / embed_square)
    products = dot_nt(three_terms(embed_grad), patch_ref[...])
    pool_grad = (products[0:8] + products[8:16] + products[16:24]) / cells

    side = info_ref[0] % 2
    third = pool_grad[:, 2 * TILE :]
    turned = pltpu.roll(third, TILE // 2, 1)
    half = jnp.where((lane < TILE // 2) == (side == 0), third, turned)
    own_grad = jnp.concatenate([jnp.where(side == 0, pool_grad[:, :TILE], pool_grad[:, TILE : 2 * TILE]), half], axis=1)

    for row in range(6):
        for t in range(LT):
            grad = second_ref[t, row].astype(F32) * own_grad[t : t + 1]
            even, odd = grad[:n], grad[n:]
            store_views(
                views, t, row, even.astype(BF), odd.astype(BF), shift_down(odd).astype(BF), shift_up(even).astype(BF)
            )

    half_rows = 8 * n
    for b in range(3):
        field = views[:, 2 - b : 6 - b].reshape(2 * half_rows, 6 * TILE)
        for blocks, lanes in (([near_w], slice(0, DEEP)), (far_refs, slice(DEEP, 2 * DEEP))):
            now = dot_nt(field, jnp.concatenate([tap_weights(blocks, 9 + 3 * b + c) for c in (2, 1, 0)], axis=1))
            early = dot_nt(
                field[half_rows:], jnp.concatenate([tap_weights(blocks, 3 * b + c) for c in (2, 1, 0)], axis=1)
            )
            if b == 0:
                acc[:half_rows, lanes] = now[:half_rows] + early
                acc[half_rows:, lanes] = now[half_rows:]
            else:
                acc[:half_rows, lanes] += now[:half_rows] + early
                acc[half_rows:, lanes] += now[half_rows:]
    grad_first = (acc[...] * slope_ref[...]).astype(BF)
    tokens = []
    for t in range(LT):
        for g in range(2):
            base = (8 * t + 4 * g) * n
            planes = [grad_first[base + i * n : base + (i + 1) * n] for i in range(4)]
            tokens.append(jnp.concatenate(planes, axis=1))
    patch_grad = dot_nt(jnp.concatenate(tokens, axis=0), patch_w[1])
    early = dot_nt(jnp.concatenate(tokens[2:], axis=0), patch_w[0])
    patch_grad = jnp.concatenate([patch_grad[: 2 * n] + early, patch_grad[2 * n :]], axis=0)
    spread_out = dot_nt(patch_grad.astype(BF), pick_ref[...])
    half = spread_out.shape[1] // 9
    blocks = [[], [], []]
    for t in range(LT):
        parts_of = []
        for g in range(2):
            rows = spread_out[(2 * t + g) * n : (2 * t + g + 1) * n]
            for pair_row in range(3):
                base = 3 * pair_row * half
                parts_of.append(
                    shift_up(rows[:, base : base + half])
                    + rows[:, base + half : base + 2 * half]
                    + shift_down(rows[:, base + 2 * half : base + 3 * half])
                )
        up, first, first_down, second_up, second, down = parts_of
        blocks[0].append(first + second_up)
        blocks[1].append(second + first_down)
        blocks[2].append(up + down)
    result = jnp.concatenate([jnp.concatenate(block, axis=1) for block in blocks], axis=0).astype(BF)
    for part in range(parts):
        send_ref[part] = result


def token_kernel(parts, recv_ref, modulated_ref, tokens_ref, head_ref):
    n = PAIR_COLS
    lanes = recv_ref.shape[2]
    sums = [recv_ref[i].astype(F32) + recv_ref[i + 1].astype(F32) for i in range(0, parts, 2)]
    blank = jnp.zeros((n, lanes), F32)
    lower = lax.broadcasted_iota(jnp.int32, blank.shape, 1) // (lanes // 4) % 2 == 1
    rows = []
    for i, block in enumerate(sums):
        from_above = sums[i - 1][2 * n :] if i else blank
        from_below = sums[i + 1][2 * n :] if i + 1 < len(sums) else blank
        rows.append(block[:n] + jnp.where(lower, 0.0, from_above))
        rows.append(block[n : 2 * n] + jnp.where(lower, from_below, 0.0))
    wide = jnp.concatenate(rows, axis=0)
    tokens = jnp.concatenate([wide[:, : lanes // 2], wide[:, lanes // 2 :]], axis=0)
    flipped = jnp.transpose(tokens).astype(BF)
    tokens_ref[...] = tokens.astype(BF)
    head_ref[...] = dot(flipped, modulated_ref[...]).astype(BF)


def hidden_kernel(tokens_ref, head_ref, gain_ref, out_ref):
    out_ref[...] = (dot(tokens_ref[...], head_ref[...]) * gain_ref[...]).astype(BF)


VMEM = pl.BlockSpec(memory_space=pltpu.VMEM)
SMEM = pl.BlockSpec(memory_space=pltpu.SMEM)
HBM = pl.BlockSpec(memory_space=pltpu.HBM)


def exchange(block, axis, flip):
    count = lax.axis_size(axis)
    return lax.ppermute(block, axis, [(i, i ^ flip) for i in range(count)])


def spread(piece):
    blocks = {0: piece}
    flip = lax.axis_size("dp") // 4
    while flip:
        for held in list(blocks):
            blocks[held ^ flip] = exchange(blocks[held], "dp", flip)
        flip //= 2
    unit, rows = 1, piece.shape[1]
    while rows * unit % 16:
        low = (lax.axis_index("dp") // unit) % 2 == 0
        merged = {}
        for held in blocks:
            if held % (2 * unit) == 0:
                mine, other = blocks[held], blocks[held ^ unit]
                merged[held] = jnp.where(
                    low, jnp.concatenate([mine, other], axis=1), jnp.concatenate([other, mine], axis=1)
                )
        blocks, unit = merged, 2 * unit
    return [blocks[held] for held in sorted(blocks)], unit


def local_channels(weight, unit):
    count = lax.axis_size("dp") // unit
    place = lax.axis_index("dp") // unit
    rows = weight.shape[2] // count
    blocks = [weight[..., i * rows : (i + 1) * rows] for i in range(count)]
    flip = count // 2
    while flip:
        swap = place // flip % 2 == 1
        blocks = [jnp.where(swap, blocks[i ^ flip], blocks[i]) for i in range(count)]
        flip //= 2
    spare = jnp.zeros(weight.shape[:2] + (DEEP - weight.shape[2] // 2,), weight.dtype)
    return jnp.concatenate(blocks[: count // 2] + [spare] + blocks[count // 2 :] + [spare], axis=2)


def body(hidden, mod_table, timestep, head_weight, conv_in, conv_mid, patch_weight, text_emb):
    parts = lax.axis_size("mp")
    groups = lax.axis_size("dp")
    tokens, depth = hidden.shape
    features = head_weight.shape[1]
    channels = features // 4
    width = conv_in.shape[2]
    n = PAIR_COLS
    pair_rows = tokens // (LT * n)
    cells = float(2 * pair_rows * LW)
    mp_index = lax.axis_index("mp")

    head_rows = head_weight.T
    taps = jnp.transpose(conv_mid, (1, 0, 2))
    rows = conv_mid.shape[0]
    far = groups // 2

    packed = pl.pallas_call(
        pack_kernel,
        in_specs=[HBM],
        out_specs=VMEM,
        out_shape=jax.ShapeDtypeStruct((9, rows, width), BF),
        scratch_shapes=[pltpu.VMEM((18, rows, width), BF), pltpu.SemaphoreType.DMA],
        compiler_params=params(56),
        name="pack",
    )(taps)
    distant = exchange(packed, "dp", far)
    modulated, gain, send = pl.pallas_call(
        functools.partial(head_kernel, parts),
        in_specs=[HBM] * 4,
        out_specs=[VMEM] * 3,
        out_shape=[
            jax.ShapeDtypeStruct((tokens, depth), BF),
            jax.ShapeDtypeStruct((1, depth), F32),
            jax.ShapeDtypeStruct((parts, 5 * n, 2 * features), BF),
        ],
        scratch_shapes=[
            pltpu.SMEM((1,), jnp.int32),
            pltpu.VMEM((tokens, depth), BF),
            pltpu.VMEM(mod_table.shape, BF),
            pltpu.VMEM((features, depth), BF),
            pltpu.SemaphoreType.DMA((4,)),
        ],
        compiler_params=params(56),
        name="head",
    )(timestep, hidden, mod_table, head_rows)
    send, conv_in = lax.optimization_barrier((send, conv_in))
    recv = lax.all_to_all(send, "mp", 0, 0, tiled=True)
    near_blocks, unit = spread(packed)
    recv, distant = lax.optimization_barrier((recv, distant))
    far_blocks, _ = spread(distant)
    blocks = len(near_blocks)
    info = jnp.reshape(mp_index, (1,)).astype(jnp.int32)
    taps_in = local_channels(jnp.transpose(conv_in[:, 9:], (1, 0, 2)), unit)
    pick = jnp.asarray(selection(channels))

    acc_shape = jax.ShapeDtypeStruct((24 * n, 2 * TILE), F32)
    views_shape = (LT, 8, 2 * n, 3 * DEEP)
    near_acc, far_views, slope, near_w, patch_w = pl.pallas_call(
        functools.partial(near_kernel, parts, blocks),
        in_specs=[SMEM, VMEM, VMEM, VMEM] + [HBM] * blocks,
        out_specs=[VMEM] * 5,
        out_shape=[
            acc_shape,
            jax.ShapeDtypeStruct(views_shape, BF),
            jax.ShapeDtypeStruct((16 * n, 2 * DEEP), F32),
            jax.ShapeDtypeStruct((9, width // 2, width), BF),
            jax.ShapeDtypeStruct((2, 16 * channels, 8 * DEEP), BF),
        ],
        scratch_shapes=[pltpu.VMEM(views_shape, BF), pltpu.SemaphoreType.DMA((blocks,))],
        cost_estimate=pl.CostEstimate(flops=4 * 10**9, bytes_accessed=10**7, transcendentals=10**6),
        compiler_params=params(20),
        name="near",
    )(info, recv, taps_in, pick, *near_blocks)
    sums, second_slope = pl.pallas_call(
        functools.partial(far_kernel, parts),
        in_specs=[SMEM] + [VMEM] * (2 + blocks),
        out_specs=[VMEM] * 2,
        out_shape=[
            jax.ShapeDtypeStruct((parts, 8, TILE), F32),
            jax.ShapeDtypeStruct((LT, 6, 2 * n, 2 * TILE), BF),
        ],
        scratch_shapes=[pltpu.VMEM(acc_shape.shape, F32)],
        compiler_params=params(16),
        name="far",
    )(info, near_acc, far_views, *far_blocks)
    all_sums = lax.all_to_all(sums, "mp", 0, 0, tiled=True)

    reward, contribution = pl.pallas_call(
        functools.partial(backward_kernel, parts, cells),
        in_specs=[SMEM] + [VMEM] * (8 + blocks),
        out_specs=[SMEM, VMEM],
        out_shape=[
            jax.ShapeDtypeStruct((1,), F32),
            jax.ShapeDtypeStruct((parts, 3 * n, 2 * features), BF),
        ],
        scratch_shapes=[pltpu.VMEM((LT, 6, 2 * n, 6 * TILE), BF), pltpu.VMEM((16 * n, 2 * DEEP), F32)],
        compiler_params=params(16),
        name="backward",
    )(info, all_sums, patch_weight, text_emb, second_slope, slope, pick, patch_w, near_w, *far_blocks)
    contributions = lax.all_to_all(contribution, "mp", 0, 0, tiled=True)

    token_grad, head_term = pl.pallas_call(
        functools.partial(token_kernel, parts),
        in_specs=[VMEM, VMEM],
        out_specs=[VMEM, VMEM],
        out_shape=[
            jax.ShapeDtypeStruct((tokens, features), BF),
            jax.ShapeDtypeStruct((features, depth), BF),
        ],
        compiler_params=params(8),
        name="token",
    )(contributions, modulated)
    flip = 1
    while flip < far:
        other = exchange(head_term, "dp", flip)
        head_term = (head_term.astype(F32) + other.astype(F32)).astype(BF)
        flip *= 2
    head_other = exchange(head_term, "dp", far)
    hidden_grad = pl.pallas_call(
        hidden_kernel,
        in_specs=[VMEM] * 3,
        out_specs=VMEM,
        out_shape=jax.ShapeDtypeStruct((tokens, depth), BF),
        compiler_params=params(8),
        name="hidden_grad",
    )(token_grad, head_rows, gain)
    head_grad = head_term.astype(F32) + head_other.astype(F32)
    return (reward, head_grad.T, hidden_grad)


def solution(mesh):
    in_specs = (
        P("dp", "mp"),
        P(None, None, "mp"),
        P("dp"),
        P("mp", None),
        P(),
        P("dp", None, None),
        P(),
        P("dp", None),
    )
    out_specs = (P("dp"), P("mp", None), P("dp", "mp"))
    return jax.shard_map(body, mesh=mesh, in_specs=in_specs, out_specs=out_specs, check_vma=False)
```

time: 263 us -> 62.7 us (0.24)
  waiting for transfers between devices: 109 us -> 14.1 us
  matrix products: 56.7 us -> 0 us
  blocking collectives: 48.8 us -> 20.3 us
  between operations: 19.6 us -> 1.51 us
  Pallas kernels: 0 us -> 15.8 us
  starting transfers between devices: 21.4 us -> 9.56 us
  local copies, waits for them, and re-layouts: 3.66 us -> 0.29 us
    reduce_scatter x1 -> x0, waiting for transfers between devices: 57.8 us -> none  [body(): lax.psum_scatter(latent_grid.astype(jnp.bfloat16), 'mp', scatter_dimensio...]
    dot_general x115 -> x0, matrix products: 56.7 us -> none  [the longest x54 27.2 us: forward_full(): jnp.einsum('thwi,io->thwo', views[tap_index], weight[:, tap_index, :], pr...]
    all_gather x1 -> x0, blocking collectives: 30.6 us -> none  [body(): full_grad = lax.all_gather(latent_grad, 'mp', axis=1, tiled=True)]
    psum x1 -> x0, waiting for transfers between devices: 26.1 us -> none  [body(): lax.psum(head_local.astype(jnp.bfloat16), 'dp').astype(jnp.float32)]
    all_to_all x0 -> x2, blocking collectives: none -> 20.3 us  [the longest x1 10.2 us: body(): contributions = lax.all_to_all(contribution, 'mp', 0, 0, tiled=True)]
    psum x1 -> x0, blocking collectives: 18.2 us -> none  [body(): pooled = lax.psum(frame_sums, 'mp') / cell_count]
    pallas_call x0 -> x7, Pallas kernels: none -> 15.8 us  [the longest x1 4.67 us: body(): pl.pallas_call(functools.partial(backward_kernel, parts, cells), in_specs...]
    ppermute x8 -> x5, starting transfers between devices: 17.7 us -> 3.68 us  [exchange(): return lax.ppermute(block, axis, [(i, i ^ flip) for i in range(count)])]
  transfers between devices with their start and end apart: 12 -> 6, of which waited for: 9 -> 3; matrix products, arithmetic and copies ran while one was open for 6% -> 1% of each run, Pallas kernels for 0% -> 11%
where the time goes in v1:
time: 62.7 us; the launch traced here: 62.4 us
  blocking collectives  20.3 us (32%)
  Pallas kernels  15.8 us (25%)
  waiting for transfers between devices  14.1 us (22%)
  starting transfers between devices  9.56 us (15%)
  between operations  1.51 us (2%)
  other arithmetic  0.84 us (1%)
    all_to_all x1, blocking collectives, body(): contributions = lax.all_to_all(contribution, 'mp', 0, 0, tiled=True)  10.2 us
    all_to_all x1, blocking collectives, body(): all_sums = lax.all_to_all(sums, 'mp', 0, 0, tiled=True)  10.1 us
    all_to_all x1, waiting for transfers between devices, body(): recv = lax.all_to_all(send, 'mp', 0, 0, tiled=True)  10 us
    all_to_all x1, starting transfers between devices, body(): recv = lax.all_to_all(send, 'mp', 0, 0, tiled=True)  5.87 us
    pallas_call x1, Pallas kernels, body(): pl.pallas_call(functools.partial(backward_kernel, parts, cells), in_specs...  4.67 us
    ppermute x5, waiting for transfers between devices, exchange(): return lax.ppermute(block, axis, [(i, i ^ flip) for i in range(count)])  4.08 us
    ppermute x5, starting transfers between devices, exchange(): return lax.ppermute(block, axis, [(i, i ^ flip) for i in range(count)])  3.68 us
    pallas_call x1, Pallas kernels, body(): pl.pallas_call(functools.partial(near_kernel, parts, blocks), in_specs=[S...  3.21 us
  transfers between devices with their start and end apart: 6, of which 3 were waited for; matrix products, arithmetic and copies ran while one was open for 1% of the time, Pallas kernels for 11%

profile of v1, /device:TPU:0, one launch (start us, length us, event | category | flops | bytes accessed | tf_op | source)
XLA Modules:
  0.0 62.4 jit_solution(14848417876228695511)
XLA Ops:
  0.6 0.0 copy-start.7
  0.6 2.4 %pack.1.refs_0_ = bf16[9,96,384]{2,1,0:T(8,128)(2,1)} custom-call(bf16[27,96,384]{2,1,0:T(8,128)(2,1)} %bitcast.9), custom_call_target="tpu_custom_call" | custom-call | tf_op jit(solution)/shard_map/pack/pallas_call | solution.py:453
  3.0 0.0 copy-start.1
  3.0 0.0 copy-start.4
  3.0 3.0 %collective-permute-start = (bf16[9,96,384]{2,1,0:T(8,128)(2,1)}, bf16[9,96,384]{2,1,0:T(8,128)(2,1)S(1)}, u32[]{:S(2)}, u32[]{:S(2)}) collective-permute-start(bf16[9,96,384]{2,1,0:T(8,128)(2,1)} %pack.1.refs_0_), channel_id=1, source_target_pairs={{0,16},{8,24},{16,0},{24,8},{1,17},{9,25},{17,1},{25,9},{2,18},{10... | collective-permute-start | bytes 1990664 | tf_op jit(solution)/shard_map/ppermute | solution.py:398
  6.7 2.3 %head.1 = (bf16[512,640]{1,0:T(8,128)(2,1)}, f32[1,640]{1,0:T(1,128)}, bf16[8,160,128]{2,1,0:T(8,128)(2,1)}) custom-call(s32[1]{0:T(128)S(6)} %copy.12.step_hbm, bf16[512,640]{1,0:T(8,128)(2,1)} %hidden_hbm.1, bf16[50,2,640]{2,1,0:T(2,128)(2,1)} %mod_hbm.1, bf16[64,640]{1,0:T(8,128)(2,1)} %bitcast.7), custom_call_target="tpu_custom_call" | custom-call | tf_op jit(solution)/shard_map/head/pallas_call | solution.py:463
  9.0 5.9 %all-to-all-start = ((bf16[8,160,128]{2,1,0:T(8,128)(2,1)}), bf16[8,160,128]{2,1,0:T(8,128)(2,1)S(1)}, u32[]{:S(2)}, u32[]{:S(2)}) async-start(bf16[8,160,128]{2,1,0:T(8,128)(2,1)} %get-tuple-element.22), calls=%async_computation | async-start | bytes 655360 | tf_op jit(solution)/shard_map/all_to_all | solution.py:483
  14.9 0.0 collective-permute-start.1
  14.9 10.0 %all-to-all-done.recv_ref = bf16[8,160,128]{2,1,0:T(8,128)(2,1)S(1)} async-done(((bf16[8,160,128]{2,1,0:T(8,128)(2,1)}), bf16[8,160,128]{2,1,0:T(8,128)(2,1)S(1)}, u32[]{:S(2)}, u32[]{:S(2)}) %all-to-all-start) | async-done | bytes 327712 | tf_op jit(solution)/shard_map/all_to_all | solution.py:483
  24.9 0.0 collective-permute-done.refs_0_
  24.9 0.0 collective-permute-start.2
  25.0 0.0 copy-done.7
  25.0 0.1 broadcast_select_fusion.4
  25.2 0.2 concatenate.3.conv_ref
  25.4 0.0 collective-permute-done.1.refs_1_
  25.4 0.0 copy-done.1
  25.4 0.0 copy-done.4
  25.4 3.2 %near.1 = (f32[768,256]{1,0:T(8,128)S(1)}, bf16[2,8,64,768]{3,2,1,0:T(8,128)(2,1)S(1)}, f32[512,512]{1,0:T(8,128)S(1)}, bf16[9,192,384]{2,1,0:T(8,128)(2,1)S(1)}, bf16[2,256,2048]{2,1,0:T(8,128)(2,1)S(1)}) custom-call(s32[1]{0:T(128)} %bitcast.info_ref, bf16[8,160,128]{2,1,0:T(8,128)(2,1)S(1)} %all-to-all-done.recv_ref, ...), custom_call_target="tpu_custom_call" | custom-call | flops 4000000000 | bytes 10000000 | tf_op jit(solution)/shard_map/near/pallas_call | solution.py:494
  28.7 0.0 copy-start
  28.7 0.0 copy-start.5
  28.7 0.0 collective-permute-done.2.refs_1_
  28.7 1.8 %far.1 = (f32[8,8,128]{2,1,0:T(8,128)S(1)}, bf16[2,6,64,256]{3,2,1,0:T(8,128)(2,1)S(1)}) custom-call(s32[1]{0:T(128)} %bitcast.info_ref, f32[768,256]{1,0:T(8,128)S(1)} %get-tuple-element.25.near_ref, bf16[2,8,64,768]{3,2,1,0:T(8,128)(2,1)S(1)} %get-tuple-element.26.views, bf16[9,96,384]{2,1,0:T(8,128)(2,1)S(1)} %collective-permute-done.refs_0_, ...), custom_call_target="tpu_custom_call" | custom-call | tf_op jit(solution)/shard_map/far/pallas_call | solution.py:510
  30.5 10.1 %all_to_all.15.sums_ref = f32[8,8,128]{2,1,0:T(8,128)S(1)} all-to-all(f32[8,8,128]{2,1,0:T(8,128)S(1)} %get-tuple-element.28), channel_id=1, replica_groups=mesh['dp'=4,'mp'=8] {'mp'}, dimensions={0} | all-to-all | bytes 65536 | tf_op jit(solution)/shard_map/all_to_all | solution.py:522
  40.5 0.0 copy-done
  40.5 0.0 copy-done.5
  40.5 0.0 copy-start.2
  40.5 0.0 copy-start.3
  40.6 0.0 copy-start.6
  40.6 4.7 %backward.1 = (f32[1]{0:T(128)}, bf16[8,96,128]{2,1,0:T(8,128)(2,1)S(1)}) custom-call(s32[1]{0:T(128)} %bitcast.info_ref, f32[8,8,128]{2,1,0:T(8,128)S(1)} %all_to_all.15.sums_ref, bf16[384,1024]{1,0:T(8,128)(2,1)S(1)} %copy-done, f32[1,1024]{1,0:T(1,128)S(1)} %copy-done.5, bf16[2,6,64,256]{3,2,1,0:T(8,128)(2,1)S(1)} %get-tuple-element.29.second_ref, ...), custom_call_target="tpu_custom_call" | custom-call | tf_op jit(solution)/shard_map/backward/pallas_call | solution.py:524
  45.2 10.2 %all_to_all.16.recv_ref = bf16[8,96,128]{2,1,0:T(8,128)(2,1)S(1)} all-to-all(bf16[8,96,128]{2,1,0:T(8,128)(2,1)S(1)} %get-tuple-element.34), channel_id=1, replica_groups=mesh['dp'=4,'mp'=8] {'mp'}, dimensions={0} | all-to-all | bytes 393216 | tf_op jit(solution)/shard_map/all_to_all | solution.py:536
  55.4 0.0 copy-done.2
  55.4 0.3 token_.1
  55.8 0.1 collective-permute-start.3
  55.8 1.3 %collective-permute-done.3 = bf16[64,640]{1,0:T(8,128)(2,1)S(1)} collective-permute-done((bf16[64,640]{1,0:T(8,128)(2,1)S(1)}, bf16[64,640]{1,0:T(8,128)(2,1)S(1)}, u32[]{:S(2)}, u32[]{:S(2)}) %collective-permute-start.3) | collective-permute-done | bytes 81952 | tf_op jit(solution)/shard_map/ppermute | solution.py:398
  57.1 0.6 collective-permute-start.4
  57.7 0.0 copy-done.3
  57.7 0.0 copy-done.6
  57.7 1.2 %hidden_grad.1 = bf16[512,640]{1,0:T(8,128)(2,1)} custom-call(bf16[512,64]{1,0:T(8,128)(2,1)S(1)} %get-tuple-element.37.tokens_ref, bf16[64,640]{1,0:T(8,128)(2,1)S(1)} %bitcast.8, f32[1,640]{1,0:T(1,128)S(1)} %copy-done.6), custom_call_target="tpu_custom_call" | custom-call | tf_op jit(solution)/shard_map/hidden_grad/pallas_call | solution.py:555
  58.9 2.8 %collective-permute-done.4 = bf16[64,640]{1,0:T(8,128)(2,1)S(1)} collective-permute-done((bf16[64,640]{1,0:T(8,128)(2,1)S(1)}, bf16[64,640]{1,0:T(8,128)(2,1)S(1)}, u32[]{:S(2)}, u32[]{:S(2)}) %collective-permute-start.4) | collective-permute-done | bytes 81952 | tf_op jit(solution)/shard_map/ppermute | solution.py:398
  61.7 0.7 %add_bitcast_fusion = f32[640,64]{0,1:T(8,128)} fusion(bf16[64,640]{1,0:T(8,128)(2,1)S(1)} %collective-permute-done.4, bf16[64,640]{1,0:T(8,128)(2,1)S(1)} %add_convert_fusion), kind=kLoop, calls=%fused_computation.1 | loop fusion | flops 122880 | bytes 327680 | tf_op jit(solution)/shard_map/transpose | solution.py:564
  (3 shorter events, 0.1 us)
Async XLA Ops:
  0.6 24.3 %copy-start.7 = (bf16[16,27,384]{2,0,1:T(8,128)(2,1)S(1)}, bf16[16,27,384]{2,0,1:T(8,128)(2,1)}, u32[]{:S(2)}) copy-start(bf16[16,27,384]{2,0,1:T(8,128)(2,1)} %param.13) | copy-start | bytes 995332
  3.0 22.4 %copy-start.1 = (bf16[9,96,384]{2,1,0:T(8,128)(2,1)S(1)}, bf16[9,96,384]{2,1,0:T(8,128)(2,1)}, u32[]{:S(2)}) copy-start(bf16[9,96,384]{2,1,0:T(8,128)(2,1)} %pack.1.refs_0_) | copy-start | bytes 1990660
  3.0 22.4 %copy-start.4 = (bf16[576,256]{1,0:T(8,128)(2,1)S(1)}, bf16[576,256]{1,0:T(8,128)(2,1)}, u32[]{:S(2)}) copy-start(bf16[576,256]{1,0:T(8,128)(2,1)} %constant.56.clone.pick_ref) | copy-start | bytes 884740
  3.0 21.9 %collective-permute-start = (bf16[9,96,384]{2,1,0:T(8,128)(2,1)}, bf16[9,96,384]{2,1,0:T(8,128)(2,1)S(1)}, u32[]{:S(2)}, u32[]{:S(2)}) collective-permute-start(bf16[9,96,384]{2,1,0:T(8,128)(2,1)} %pack.1.refs_0_), channel_id=1, source_target_pairs={{0,16},{8,24},{16,0},{24,8},{1,17},{9,25},{17,1},{25,9},{2,18},{10... | collective-permute-start | bytes 1990664 | tf_op jit(solution)/shard_map/ppermute | solution.py:398
  9.0 15.9 %all-to-all-start = ((bf16[8,160,128]{2,1,0:T(8,128)(2,1)}), bf16[8,160,128]{2,1,0:T(8,128)(2,1)S(1)}, u32[]{:S(2)}, u32[]{:S(2)}) async-start(bf16[8,160,128]{2,1,0:T(8,128)(2,1)} %get-tuple-element.22), calls=%async_computation | async-start | bytes 655360 | tf_op jit(solution)/shard_map/all_to_all | solution.py:483
  14.9 10.5 %collective-permute-start.1 = (bf16[9,96,384]{2,1,0:T(8,128)(2,1)}, bf16[9,96,384]{2,1,0:T(8,128)(2,1)}, u32[]{:S(2)}, u32[]{:S(2)}) collective-permute-start(bf16[9,96,384]{2,1,0:T(8,128)(2,1)} %pack.1.refs_0_), channel_id=1, source_target_pairs={{0,8},{8,0},{16,24},{24,16},{1,9},{9,1},{17,25},{25,17},{2,10},{10... | collective-permute-start | bytes 1990664 | tf_op jit(solution)/shard_map/ppermute | solution.py:398
  24.9 3.7 %collective-permute-start.2 = (bf16[9,96,384]{2,1,0:T(8,128)(2,1)S(1)}, bf16[9,96,384]{2,1,0:T(8,128)(2,1)S(1)}, u32[]{:S(2)}, u32[]{:S(2)}) collective-permute-start(bf16[9,96,384]{2,1,0:T(8,128)(2,1)S(1)} %collective-permute-done.refs_0_), channel_id=1, source_target_pairs={{0,8},{8,0},{16,24},{24,16},{1,9},{9,1},{17,25},{25,17},{2,10},{10... | collective-permute-start | bytes 1990664 | tf_op jit(solution)/shard_map/ppermute | solution.py:398
  28.7 11.9 %copy-start = (bf16[384,1024]{1,0:T(8,128)(2,1)S(1)}, bf16[384,1024]{1,0:T(8,128)(2,1)}, u32[]{:S(2)}) copy-start(bf16[384,1024]{1,0:T(8,128)(2,1)} %patch_ref.1) | copy-start | bytes 2359300
  28.7 11.9 %copy-start.5 = (f32[1,1024]{1,0:T(1,128)S(1)}, f32[1,1024]{1,0:T(1,128)}, u32[]{:S(2)}) copy-start(f32[1,1024]{1,0:T(1,128)} %text_ref.1) | copy-start | bytes 12292
  40.5 14.9 %copy-start.2 = (bf16[512,640]{1,0:T(8,128)(2,1)S(1)}, bf16[512,640]{1,0:T(8,128)(2,1)}, u32[]{:S(2)}) copy-start(bf16[512,640]{1,0:T(8,128)(2,1)} %get-tuple-element.35.modulated_ref) | copy-start | bytes 1966084
  40.5 17.2 %copy-start.3 = (bf16[640,64]{0,1:T(8,128)(2,1)S(1)}, bf16[640,64]{0,1:T(8,128)(2,1)}, u32[]{:S(2)}) copy-start(bf16[640,64]{0,1:T(8,128)(2,1)} %param.12) | copy-start | bytes 245764
  40.6 17.2 %copy-start.6 = (f32[1,640]{1,0:T(1,128)S(1)}, f32[1,640]{1,0:T(1,128)}, u32[]{:S(2)}) copy-start(f32[1,640]{1,0:T(1,128)} %get-tuple-element.38.gain_ref) | copy-start | bytes 7684
  55.8 1.3 %collective-permute-start.3 = (bf16[64,640]{1,0:T(8,128)(2,1)S(1)}, bf16[64,640]{1,0:T(8,128)(2,1)S(1)}, u32[]{:S(2)}, u32[]{:S(2)}) collective-permute-start(bf16[64,640]{1,0:T(8,128)(2,1)S(1)} %get-tuple-element.36), channel_id=1, source_target_pairs={{0,8},{8,0},{16,24},{24,16},{1,9},{9,1},{17,25},{25,17},{2,10},{10... | collective-permute-start | bytes 245768 | tf_op jit(solution)/shard_map/ppermute | solution.py:398
  57.1 4.6 %collective-permute-start.4 = (bf16[64,640]{1,0:T(8,128)(2,1)S(1)}, bf16[64,640]{1,0:T(8,128)(2,1)S(1)}, u32[]{:S(2)}, u32[]{:S(2)}) collective-permute-start(bf16[64,640]{1,0:T(8,128)(2,1)S(1)} %add_convert_fusion), channel_id=1, source_target_pairs={{0,16},{8,24},{16,0},{24,8},{1,17},{9,25},{17,1},{25,9},{2,18},{10... | collective-permute-start | bytes 245768 | tf_op jit(solution)/shard_map/ppermute | solution.py:398

commit v2 on v1

--- a/solution.py
+++ b/solution.py
@@ -48,64 +48,90 @@
     return pick.reshape(36 * channels, 16 * channels).astype(BF)
 
 
-def pack_kernel(taps_hbm, packed_ref, taps, sem):
-    count = taps.shape[0]
-    copy = pltpu.make_async_copy(taps_hbm.at[pl.ds(taps_hbm.shape[0] - count, count)], taps, sem)
-    copy.start()
-    copy.wait()
+def pack_kernel(taps_hbm, packed_hbm, packed, thirds, in_sems, out_sems):
+    first = taps_hbm.shape[0] - 18
     odd = lax.axis_index("mp") % 2
-    lane = lax.broadcasted_iota(jnp.int32, (taps.shape[1], TILE), 1)
-    for side in range(2):
-
-        @pl.when(odd == side)
-        def _():
-            for pair in range(count // 2):
-                first, second = taps[2 * pair], taps[2 * pair + 1]
-                packed_ref[pair, :, :TILE] = first[:, side * TILE : (side + 1) * TILE]
-                packed_ref[pair, :, TILE : 2 * TILE] = second[:, side * TILE : (side + 1) * TILE]
-                left, right = first[:, 2 * TILE :].astype(F32), second[:, 2 * TILE :].astype(F32)
-                if side == 0:
-                    right = pltpu.roll(right, TILE // 2, 1)
-                else:
-                    left = pltpu.roll(left, TILE // 2, 1)
-                packed_ref[pair, :, 2 * TILE :] = jnp.where(lane < TILE // 2, left, right).astype(BF)
+    own = pl.ds(pl.multiple_of(odd * TILE, TILE), TILE)
+    copies, results = [], []
+    for chunk in range(3):
+        pairs = pl.ds(3 * chunk, 3)
+        here = []
+        for side in range(2):
+            source = taps_hbm.at[pl.ds(first + 9 * side + 3 * chunk, 3)]
+            here.append((source.at[:, :, own], packed.at[pairs, :, pl.ds(side * TILE, TILE)]))
+            here.append((source.at[:, :, pl.ds(2 * TILE, TILE)], thirds.at[side, pairs]))
+        copies.append([pltpu.make_async_copy(*ends, in_sems.at[chunk, i]) for i, ends in enumerate(here)])
+        results.append(pltpu.make_async_copy(packed.at[pairs], packed_hbm.at[pairs], out_sems.at[chunk]))
+    for chunk in range(3):
+        for copy in copies[chunk]:
+            copy.start()
+    lane = lax.broadcasted_iota(jnp.int32, thirds.shape[2:], 1)
+    for chunk in range(3):
+        for copy in copies[chunk]:
+            copy.wait()
+        for pair in range(3 * chunk, 3 * chunk + 3):
+            left, right = thirds[0, pair].astype(F32), thirds[1, pair].astype(F32)
+            left = jnp.where(odd == 0, left, pltpu.roll(left, TILE // 2, 1))
+            right = jnp.where(odd == 0, pltpu.roll(right, TILE // 2, 1), right)
+            packed[pair, :, 2 * TILE :] = jnp.where(lane < TILE // 2, left, right).astype(BF)
+        results[chunk].start()
+    for result in results:
+        result.wait()
 
 
 def head_kernel(
-    parts, step_hbm, hidden_hbm, mod_hbm, head_hbm, modulated_ref, gain_ref, send_ref, step_ref, hidden_ref, mod_ref,
-    head_ref, sems
+    parts, step_hbm, hidden_hbm, mod_hbm, head_hbm, modulated_hbm, gain_ref, send_hbm, step_ref, hidden_ref, mod_ref,
+    head_ref, modulated, blocks, in_sems, out_sems, send_sems
 ):
-    copies = [
-        pltpu.make_async_copy(hidden_hbm, hidden_ref, sems.at[0]),
-        pltpu.make_async_copy(mod_hbm, mod_ref, sems.at[1]),
-        pltpu.make_async_copy(head_hbm, head_ref, sems.at[2]),
-        pltpu.make_async_copy(step_hbm, step_ref, sems.at[3]),
+    n = PAIR_COLS
+    half = hidden_ref.shape[0] // LT
+    frames = [pl.ds(t * half, half) for t in range(LT)]
+    small = [
+        pltpu.make_async_copy(step_hbm, step_ref, in_sems.at[0]),
+        pltpu.make_async_copy(mod_hbm, mod_ref, in_sems.at[1]),
+        pltpu.make_async_copy(head_hbm, head_ref, in_sems.at[2]),
     ]
-    for copy in copies:
+    large = [
+        pltpu.make_async_copy(hidden_hbm.at[rows], hidden_ref.at[rows], in_sems.at[3 + t])
+        for t, rows in enumerate(frames)
+    ]
+    results = [
+        pltpu.make_async_copy(modulated.at[rows], modulated_hbm.at[rows], out_sems.at[t]) for t, rows in enumerate(frames)
+    ]
+    for copy in small + large:
         copy.start()
-    for copy in copies:
+    for copy in small:
         copy.wait()
-    mod = mod_ref[step_ref[0]].astype(F32)
+    step = jnp.broadcast_to(step_ref[...], mod_ref.shape[1:])
+    mod = jnp.zeros(mod_ref.shape[1:], F32)
+    for i in range(mod_ref.shape[0]):
+        mod = mod + jnp.where(step == i, mod_ref[i].astype(F32), 0.0)
     gain = 1.0 + mod[1:2]
-    modulated = (hidden_ref[...].astype(F32) * gain + mod[0:1]).astype(BF)
-    modulated_ref[...] = modulated
     gain_ref[...] = gain
-    terms = dot_nt(modulated, head_ref[...])
-    half = terms.shape[0] // 2
-    wide = jnp.concatenate([terms[:half], terms[half:]], axis=1)
-    n = PAIR_COLS
+    terms = []
+    for t, rows in enumerate(frames):
+        large[t].wait()
+        values = (hidden_ref[rows].astype(F32) * gain + mod[0:1]).astype(BF)
+        modulated[rows] = values
+        results[t].start()
+        terms.append(dot_nt(values, head_ref[...]))
+    wide = jnp.concatenate(terms, axis=1)
     blank = jnp.zeros((n, wide.shape[1]), F32)
     lower = lax.broadcasted_iota(jnp.int32, blank.shape, 1) // (wide.shape[1] // 4) % 2 == 1
 
     def pair_row(i):
         return blank if i < 0 or i >= parts else wide[i * n : (i + 1) * n]
 
+    sends = []
     for part in range(0, parts, 2):
         outer = jnp.where(lower, pair_row(part - 2), pair_row(part + 3))
         rows = [pair_row(part + i) for i in range(-1, 3)] + [outer]
-        block = jnp.concatenate(rows, axis=0).astype(BF)
-        send_ref[part] = block
-        send_ref[part + 1] = block
+        blocks[part // 2] = jnp.concatenate(rows, axis=0).astype(BF)
+        for i in (part, part + 1):
+            sends.append(pltpu.make_async_copy(blocks.at[part // 2], send_hbm.at[i], send_sems.at[i]))
+            sends[-1].start()
+    for result in results + sends:
+        result.wait()
 
 
 def build_patch_weights(conv_ref, patch_w):
@@ -130,7 +156,7 @@
 
 
 def tap_weights(refs, tap):
-    pair, side = tap // 2, tap % 2
+    pair, side = tap % 9, tap // 9
     blocks = []
     for ref in refs:
         half = ref[pair, :, 2 * TILE :]
@@ -453,9 +479,14 @@
     packed = pl.pallas_call(
         pack_kernel,
         in_specs=[HBM],
-        out_specs=VMEM,
+        out_specs=HBM,
         out_shape=jax.ShapeDtypeStruct((9, rows, width), BF),
-        scratch_shapes=[pltpu.VMEM((18, rows, width), BF), pltpu.SemaphoreType.DMA],
+        scratch_shapes=[
+            pltpu.VMEM((9, rows, width), BF),
+            pltpu.VMEM((2, 9, rows, TILE), BF),
+            pltpu.SemaphoreType.DMA((3, 4)),
+            pltpu.SemaphoreType.DMA((3,)),
+        ],
         compiler_params=params(56),
         name="pack",
     )(taps)
@@ -463,22 +494,26 @@
     modulated, gain, send = pl.pallas_call(
         functools.partial(head_kernel, parts),
         in_specs=[HBM] * 4,
-        out_specs=[VMEM] * 3,
+        out_specs=[HBM, VMEM, HBM],
         out_shape=[
             jax.ShapeDtypeStruct((tokens, depth), BF),
             jax.ShapeDtypeStruct((1, depth), F32),
             jax.ShapeDtypeStruct((parts, 5 * n, 2 * features), BF),
         ],
         scratch_shapes=[
-            pltpu.SMEM((1,), jnp.int32),
+            pltpu.VMEM((1, 1), jnp.int32),
             pltpu.VMEM((tokens, depth), BF),
             pltpu.VMEM(mod_table.shape, BF),
             pltpu.VMEM((features, depth), BF),
-            pltpu.SemaphoreType.DMA((4,)),
+            pltpu.VMEM((tokens, depth), BF),
+            pltpu.VMEM((parts // 2, 5 * n, 2 * features), BF),
+            pltpu.SemaphoreType.DMA((5,)),
+            pltpu.SemaphoreType.DMA((LT,)),
+            pltpu.SemaphoreType.DMA((parts,)),
         ],
         compiler_params=params(56),
         name="head",
-    )(timestep, hidden, mod_table, head_rows)
+    )(timestep.reshape(1, 1), hidden, mod_table, head_rows)
     send, conv_in = lax.optimization_barrier((send, conv_in))
     recv = lax.all_to_all(send, "mp", 0, 0, tiled=True)
     near_blocks, unit = spread(packed)

time: 62.7 us -> 63.3 us (level)
  Pallas kernels: 15.8 us -> 16.5 us
    pallas_call x1, Pallas kernels: 2.34 us -> 3.09 us  [body(): pl.pallas_call(functools.partial(head_kernel, parts), in_specs=[HBM] * 4,...]
  transfers between devices with their start and end apart: 6 -> 6, of which waited for: 3 -> 3; matrix products, arithmetic and copies ran while one was open for 1% -> 1% of each run, Pallas kernels for 11% -> 12%
where the time goes in v2:
time: 63.3 us; the launch traced here: 63 us
  blocking collectives  20.3 us (32%)
  Pallas kernels  16.5 us (26%)
  waiting for transfers between devices  14.1 us (22%)
  starting transfers between devices  9.53 us (15%)
  between operations  1.51 us (2%)
  other arithmetic  0.84 us (1%)
    all_to_all x1, blocking collectives, body(): contributions = lax.all_to_all(contribution, 'mp', 0, 0, tiled=True)  10.2 us
    all_to_all x1, blocking collectives, body(): all_sums = lax.all_to_all(sums, 'mp', 0, 0, tiled=True)  10.1 us
    all_to_all x1, waiting for transfers between devices, body(): recv = lax.all_to_all(send, 'mp', 0, 0, tiled=True)  10 us
    all_to_all x1, starting transfers between devices, body(): recv = lax.all_to_all(send, 'mp', 0, 0, tiled=True)  5.85 us
    pallas_call x1, Pallas kernels, body(): pl.pallas_call(functools.partial(backward_kernel, parts, cells), in_specs...  4.67 us
    ppermute x5, waiting for transfers between devices, exchange(): return lax.ppermute(block, axis, [(i, i ^ flip) for i in range(count)])  4.08 us
    ppermute x5, starting transfers between devices, exchange(): return lax.ppermute(block, axis, [(i, i ^ flip) for i in range(count)])  3.68 us
    pallas_call x1, Pallas kernels, body(): pl.pallas_call(functools.partial(near_kernel, parts, blocks), in_specs=[S...  3.21 us
  transfers between devices with their start and end apart: 6, of which 3 were waited for; matrix products, arithmetic and copies ran while one was open for 1% of the time, Pallas kernels for 12%

profile of v2, /device:TPU:0, one launch (start us, length us, event | category | flops | bytes accessed | tf_op | source)
XLA Modules:
  0.0 63.0 jit_solution(6791328363057310706)
XLA Ops:
  0.6 0.0 copy-start.7
  0.6 2.2 %pack.1.refs_0_ = bf16[9,96,384]{2,1,0:T(8,128)(2,1)} custom-call(bf16[27,96,384]{2,1,0:T(8,128)(2,1)} %bitcast.11), custom_call_target="tpu_custom_call" | custom-call | tf_op jit(solution)/shard_map/pack/pallas_call | solution.py:479
  2.9 0.0 copy-start.1
  2.9 0.0 copy-start.4
  2.9 3.0 %collective-permute-start = (bf16[9,96,384]{2,1,0:T(8,128)(2,1)}, bf16[9,96,384]{2,1,0:T(8,128)(2,1)S(1)}, u32[]{:S(2)}, u32[]{:S(2)}) collective-permute-start(bf16[9,96,384]{2,1,0:T(8,128)(2,1)} %pack.1.refs_0_), channel_id=1, source_target_pairs={{0,16},{8,24},{16,0},{24,8},{1,17},{9,25},{17,1},{25,9},{2,18},{10... | collective-permute-start | bytes 1990664 | tf_op jit(solution)/shard_map/ppermute | solution.py:424
  6.6 3.1 %head.1 = (bf16[512,640]{1,0:T(8,128)(2,1)}, f32[1,640]{1,0:T(1,128)}, bf16[8,160,128]{2,1,0:T(8,128)(2,1)}) custom-call(s32[1,1]{1,0:T(1,128)} %bitcast.8.step_hbm, bf16[512,640]{1,0:T(8,128)(2,1)} %hidden_hbm.1, bf16[50,2,640]{2,1,0:T(2,128)(2,1)} %mod_hbm.1, bf16[64,640]{1,0:T(8,128)(2,1)} %bitcast.9), custom_call_target="tpu_custom_call" | custom-call | tf_op jit(solution)/shard_map/head/pallas_call | solution.py:494
  9.7 5.8 %all-to-all-start = ((bf16[8,160,128]{2,1,0:T(8,128)(2,1)}), bf16[8,160,128]{2,1,0:T(8,128)(2,1)S(1)}, u32[]{:S(2)}, u32[]{:S(2)}) async-start(bf16[8,160,128]{2,1,0:T(8,128)(2,1)} %get-tuple-element.22), calls=%async_computation | async-start | bytes 655360 | tf_op jit(solution)/shard_map/all_to_all | solution.py:518
  15.5 0.0 collective-permute-start.1
  15.5 10.0 %all-to-all-done.recv_ref = bf16[8,160,128]{2,1,0:T(8,128)(2,1)S(1)} async-done(((bf16[8,160,128]{2,1,0:T(8,128)(2,1)}), bf16[8,160,128]{2,1,0:T(8,128)(2,1)S(1)}, u32[]{:S(2)}, u32[]{:S(2)}) %all-to-all-start) | async-done | bytes 327712 | tf_op jit(solution)/shard_map/all_to_all | solution.py:518
  25.5 0.0 collective-permute-done.refs_0_
  25.5 0.0 collective-permute-start.2
  25.6 0.0 copy-done.7
  25.6 0.1 broadcast_select_fusion.4
  25.8 0.2 concatenate.3.conv_ref
  26.0 0.0 collective-permute-done.1.refs_1_
  26.0 0.0 copy-done.1
  26.0 0.0 copy-done.4
  26.0 3.2 %near.1 = (f32[768,256]{1,0:T(8,128)S(1)}, bf16[2,8,64,768]{3,2,1,0:T(8,128)(2,1)S(1)}, f32[512,512]{1,0:T(8,128)S(1)}, bf16[9,192,384]{2,1,0:T(8,128)(2,1)S(1)}, bf16[2,256,2048]{2,1,0:T(8,128)(2,1)S(1)}) custom-call(s32[1]{0:T(128)} %bitcast.info_ref, bf16[8,160,128]{2,1,0:T(8,128)(2,1)S(1)} %all-to-all-done.recv_ref, ...), custom_call_target="tpu_custom_call" | custom-call | flops 4000000000 | bytes 10000000 | tf_op jit(solution)/shard_map/near/pallas_call | solution.py:529
  29.3 0.0 copy-start
  29.3 0.0 copy-start.5
  29.3 0.0 collective-permute-done.2.refs_1_
  29.3 1.8 %far.1 = (f32[8,8,128]{2,1,0:T(8,128)S(1)}, bf16[2,6,64,256]{3,2,1,0:T(8,128)(2,1)S(1)}) custom-call(s32[1]{0:T(128)} %bitcast.info_ref, f32[768,256]{1,0:T(8,128)S(1)} %get-tuple-element.25.near_ref, bf16[2,8,64,768]{3,2,1,0:T(8,128)(2,1)S(1)} %get-tuple-element.26.views, bf16[9,96,384]{2,1,0:T(8,128)(2,1)S(1)} %collective-permute-done.refs_0_, ...), custom_call_target="tpu_custom_call" | custom-call | tf_op jit(solution)/shard_map/far/pallas_call | solution.py:545
  31.1 10.1 %all_to_all.15.sums_ref = f32[8,8,128]{2,1,0:T(8,128)S(1)} all-to-all(f32[8,8,128]{2,1,0:T(8,128)S(1)} %get-tuple-element.28), channel_id=1, replica_groups=mesh['dp'=4,'mp'=8] {'mp'}, dimensions={0} | all-to-all | bytes 65536 | tf_op jit(solution)/shard_map/all_to_all | solution.py:557
  41.1 0.0 copy-done
  41.1 0.0 copy-done.5
  41.2 0.0 copy-start.2
  41.2 0.0 copy-start.3
  41.2 0.0 copy-start.6
  41.2 4.7 %backward.1 = (f32[1]{0:T(128)}, bf16[8,96,128]{2,1,0:T(8,128)(2,1)S(1)}) custom-call(s32[1]{0:T(128)} %bitcast.info_ref, f32[8,8,128]{2,1,0:T(8,128)S(1)} %all_to_all.15.sums_ref, bf16[384,1024]{1,0:T(8,128)(2,1)S(1)} %copy-done, f32[1,1024]{1,0:T(1,128)S(1)} %copy-done.5, bf16[2,6,64,256]{3,2,1,0:T(8,128)(2,1)S(1)} %get-tuple-element.29.second_ref, ...), custom_call_target="tpu_custom_call" | custom-call | tf_op jit(solution)/shard_map/backward/pallas_call | solution.py:559
  45.9 10.2 %all_to_all.16.recv_ref = bf16[8,96,128]{2,1,0:T(8,128)(2,1)S(1)} all-to-all(bf16[8,96,128]{2,1,0:T(8,128)(2,1)S(1)} %get-tuple-element.34), channel_id=1, replica_groups=mesh['dp'=4,'mp'=8] {'mp'}, dimensions={0} | all-to-all | bytes 393216 | tf_op jit(solution)/shard_map/all_to_all | solution.py:571
  56.0 0.0 copy-done.2
  56.0 0.3 token_.1
  56.4 0.1 collective-permute-start.3
  56.5 1.3 %collective-permute-done.3 = bf16[64,640]{1,0:T(8,128)(2,1)S(1)} collective-permute-done((bf16[64,640]{1,0:T(8,128)(2,1)S(1)}, bf16[64,640]{1,0:T(8,128)(2,1)S(1)}, u32[]{:S(2)}, u32[]{:S(2)}) %collective-permute-start.3) | collective-permute-done | bytes 81952 | tf_op jit(solution)/shard_map/ppermute | solution.py:424
  57.7 0.6 collective-permute-start.4
  58.4 0.0 copy-done.3
  58.4 0.0 copy-done.6
  58.4 1.2 %hidden_grad.1 = bf16[512,640]{1,0:T(8,128)(2,1)} custom-call(bf16[512,64]{1,0:T(8,128)(2,1)S(1)} %get-tuple-element.37.tokens_ref, bf16[64,640]{1,0:T(8,128)(2,1)S(1)} %bitcast.10, f32[1,640]{1,0:T(1,128)S(1)} %copy-done.6), custom_call_target="tpu_custom_call" | custom-call | tf_op jit(solution)/shard_map/hidden_grad/pallas_call | solution.py:590
  59.5 2.8 %collective-permute-done.4 = bf16[64,640]{1,0:T(8,128)(2,1)S(1)} collective-permute-done((bf16[64,640]{1,0:T(8,128)(2,1)S(1)}, bf16[64,640]{1,0:T(8,128)(2,1)S(1)}, u32[]{:S(2)}, u32[]{:S(2)}) %collective-permute-start.4) | collective-permute-done | bytes 81952 | tf_op jit(solution)/shard_map/ppermute | solution.py:424
  62.3 0.7 %add_bitcast_fusion = f32[640,64]{0,1:T(8,128)} fusion(bf16[64,640]{1,0:T(8,128)(2,1)S(1)} %collective-permute-done.4, bf16[64,640]{1,0:T(8,128)(2,1)S(1)} %add_convert_fusion), kind=kLoop, calls=%fused_computation.1 | loop fusion | flops 122880 | bytes 327680 | tf_op jit(solution)/shard_map/transpose | solution.py:599
  (3 shorter events, 0.1 us)
Async XLA Ops:
  0.6 24.9 %copy-start.7 = (bf16[16,27,384]{2,0,1:T(8,128)(2,1)S(1)}, bf16[16,27,384]{2,0,1:T(8,128)(2,1)}, u32[]{:S(2)}) copy-start(bf16[16,27,384]{2,0,1:T(8,128)(2,1)} %param.13) | copy-start | bytes 995332
  2.9 23.1 %copy-start.1 = (bf16[9,96,384]{2,1,0:T(8,128)(2,1)S(1)}, bf16[9,96,384]{2,1,0:T(8,128)(2,1)}, u32[]{:S(2)}) copy-start(bf16[9,96,384]{2,1,0:T(8,128)(2,1)} %pack.1.refs_0_) | copy-start | bytes 1990660
  2.9 23.1 %copy-start.4 = (bf16[576,256]{1,0:T(8,128)(2,1)S(1)}, bf16[576,256]{1,0:T(8,128)(2,1)}, u32[]{:S(2)}) copy-start(bf16[576,256]{1,0:T(8,128)(2,1)} %constant.56.clone.pick_ref) | copy-start | bytes 884740
  2.9 22.6 %collective-permute-start = (bf16[9,96,384]{2,1,0:T(8,128)(2,1)}, bf16[9,96,384]{2,1,0:T(8,128)(2,1)S(1)}, u32[]{:S(2)}, u32[]{:S(2)}) collective-permute-start(bf16[9,96,384]{2,1,0:T(8,128)(2,1)} %pack.1.refs_0_), channel_id=1, source_target_pairs={{0,16},{8,24},{16,0},{24,8},{1,17},{9,25},{17,1},{25,9},{2,18},{10... | collective-permute-start | bytes 1990664 | tf_op jit(solution)/shard_map/ppermute | solution.py:424
  9.7 15.9 %all-to-all-start = ((bf16[8,160,128]{2,1,0:T(8,128)(2,1)}), bf16[8,160,128]{2,1,0:T(8,128)(2,1)S(1)}, u32[]{:S(2)}, u32[]{:S(2)}) async-start(bf16[8,160,128]{2,1,0:T(8,128)(2,1)} %get-tuple-element.22), calls=%async_computation | async-start | bytes 655360 | tf_op jit(solution)/shard_map/all_to_all | solution.py:518
  15.5 10.5 %collective-permute-start.1 = (bf16[9,96,384]{2,1,0:T(8,128)(2,1)}, bf16[9,96,384]{2,1,0:T(8,128)(2,1)}, u32[]{:S(2)}, u32[]{:S(2)}) collective-permute-start(bf16[9,96,384]{2,1,0:T(8,128)(2,1)} %pack.1.refs_0_), channel_id=1, source_target_pairs={{0,8},{8,0},{16,24},{24,16},{1,9},{9,1},{17,25},{25,17},{2,10},{10... | collective-permute-start | bytes 1990664 | tf_op jit(solution)/shard_map/ppermute | solution.py:424
  25.5 3.7 %collective-permute-start.2 = (bf16[9,96,384]{2,1,0:T(8,128)(2,1)S(1)}, bf16[9,96,384]{2,1,0:T(8,128)(2,1)S(1)}, u32[]{:S(2)}, u32[]{:S(2)}) collective-permute-start(bf16[9,96,384]{2,1,0:T(8,128)(2,1)S(1)} %collective-permute-done.refs_0_), channel_id=1, source_target_pairs={{0,8},{8,0},{16,24},{24,16},{1,9},{9,1},{17,25},{25,17},{2,10},{10... | collective-permute-start | bytes 1990664 | tf_op jit(solution)/shard_map/ppermute | solution.py:424
  29.3 11.9 %copy-start = (bf16[384,1024]{1,0:T(8,128)(2,1)S(1)}, bf16[384,1024]{1,0:T(8,128)(2,1)}, u32[]{:S(2)}) copy-start(bf16[384,1024]{1,0:T(8,128)(2,1)} %patch_ref.1) | copy-start | bytes 2359300
  29.3 11.9 %copy-start.5 = (f32[1,1024]{1,0:T(1,128)S(1)}, f32[1,1024]{1,0:T(1,128)}, u32[]{:S(2)}) copy-start(f32[1,1024]{1,0:T(1,128)} %text_ref.1) | copy-start | bytes 12292
  41.2 14.9 %copy-start.2 = (bf16[512,640]{1,0:T(8,128)(2,1)S(1)}, bf16[512,640]{1,0:T(8,128)(2,1)}, u32[]{:S(2)}) copy-start(bf16[512,640]{1,0:T(8,128)(2,1)} %get-tuple-element.35.modulated_ref) | copy-start | bytes 1966084
  41.2 17.2 %copy-start.3 = (bf16[640,64]{0,1:T(8,128)(2,1)S(1)}, bf16[640,64]{0,1:T(8,128)(2,1)}, u32[]{:S(2)}) copy-start(bf16[640,64]{0,1:T(8,128)(2,1)} %param.12) | copy-start | bytes 245764
  41.2 17.2 %copy-start.6 = (f32[1,640]{1,0:T(1,128)S(1)}, f32[1,640]{1,0:T(1,128)}, u32[]{:S(2)}) copy-start(f32[1,640]{1,0:T(1,128)} %get-tuple-element.38.gain_ref) | copy-start | bytes 7684
  56.4 1.3 %collective-permute-start.3 = (bf16[64,640]{1,0:T(8,128)(2,1)S(1)}, bf16[64,640]{1,0:T(8,128)(2,1)S(1)}, u32[]{:S(2)}, u32[]{:S(2)}) collective-permute-start(bf16[64,640]{1,0:T(8,128)(2,1)S(1)} %get-tuple-element.36), channel_id=1, source_target_pairs={{0,8},{8,0},{16,24},{24,16},{1,9},{9,1},{17,25},{25,17},{2,10},{10... | collective-permute-start | bytes 245768 | tf_op jit(solution)/shard_map/ppermute | solution.py:424
  57.7 4.6 %collective-permute-start.4 = (bf16[64,640]{1,0:T(8,128)(2,1)S(1)}, bf16[64,640]{1,0:T(8,128)(2,1)S(1)}, u32[]{:S(2)}, u32[]{:S(2)}) collective-permute-start(bf16[64,640]{1,0:T(8,128)(2,1)S(1)} %add_convert_fusion), channel_id=1, source_target_pairs={{0,16},{8,24},{16,0},{24,8},{1,17},{9,25},{17,1},{25,9},{2,18},{10... | collective-permute-start | bytes 245768 | tf_op jit(solution)/shard_map/ppermute | solution.py:424

commit v3 on v2

--- a/solution.py
+++ b/solution.py
@@ -23,7 +23,7 @@
 
 
 def sigmoid(value):
-    return 1.0 / (1.0 + jnp.exp(-value))
+    return 0.5 + 0.5 * jnp.tanh(0.5 * value)
 
 
 def dot(left, right):
@@ -80,19 +80,18 @@
 
 
 def head_kernel(
-    parts, step_hbm, hidden_hbm, mod_hbm, head_hbm, modulated_hbm, gain_ref, send_hbm, step_ref, hidden_ref, mod_ref,
-    head_ref, modulated, blocks, in_sems, out_sems, send_sems
+    parts, step_ref, hidden_hbm, mod_hbm, head_hbm, modulated_hbm, gain_ref, send_hbm, hidden_ref, mod_ref, head_ref,
+    modulated, blocks, in_sems, out_sems, send_sems
 ):
     n = PAIR_COLS
     half = hidden_ref.shape[0] // LT
     frames = [pl.ds(t * half, half) for t in range(LT)]
     small = [
-        pltpu.make_async_copy(step_hbm, step_ref, in_sems.at[0]),
-        pltpu.make_async_copy(mod_hbm, mod_ref, in_sems.at[1]),
-        pltpu.make_async_copy(head_hbm, head_ref, in_sems.at[2]),
+        pltpu.make_async_copy(mod_hbm, mod_ref, in_sems.at[0]),
+        pltpu.make_async_copy(head_hbm, head_ref, in_sems.at[1]),
     ]
     large = [
-        pltpu.make_async_copy(hidden_hbm.at[rows], hidden_ref.at[rows], in_sems.at[3 + t])
+        pltpu.make_async_copy(hidden_hbm.at[rows], hidden_ref.at[rows], in_sems.at[2 + t])
         for t, rows in enumerate(frames)
     ]
     results = [
@@ -102,10 +101,7 @@
         copy.start()
     for copy in small:
         copy.wait()
-    step = jnp.broadcast_to(step_ref[...], mod_ref.shape[1:])
-    mod = jnp.zeros(mod_ref.shape[1:], F32)
-    for i in range(mod_ref.shape[0]):
-        mod = mod + jnp.where(step == i, mod_ref[i].astype(F32), 0.0)
+    mod = mod_ref[step_ref[0]].astype(F32)
     gain = 1.0 + mod[1:2]
     gain_ref[...] = gain
     terms = []
@@ -122,15 +118,15 @@
     def pair_row(i):
         return blank if i < 0 or i >= parts else wide[i * n : (i + 1) * n]
 
-    sends = []
     for part in range(0, parts, 2):
         outer = jnp.where(lower, pair_row(part - 2), pair_row(part + 3))
         rows = [pair_row(part + i) for i in range(-1, 3)] + [outer]
         blocks[part // 2] = jnp.concatenate(rows, axis=0).astype(BF)
         for i in (part, part + 1):
-            sends.append(pltpu.make_async_copy(blocks.at[part // 2], send_hbm.at[i], send_sems.at[i]))
-            sends[-1].start()
-    for result in results + sends:
+            results.append(pltpu.make_async_copy(blocks.at[part // 2], send_hbm.at[i], send_sems.at[i]))
+            results[-1].start()
+
+    for result in results:
         result.wait()
 
 
@@ -161,7 +157,7 @@
     for ref in refs:
         half = ref[pair, :, 2 * TILE :]
         lane = lax.broadcasted_iota(jnp.int32, half.shape, 1)
-        half = jnp.where((lane < TILE // 2) == (side == 0), half, jnp.zeros_like(half))
+        half = half * jnp.where((lane < TILE // 2) == (side == 0), 1.0, 0.0).astype(BF)
         blocks.append(jnp.concatenate([ref[pair, :, side * TILE : (side + 1) * TILE], half], axis=1))
     filled = sum(block.shape[0] for block in blocks)
     return jnp.concatenate(blocks + [jnp.zeros((DEEP - filled, 2 * TILE), BF)], axis=0)
@@ -445,6 +441,15 @@
     return [blocks[held] for held in sorted(blocks)], unit
 
 
+def half_sum(term):
+    total, flip = term.astype(F32), 1
+    while flip < lax.axis_size("dp") // 2:
+        other = exchange(term, "dp", flip)
+        total = total + other.astype(F32)
+        term, flip = total.astype(BF), 2 * flip
+    return total
+
+
 def local_channels(weight, unit):
     count = lax.axis_size("dp") // unit
     place = lax.axis_index("dp") // unit
@@ -493,7 +498,7 @@
     distant = exchange(packed, "dp", far)
     modulated, gain, send = pl.pallas_call(
         functools.partial(head_kernel, parts),
-        in_specs=[HBM] * 4,
+        in_specs=[SMEM] + [HBM] * 3,
         out_specs=[HBM, VMEM, HBM],
         out_shape=[
             jax.ShapeDtypeStruct((tokens, depth), BF),
@@ -501,19 +506,18 @@
             jax.ShapeDtypeStruct((parts, 5 * n, 2 * features), BF),
         ],
         scratch_shapes=[
-            pltpu.VMEM((1, 1), jnp.int32),
             pltpu.VMEM((tokens, depth), BF),
             pltpu.VMEM(mod_table.shape, BF),
             pltpu.VMEM((features, depth), BF),
             pltpu.VMEM((tokens, depth), BF),
             pltpu.VMEM((parts // 2, 5 * n, 2 * features), BF),
-            pltpu.SemaphoreType.DMA((5,)),
+            pltpu.SemaphoreType.DMA((2 + LT,)),
             pltpu.SemaphoreType.DMA((LT,)),
             pltpu.SemaphoreType.DMA((parts,)),
         ],
         compiler_params=params(56),
         name="head",
-    )(timestep.reshape(1, 1), hidden, mod_table, head_rows)
+    )(timestep, hidden, mod_table, head_rows)
     send, conv_in = lax.optimization_barrier((send, conv_in))
     recv = lax.all_to_all(send, "mp", 0, 0, tiled=True)
     near_blocks, unit = spread(packed)
@@ -581,12 +585,7 @@
         compiler_params=params(8),
         name="token",
     )(contributions, modulated)
-    flip = 1
-    while flip < far:
-        other = exchange(head_term, "dp", flip)
-        head_term = (head_term.astype(F32) + other.astype(F32)).astype(BF)
-        flip *= 2
-    head_other = exchange(head_term, "dp", far)
+    from_far = exchange(head_term, "dp", far)
     hidden_grad = pl.pallas_call(
         hidden_kernel,
         in_specs=[VMEM] * 3,
@@ -595,7 +594,7 @@
         compiler_params=params(8),
         name="hidden_grad",
     )(token_grad, head_rows, gain)
-    head_grad = head_term.astype(F32) + head_other.astype(F32)
+    head_grad = half_sum(head_term) + half_sum(from_far)
     return (reward, head_grad.T, hidden_grad)
 
 

time: 63.3 us -> 63.3 us (level)
    ppermute x5 -> x6, starting transfers between devices: 3.68 us -> 3.6 us  [exchange(): return lax.ppermute(block, axis, [(i, i ^ flip) for i in range(count)])]
    ppermute x5 -> x6, waiting for transfers between devices: 4.08 us -> 4.04 us  [exchange(): return lax.ppermute(block, axis, [(i, i ^ flip) for i in range(count)])]
  transfers between devices with their start and end apart: 6 -> 7, of which waited for: 3 -> 3; matrix products, arithmetic and copies ran while one was open for 1% -> 1% of each run, Pallas kernels for 12% -> 12%
where the time goes in v3:
time: 63.3 us; the launch traced here: 63 us
  blocking collectives  20.3 us (32%)
  Pallas kernels  16.5 us (26%)
  waiting for transfers between devices  14.1 us (22%)
  starting transfers between devices  9.45 us (15%)
  between operations  1.5 us (2%)
  other arithmetic  0.84 us (1%)
    all_to_all x1, blocking collectives, body(): contributions = lax.all_to_all(contribution, 'mp', 0, 0, tiled=True)  10.2 us
    all_to_all x1, blocking collectives, body(): all_sums = lax.all_to_all(sums, 'mp', 0, 0, tiled=True)  10.1 us
    all_to_all x1, waiting for transfers between devices, body(): recv = lax.all_to_all(send, 'mp', 0, 0, tiled=True)  10 us
    all_to_all x1, starting transfers between devices, body(): recv = lax.all_to_all(send, 'mp', 0, 0, tiled=True)  5.85 us
    pallas_call x1, Pallas kernels, body(): pl.pallas_call(functools.partial(backward_kernel, parts, cells), in_specs...  4.68 us
    ppermute x6, waiting for transfers between devices, exchange(): return lax.ppermute(block, axis, [(i, i ^ flip) for i in range(count)])  4.04 us
    ppermute x6, starting transfers between devices, exchange(): return lax.ppermute(block, axis, [(i, i ^ flip) for i in range(count)])  3.6 us
    pallas_call x1, Pallas kernels, body(): pl.pallas_call(functools.partial(near_kernel, parts, blocks), in_specs=[S...  3.32 us
  transfers between devices with their start and end apart: 7, of which 3 were waited for; matrix products, arithmetic and copies ran while one was open for 1% of the time, Pallas kernels for 12%

profile of v3, /device:TPU:0, one launch (start us, length us, event | category | flops | bytes accessed | tf_op | source)
XLA Modules:
  0.0 63.0 jit_solution(12740520579501099171)
XLA Ops:
  0.6 0.0 copy-start.7
  0.6 2.2 %pack.1.refs_0_ = bf16[9,96,384]{2,1,0:T(8,128)(2,1)} custom-call(bf16[27,96,384]{2,1,0:T(8,128)(2,1)} %bitcast.9), custom_call_target="tpu_custom_call" | custom-call | tf_op jit(solution)/shard_map/pack/pallas_call | solution.py:484
  2.9 0.0 copy-start.1
  2.9 0.0 copy-start.4
  2.9 3.0 %collective-permute-start = (bf16[9,96,384]{2,1,0:T(8,128)(2,1)}, bf16[9,96,384]{2,1,0:T(8,128)(2,1)S(1)}, u32[]{:S(2)}, u32[]{:S(2)}) collective-permute-start(bf16[9,96,384]{2,1,0:T(8,128)(2,1)} %pack.1.refs_0_), channel_id=1, source_target_pairs={{0,16},{8,24},{16,0},{24,8},{1,17},{9,25},{17,1},{25,9},{2,18},{10... | collective-permute-start | bytes 1990664 | tf_op jit(solution)/shard_map/ppermute | solution.py:420
  6.6 3.1 %head.1 = (bf16[512,640]{1,0:T(8,128)(2,1)}, f32[1,640]{1,0:T(1,128)}, bf16[8,160,128]{2,1,0:T(8,128)(2,1)}) custom-call(s32[1]{0:T(128)S(6)} %copy.12.step_ref, bf16[512,640]{1,0:T(8,128)(2,1)} %hidden_hbm.1, bf16[50,2,640]{2,1,0:T(2,128)(2,1)} %mod_hbm.1, bf16[64,640]{1,0:T(8,128)(2,1)} %bitcast.7), custom_call_target="tpu_custom_call" | custom-call | tf_op jit(solution)/shard_map/head/pallas_call | solution.py:499
  9.6 5.8 %all-to-all-start = ((bf16[8,160,128]{2,1,0:T(8,128)(2,1)}), bf16[8,160,128]{2,1,0:T(8,128)(2,1)S(1)}, u32[]{:S(2)}, u32[]{:S(2)}) async-start(bf16[8,160,128]{2,1,0:T(8,128)(2,1)} %get-tuple-element.22), calls=%async_computation | async-start | bytes 655360 | tf_op jit(solution)/shard_map/all_to_all | solution.py:522
  15.5 0.0 collective-permute-start.1
  15.5 10.0 %all-to-all-done.recv_ref = bf16[8,160,128]{2,1,0:T(8,128)(2,1)S(1)} async-done(((bf16[8,160,128]{2,1,0:T(8,128)(2,1)}), bf16[8,160,128]{2,1,0:T(8,128)(2,1)S(1)}, u32[]{:S(2)}, u32[]{:S(2)}) %all-to-all-start) | async-done | bytes 327712 | tf_op jit(solution)/shard_map/all_to_all | solution.py:522
  25.5 0.0 collective-permute-done.refs_0_
  25.5 0.0 collective-permute-start.2
  25.5 0.0 copy-done.7
  25.6 0.1 broadcast_select_fusion.4
  25.8 0.2 concatenate.3.conv_ref
  26.0 0.0 collective-permute-done.1.refs_1_
  26.0 0.0 copy-done.1
  26.0 0.0 copy-done.4
  26.0 3.3 %near.1 = (f32[768,256]{1,0:T(8,128)S(1)}, bf16[2,8,64,768]{3,2,1,0:T(8,128)(2,1)S(1)}, f32[512,512]{1,0:T(8,128)S(1)}, bf16[9,192,384]{2,1,0:T(8,128)(2,1)S(1)}, bf16[2,256,2048]{2,1,0:T(8,128)(2,1)S(1)}) custom-call(s32[1]{0:T(128)} %bitcast.info_ref, bf16[8,160,128]{2,1,0:T(8,128)(2,1)S(1)} %all-to-all-done.recv_ref, ...), custom_call_target="tpu_custom_call" | custom-call | flops 4000000000 | bytes 10000000 | tf_op jit(solution)/shard_map/near/pallas_call | solution.py:533
  29.4 0.0 copy-start
  29.4 0.0 copy-start.5
  29.4 0.0 collective-permute-done.2.refs_1_
  29.4 1.8 %far.1 = (f32[8,8,128]{2,1,0:T(8,128)S(1)}, bf16[2,6,64,256]{3,2,1,0:T(8,128)(2,1)S(1)}) custom-call(s32[1]{0:T(128)} %bitcast.info_ref, f32[768,256]{1,0:T(8,128)S(1)} %get-tuple-element.25.near_ref, bf16[2,8,64,768]{3,2,1,0:T(8,128)(2,1)S(1)} %get-tuple-element.26.views, bf16[9,96,384]{2,1,0:T(8,128)(2,1)S(1)} %collective-permute-done.refs_0_, ...), custom_call_target="tpu_custom_call" | custom-call | tf_op jit(solution)/shard_map/far/pallas_call | solution.py:549
  31.1 10.1 %all_to_all.15.sums_ref = f32[8,8,128]{2,1,0:T(8,128)S(1)} all-to-all(f32[8,8,128]{2,1,0:T(8,128)S(1)} %get-tuple-element.28), channel_id=1, replica_groups=mesh['dp'=4,'mp'=8] {'mp'}, dimensions={0} | all-to-all | bytes 65536 | tf_op jit(solution)/shard_map/all_to_all | solution.py:561
  41.2 0.0 copy-done
  41.2 0.0 copy-done.5
  41.2 0.0 copy-start.2
  41.2 0.0 copy-start.3
  41.2 0.0 copy-start.6
  41.2 4.7 %backward.1 = (f32[1]{0:T(128)}, bf16[8,96,128]{2,1,0:T(8,128)(2,1)S(1)}) custom-call(s32[1]{0:T(128)} %bitcast.info_ref, f32[8,8,128]{2,1,0:T(8,128)S(1)} %all_to_all.15.sums_ref, bf16[384,1024]{1,0:T(8,128)(2,1)S(1)} %copy-done, f32[1,1024]{1,0:T(1,128)S(1)} %copy-done.5, bf16[2,6,64,256]{3,2,1,0:T(8,128)(2,1)S(1)} %get-tuple-element.29.second_ref, ...), custom_call_target="tpu_custom_call" | custom-call | tf_op jit(solution)/shard_map/backward/pallas_call | solution.py:563
  45.9 10.2 %all_to_all.16.recv_ref = bf16[8,96,128]{2,1,0:T(8,128)(2,1)S(1)} all-to-all(bf16[8,96,128]{2,1,0:T(8,128)(2,1)S(1)} %get-tuple-element.34), channel_id=1, replica_groups=mesh['dp'=4,'mp'=8] {'mp'}, dimensions={0} | all-to-all | bytes 393216 | tf_op jit(solution)/shard_map/all_to_all | solution.py:575
  56.1 0.0 copy-done.2
  56.1 0.3 token_.1
  56.5 0.6 collective-permute-start.4
  57.0 0.0 collective-permute-start.3
  57.1 3.9 %collective-permute-done.4 = bf16[64,640]{1,0:T(8,128)(2,1)S(1)} collective-permute-done((bf16[64,640]{1,0:T(8,128)(2,1)S(1)}, bf16[64,640]{1,0:T(8,128)(2,1)S(1)}, u32[]{:S(2)}, u32[]{:S(2)}) %collective-permute-start.4) | collective-permute-done | bytes 81952 | tf_op jit(solution)/shard_map/ppermute | solution.py:420
  61.0 0.0 collective-permute-start.5
  61.0 0.0 copy-done.3
  61.0 0.0 copy-done.6
  61.0 1.1 %hidden_grad.1 = bf16[512,640]{1,0:T(8,128)(2,1)} custom-call(bf16[512,64]{1,0:T(8,128)(2,1)S(1)} %get-tuple-element.37.tokens_ref, bf16[64,640]{1,0:T(8,128)(2,1)S(1)} %bitcast.8, f32[1,640]{1,0:T(1,128)S(1)} %copy-done.6), custom_call_target="tpu_custom_call" | custom-call | tf_op jit(solution)/shard_map/hidden_grad/pallas_call | solution.py:589
  62.1 0.0 collective-permute-done.3
  62.1 0.1 collective-permute-done.5
  62.2 0.7 %add_bitcast_fusion = f32[640,64]{0,1:T(8,128)} fusion(bf16[64,640]{1,0:T(8,128)(2,1)S(1)} %collective-permute-done.5, bf16[64,640]{1,0:T(8,128)(2,1)S(1)} %collective-permute-done.4, bf16[64,640]{1,0:T(8,128)(2,1)S(1)} %collective-permute-done.3, bf16[64,640]{1,0:T(8,128)(2,1)S(1)} %get-tuple-element.36), kind=kLoop, calls=%fused_computation.1 | loop fusion | flops 286720 | bytes 491520 | tf_op jit(solution)/shard_map/transpose | solution.py:598
  (2 shorter events, 0.0 us)
Async XLA Ops:
  0.6 24.9 %copy-start.7 = (bf16[16,27,384]{2,0,1:T(8,128)(2,1)S(1)}, bf16[16,27,384]{2,0,1:T(8,128)(2,1)}, u32[]{:S(2)}) copy-start(bf16[16,27,384]{2,0,1:T(8,128)(2,1)} %param.13) | copy-start | bytes 995332
  2.9 23.1 %copy-start.1 = (bf16[9,96,384]{2,1,0:T(8,128)(2,1)S(1)}, bf16[9,96,384]{2,1,0:T(8,128)(2,1)}, u32[]{:S(2)}) copy-start(bf16[9,96,384]{2,1,0:T(8,128)(2,1)} %pack.1.refs_0_) | copy-start | bytes 1990660
  2.9 23.1 %copy-start.4 = (bf16[576,256]{1,0:T(8,128)(2,1)S(1)}, bf16[576,256]{1,0:T(8,128)(2,1)}, u32[]{:S(2)}) copy-start(bf16[576,256]{1,0:T(8,128)(2,1)} %constant.56.clone.pick_ref) | copy-start | bytes 884740
  2.9 22.6 %collective-permute-start = (bf16[9,96,384]{2,1,0:T(8,128)(2,1)}, bf16[9,96,384]{2,1,0:T(8,128)(2,1)S(1)}, u32[]{:S(2)}, u32[]{:S(2)}) collective-permute-start(bf16[9,96,384]{2,1,0:T(8,128)(2,1)} %pack.1.refs_0_), channel_id=1, source_target_pairs={{0,16},{8,24},{16,0},{24,8},{1,17},{9,25},{17,1},{25,9},{2,18},{10... | collective-permute-start | bytes 1990664 | tf_op jit(solution)/shard_map/ppermute | solution.py:420
  9.6 15.9 %all-to-all-start = ((bf16[8,160,128]{2,1,0:T(8,128)(2,1)}), bf16[8,160,128]{2,1,0:T(8,128)(2,1)S(1)}, u32[]{:S(2)}, u32[]{:S(2)}) async-start(bf16[8,160,128]{2,1,0:T(8,128)(2,1)} %get-tuple-element.22), calls=%async_computation | async-start | bytes 655360 | tf_op jit(solution)/shard_map/all_to_all | solution.py:522
  15.5 10.5 %collective-permute-start.1 = (bf16[9,96,384]{2,1,0:T(8,128)(2,1)}, bf16[9,96,384]{2,1,0:T(8,128)(2,1)}, u32[]{:S(2)}, u32[]{:S(2)}) collective-permute-start(bf16[9,96,384]{2,1,0:T(8,128)(2,1)} %pack.1.refs_0_), channel_id=1, source_target_pairs={{0,8},{8,0},{16,24},{24,16},{1,9},{9,1},{17,25},{25,17},{2,10},{10... | collective-permute-start | bytes 1990664 | tf_op jit(solution)/shard_map/ppermute | solution.py:420
  25.5 3.8 %collective-permute-start.2 = (bf16[9,96,384]{2,1,0:T(8,128)(2,1)S(1)}, bf16[9,96,384]{2,1,0:T(8,128)(2,1)S(1)}, u32[]{:S(2)}, u32[]{:S(2)}) collective-permute-start(bf16[9,96,384]{2,1,0:T(8,128)(2,1)S(1)} %collective-permute-done.refs_0_), channel_id=1, source_target_pairs={{0,8},{8,0},{16,24},{24,16},{1,9},{9,1},{17,25},{25,17},{2,10},{10... | collective-permute-start | bytes 1990664 | tf_op jit(solution)/shard_map/ppermute | solution.py:420
  29.4 11.9 %copy-start = (bf16[384,1024]{1,0:T(8,128)(2,1)S(1)}, bf16[384,1024]{1,0:T(8,128)(2,1)}, u32[]{:S(2)}) copy-start(bf16[384,1024]{1,0:T(8,128)(2,1)} %patch_ref.1) | copy-start | bytes 2359300
  29.4 11.9 %copy-start.5 = (f32[1,1024]{1,0:T(1,128)S(1)}, f32[1,1024]{1,0:T(1,128)}, u32[]{:S(2)}) copy-start(f32[1,1024]{1,0:T(1,128)} %text_ref.1) | copy-start | bytes 12292
  41.2 14.9 %copy-start.2 = (bf16[512,640]{1,0:T(8,128)(2,1)S(1)}, bf16[512,640]{1,0:T(8,128)(2,1)}, u32[]{:S(2)}) copy-start(bf16[512,640]{1,0:T(8,128)(2,1)} %get-tuple-element.35.modulated_ref) | copy-start | bytes 1966084
  41.2 19.7 %copy-start.3 = (bf16[640,64]{0,1:T(8,128)(2,1)S(1)}, bf16[640,64]{0,1:T(8,128)(2,1)}, u32[]{:S(2)}) copy-start(bf16[640,64]{0,1:T(8,128)(2,1)} %param.12) | copy-start | bytes 245764
  41.2 19.7 %copy-start.6 = (f32[1,640]{1,0:T(1,128)S(1)}, f32[1,640]{1,0:T(1,128)}, u32[]{:S(2)}) copy-start(f32[1,640]{1,0:T(1,128)} %get-tuple-element.38.gain_ref) | copy-start | bytes 7684
  56.5 4.5 %collective-permute-start.4 = (bf16[64,640]{1,0:T(8,128)(2,1)S(1)}, bf16[64,640]{1,0:T(8,128)(2,1)S(1)}, u32[]{:S(2)}, u32[]{:S(2)}) collective-permute-start(bf16[64,640]{1,0:T(8,128)(2,1)S(1)} %get-tuple-element.36), channel_id=1, source_target_pairs={{0,16},{8,24},{16,0},{24,8},{1,17},{9,25},{17,1},{25,9},{2,18},{10... | collective-permute-start | bytes 245768 | tf_op jit(solution)/shard_map/ppermute | solution.py:420
  57.0 5.1 %collective-permute-start.3 = (bf16[64,640]{1,0:T(8,128)(2,1)S(1)}, bf16[64,640]{1,0:T(8,128)(2,1)S(1)}, u32[]{:S(2)}, u32[]{:S(2)}) collective-permute-start(bf16[64,640]{1,0:T(8,128)(2,1)S(1)} %get-tuple-element.36), channel_id=1, source_target_pairs={{0,8},{8,0},{16,24},{24,16},{1,9},{9,1},{17,25},{25,17},{2,10},{10... | collective-permute-start | bytes 245768 | tf_op jit(solution)/shard_map/ppermute | solution.py:420
  61.0 1.3 %collective-permute-start.5 = (bf16[64,640]{1,0:T(8,128)(2,1)S(1)}, bf16[64,640]{1,0:T(8,128)(2,1)S(1)}, u32[]{:S(2)}, u32[]{:S(2)}) collective-permute-start(bf16[64,640]{1,0:T(8,128)(2,1)S(1)} %collective-permute-done.4), channel_id=1, source_target_pairs={{0,8},{8,0},{16,24},{24,16},{1,9},{9,1},{17,25},{25,17},{2,10},{10... | collective-permute-start | bytes 245768 | tf_op jit(solution)/shard_map/ppermute | solution.py:420

commit v4 on v3

--- a/solution.py
+++ b/solution.py
@@ -23,7 +23,7 @@
 
 
 def sigmoid(value):
-    return 0.5 + 0.5 * jnp.tanh(0.5 * value)
+    return pl.reciprocal(1.0 + jnp.exp(-value), approx=True)
 
 
 def dot(left, right):
@@ -80,38 +80,27 @@
 
 
 def head_kernel(
-    parts, step_ref, hidden_hbm, mod_hbm, head_hbm, modulated_hbm, gain_ref, send_hbm, hidden_ref, mod_ref, head_ref,
-    modulated, blocks, in_sems, out_sems, send_sems
+    parts, step_ref, hidden_hbm, mod_hbm, head_hbm, modulated_ref, gain_ref, send_ref, hidden_ref, mod_ref, head_ref,
+    sems
 ):
-    n = PAIR_COLS
-    half = hidden_ref.shape[0] // LT
-    frames = [pl.ds(t * half, half) for t in range(LT)]
-    small = [
-        pltpu.make_async_copy(mod_hbm, mod_ref, in_sems.at[0]),
-        pltpu.make_async_copy(head_hbm, head_ref, in_sems.at[1]),
+    copies = [
+        pltpu.make_async_copy(hidden_hbm, hidden_ref, sems.at[0]),
+        pltpu.make_async_copy(mod_hbm, mod_ref, sems.at[1]),
+        pltpu.make_async_copy(head_hbm, head_ref, sems.at[2]),
     ]
-    large = [
-        pltpu.make_async_copy(hidden_hbm.at[rows], hidden_ref.at[rows], in_sems.at[2 + t])
-        for t, rows in enumerate(frames)
-    ]
-    results = [
-        pltpu.make_async_copy(modulated.at[rows], modulated_hbm.at[rows], out_sems.at[t]) for t, rows in enumerate(frames)
-    ]
-    for copy in small + large:
+    for copy in copies:
         copy.start()
-    for copy in small:
+    for copy in copies:
         copy.wait()
     mod = mod_ref[step_ref[0]].astype(F32)
     gain = 1.0 + mod[1:2]
+    modulated = (hidden_ref[...].astype(F32) * gain + mod[0:1]).astype(BF)
+    modulated_ref[...] = modulated
     gain_ref[...] = gain
-    terms = []
-    for t, rows in enumerate(frames):
-        large[t].wait()
-        values = (hidden_ref[rows].astype(F32) * gain + mod[0:1]).astype(BF)
-        modulated[rows] = values
-        results[t].start()
-        terms.append(dot_nt(values, head_ref[...]))
-    wide = jnp.concatenate(terms, axis=1)
+    terms = dot_nt(modulated, head_ref[...])
+    half = terms.shape[0] // 2
+    wide = jnp.concatenate([terms[:half], terms[half:]], axis=1)
+    n = PAIR_COLS
     blank = jnp.zeros((n, wide.shape[1]), F32)
     lower = lax.broadcasted_iota(jnp.int32, blank.shape, 1) // (wide.shape[1] // 4) % 2 == 1
 
@@ -121,13 +110,9 @@
     for part in range(0, parts, 2):
         outer = jnp.where(lower, pair_row(part - 2), pair_row(part + 3))
         rows = [pair_row(part + i) for i in range(-1, 3)] + [outer]
-        blocks[part // 2] = jnp.concatenate(rows, axis=0).astype(BF)
-        for i in (part, part + 1):
-            results.append(pltpu.make_async_copy(blocks.at[part // 2], send_hbm.at[i], send_sems.at[i]))
-            results[-1].start()
-
-    for result in results:
-        result.wait()
+        block = jnp.concatenate(rows, axis=0).astype(BF)
+        send_ref[part] = block
+        send_ref[part + 1] = block
 
 
 def build_patch_weights(conv_ref, patch_w):
@@ -499,7 +484,7 @@
     modulated, gain, send = pl.pallas_call(
         functools.partial(head_kernel, parts),
         in_specs=[SMEM] + [HBM] * 3,
-        out_specs=[HBM, VMEM, HBM],
+        out_specs=[VMEM] * 3,
         out_shape=[
             jax.ShapeDtypeStruct((tokens, depth), BF),
             jax.ShapeDtypeStruct((1, depth), F32),
@@ -509,11 +494,7 @@
             pltpu.VMEM((tokens, depth), BF),
             pltpu.VMEM(mod_table.shape, BF),
             pltpu.VMEM((features, depth), BF),
-            pltpu.VMEM((tokens, depth), BF),
-            pltpu.VMEM((parts // 2, 5 * n, 2 * features), BF),
-            pltpu.SemaphoreType.DMA((2 + LT,)),
-            pltpu.SemaphoreType.DMA((LT,)),
-            pltpu.SemaphoreType.DMA((parts,)),
+            pltpu.SemaphoreType.DMA((3,)),
         ],
         compiler_params=params(56),
         name="head",
@@ -594,6 +575,7 @@
         compiler_params=params(8),
         name="hidden_grad",
     )(token_grad, head_rows, gain)
+    hidden_grad, from_far = lax.optimization_barrier((hidden_grad, from_far))
     head_grad = half_sum(head_term) + half_sum(from_far)
     return (reward, head_grad.T, hidden_grad)
 

time: 63.3 us -> 62.4 us (0.986)
  Pallas kernels: 16.5 us -> 15.7 us
    pallas_call x1, Pallas kernels: 3.07 us -> 2.32 us  [body(): pl.pallas_call(functools.partial(head_kernel, parts), in_specs=[SMEM] + [...]
  transfers between devices with their start and end apart: 7 -> 7, of which waited for: 3 -> 3; matrix products, arithmetic and copies ran while one was open for 1% -> 1% of each run, Pallas kernels for 12% -> 11%
where the time goes in v4:
time: 62.4 us; the launch traced here: 62.1 us
  blocking collectives  20.3 us (33%)
  Pallas kernels  15.7 us (25%)
  waiting for transfers between devices  14 us (22%)
  starting transfers between devices  9.46 us (15%)
  between operations  1.5 us (2%)
  other arithmetic  0.84 us (1%)
    all_to_all x1, blocking collectives, body(): contributions = lax.all_to_all(contribution, 'mp', 0, 0, tiled=True)  10.2 us
    all_to_all x1, blocking collectives, body(): all_sums = lax.all_to_all(sums, 'mp', 0, 0, tiled=True)  10.1 us
    all_to_all x1, waiting for transfers between devices, body(): recv = lax.all_to_all(send, 'mp', 0, 0, tiled=True)  10 us
    all_to_all x1, starting transfers between devices, body(): recv = lax.all_to_all(send, 'mp', 0, 0, tiled=True)  5.84 us
    pallas_call x1, Pallas kernels, body(): pl.pallas_call(functools.partial(backward_kernel, parts, cells), in_specs...  4.67 us
    ppermute x6, waiting for transfers between devices, exchange(): return lax.ppermute(block, axis, [(i, i ^ flip) for i in range(count)])  4.02 us
    ppermute x6, starting transfers between devices, exchange(): return lax.ppermute(block, axis, [(i, i ^ flip) for i in range(count)])  3.63 us
    pallas_call x1, Pallas kernels, body(): pl.pallas_call(functools.partial(near_kernel, parts, blocks), in_specs=[S...  3.21 us
  transfers between devices with their start and end apart: 7, of which 3 were waited for; matrix products, arithmetic and copies ran while one was open for 1% of the time, Pallas kernels for 11%

profile of v4, /device:TPU:0, one launch (start us, length us, event | category | flops | bytes accessed | tf_op | source)
XLA Modules:
  0.0 62.1 jit_solution(16026552648085080086)
XLA Ops:
  0.6 0.0 copy-start.7
  0.6 2.2 %pack.1.refs_0_ = bf16[9,96,384]{2,1,0:T(8,128)(2,1)} custom-call(bf16[27,96,384]{2,1,0:T(8,128)(2,1)} %bitcast.9), custom_call_target="tpu_custom_call" | custom-call | tf_op jit(solution)/shard_map/pack/pallas_call | solution.py:469
  2.9 0.0 copy-start.1
  2.9 0.0 copy-start.4
  2.9 3.0 %collective-permute-start = (bf16[9,96,384]{2,1,0:T(8,128)(2,1)}, bf16[9,96,384]{2,1,0:T(8,128)(2,1)S(1)}, u32[]{:S(2)}, u32[]{:S(2)}) collective-permute-start(bf16[9,96,384]{2,1,0:T(8,128)(2,1)} %pack.1.refs_0_), channel_id=1, source_target_pairs={{0,16},{8,24},{16,0},{24,8},{1,17},{9,25},{17,1},{25,9},{2,18},{10... | collective-permute-start | bytes 1990664 | tf_op jit(solution)/shard_map/ppermute | solution.py:405
  6.6 2.3 %head.1 = (bf16[512,640]{1,0:T(8,128)(2,1)}, f32[1,640]{1,0:T(1,128)}, bf16[8,160,128]{2,1,0:T(8,128)(2,1)}) custom-call(s32[1]{0:T(128)S(6)} %copy.12.step_ref, bf16[512,640]{1,0:T(8,128)(2,1)} %hidden_hbm.1, bf16[50,2,640]{2,1,0:T(2,128)(2,1)} %mod_hbm.1, bf16[64,640]{1,0:T(8,128)(2,1)} %bitcast.7), custom_call_target="tpu_custom_call" | custom-call | tf_op jit(solution)/shard_map/head/pallas_call | solution.py:484
  8.9 5.8 %all-to-all-start = ((bf16[8,160,128]{2,1,0:T(8,128)(2,1)}), bf16[8,160,128]{2,1,0:T(8,128)(2,1)S(1)}, u32[]{:S(2)}, u32[]{:S(2)}) async-start(bf16[8,160,128]{2,1,0:T(8,128)(2,1)} %get-tuple-element.24), calls=%async_computation | async-start | bytes 655360 | tf_op jit(solution)/shard_map/all_to_all | solution.py:503
  14.7 0.0 collective-permute-start.1
  14.7 10.0 %all-to-all-done.recv_ref = bf16[8,160,128]{2,1,0:T(8,128)(2,1)S(1)} async-done(((bf16[8,160,128]{2,1,0:T(8,128)(2,1)}), bf16[8,160,128]{2,1,0:T(8,128)(2,1)S(1)}, u32[]{:S(2)}, u32[]{:S(2)}) %all-to-all-start) | async-done | bytes 327712 | tf_op jit(solution)/shard_map/all_to_all | solution.py:503
  24.8 0.0 collective-permute-done.refs_0_
  24.8 0.0 collective-permute-start.2
  24.8 0.0 copy-done.7
  24.9 0.1 broadcast_select_fusion.4
  25.0 0.2 concatenate.3.conv_ref
  25.2 0.0 collective-permute-done.1.refs_1_
  25.2 0.0 copy-done.1
  25.3 0.0 copy-done.4
  25.3 3.2 %near.1 = (f32[768,256]{1,0:T(8,128)S(1)}, bf16[2,8,64,768]{3,2,1,0:T(8,128)(2,1)S(1)}, f32[512,512]{1,0:T(8,128)S(1)}, bf16[9,192,384]{2,1,0:T(8,128)(2,1)S(1)}, bf16[2,256,2048]{2,1,0:T(8,128)(2,1)S(1)}) custom-call(s32[1]{0:T(128)} %bitcast.info_ref, bf16[8,160,128]{2,1,0:T(8,128)(2,1)S(1)} %all-to-all-done.recv_ref, ...), custom_call_target="tpu_custom_call" | custom-call | flops 4000000000 | bytes 10000000 | tf_op jit(solution)/shard_map/near/pallas_call | solution.py:514
  28.5 0.0 copy-start
  28.5 0.0 copy-start.5
  28.5 0.0 collective-permute-done.2.refs_1_
  28.5 1.8 %far.1 = (f32[8,8,128]{2,1,0:T(8,128)S(1)}, bf16[2,6,64,256]{3,2,1,0:T(8,128)(2,1)S(1)}) custom-call(s32[1]{0:T(128)} %bitcast.info_ref, f32[768,256]{1,0:T(8,128)S(1)} %get-tuple-element.27.near_ref, bf16[2,8,64,768]{3,2,1,0:T(8,128)(2,1)S(1)} %get-tuple-element.28.views, bf16[9,96,384]{2,1,0:T(8,128)(2,1)S(1)} %collective-permute-done.refs_0_, ...), custom_call_target="tpu_custom_call" | custom-call | tf_op jit(solution)/shard_map/far/pallas_call | solution.py:530
  30.3 10.1 %all_to_all.15.sums_ref = f32[8,8,128]{2,1,0:T(8,128)S(1)} all-to-all(f32[8,8,128]{2,1,0:T(8,128)S(1)} %get-tuple-element.30), channel_id=1, replica_groups=mesh['dp'=4,'mp'=8] {'mp'}, dimensions={0} | all-to-all | bytes 65536 | tf_op jit(solution)/shard_map/all_to_all | solution.py:542
  40.4 0.0 copy-done
  40.4 0.0 copy-done.5
  40.4 0.0 copy-start.2
  40.4 0.0 copy-start.3
  40.4 0.0 copy-start.6
  40.4 4.7 %backward.1 = (f32[1]{0:T(128)}, bf16[8,96,128]{2,1,0:T(8,128)(2,1)S(1)}) custom-call(s32[1]{0:T(128)} %bitcast.info_ref, f32[8,8,128]{2,1,0:T(8,128)S(1)} %all_to_all.15.sums_ref, bf16[384,1024]{1,0:T(8,128)(2,1)S(1)} %copy-done, f32[1,1024]{1,0:T(1,128)S(1)} %copy-done.5, bf16[2,6,64,256]{3,2,1,0:T(8,128)(2,1)S(1)} %get-tuple-element.31.second_ref, ...), custom_call_target="tpu_custom_call" | custom-call | tf_op jit(solution)/shard_map/backward/pallas_call | solution.py:544
  45.1 10.2 %all_to_all.16.recv_ref = bf16[8,96,128]{2,1,0:T(8,128)(2,1)S(1)} all-to-all(bf16[8,96,128]{2,1,0:T(8,128)(2,1)S(1)} %get-tuple-element.36), channel_id=1, replica_groups=mesh['dp'=4,'mp'=8] {'mp'}, dimensions={0} | all-to-all | bytes 393216 | tf_op jit(solution)/shard_map/all_to_all | solution.py:556
  55.3 0.0 copy-done.2
  55.3 0.3 token_.1
  55.6 0.6 collective-permute-start.4
  56.2 0.0 collective-permute-start.3
  56.2 0.0 copy-done.3
  56.2 0.0 copy-done.6
  56.2 1.1 %hidden_grad.1 = bf16[512,640]{1,0:T(8,128)(2,1)} custom-call(bf16[512,64]{1,0:T(8,128)(2,1)S(1)} %get-tuple-element.39.tokens_ref, bf16[64,640]{1,0:T(8,128)(2,1)S(1)} %bitcast.8, f32[1,640]{1,0:T(1,128)S(1)} %copy-done.6), custom_call_target="tpu_custom_call" | custom-call | tf_op jit(solution)/shard_map/hidden_grad/pallas_call | solution.py:570
  57.4 2.7 %collective-permute-done.4 = bf16[64,640]{1,0:T(8,128)(2,1)S(1)} collective-permute-done((bf16[64,640]{1,0:T(8,128)(2,1)S(1)}, bf16[64,640]{1,0:T(8,128)(2,1)S(1)}, u32[]{:S(2)}, u32[]{:S(2)}) %collective-permute-start.4) | collective-permute-done | bytes 81952 | tf_op jit(solution)/shard_map/ppermute | solution.py:405
  60.1 0.0 collective-permute-start.5
  60.1 0.0 collective-permute-done.3
  60.1 1.3 %collective-permute-done.5 = bf16[64,640]{1,0:T(8,128)(2,1)S(1)} collective-permute-done((bf16[64,640]{1,0:T(8,128)(2,1)S(1)}, bf16[64,640]{1,0:T(8,128)(2,1)S(1)}, u32[]{:S(2)}, u32[]{:S(2)}) %collective-permute-start.5) | collective-permute-done | bytes 81952 | tf_op jit(solution)/shard_map/ppermute | solution.py:405
  61.4 0.7 %add_bitcast_fusion = f32[640,64]{0,1:T(8,128)} fusion(bf16[64,640]{1,0:T(8,128)(2,1)S(1)} %collective-permute-done.5, bf16[64,640]{1,0:T(8,128)(2,1)S(1)} %collective-permute-done.4, bf16[64,640]{1,0:T(8,128)(2,1)S(1)} %collective-permute-done.3, bf16[64,640]{1,0:T(8,128)(2,1)S(1)} %get-tuple-element.38), kind=kLoop, calls=%fused_computation.1 | loop fusion | flops 286720 | bytes 491520 | tf_op jit(solution)/shard_map/transpose | solution.py:580
  (2 shorter events, 0.0 us)
Async XLA Ops:
  0.6 24.1 %copy-start.7 = (bf16[16,27,384]{2,0,1:T(8,128)(2,1)S(1)}, bf16[16,27,384]{2,0,1:T(8,128)(2,1)}, u32[]{:S(2)}) copy-start(bf16[16,27,384]{2,0,1:T(8,128)(2,1)} %param.13) | copy-start | bytes 995332
  2.9 22.4 %copy-start.1 = (bf16[9,96,384]{2,1,0:T(8,128)(2,1)S(1)}, bf16[9,96,384]{2,1,0:T(8,128)(2,1)}, u32[]{:S(2)}) copy-start(bf16[9,96,384]{2,1,0:T(8,128)(2,1)} %pack.1.refs_0_) | copy-start | bytes 1990660
  2.9 22.4 %copy-start.4 = (bf16[576,256]{1,0:T(8,128)(2,1)S(1)}, bf16[576,256]{1,0:T(8,128)(2,1)}, u32[]{:S(2)}) copy-start(bf16[576,256]{1,0:T(8,128)(2,1)} %constant.56.clone.pick_ref) | copy-start | bytes 884740
  2.9 21.9 %collective-permute-start = (bf16[9,96,384]{2,1,0:T(8,128)(2,1)}, bf16[9,96,384]{2,1,0:T(8,128)(2,1)S(1)}, u32[]{:S(2)}, u32[]{:S(2)}) collective-permute-start(bf16[9,96,384]{2,1,0:T(8,128)(2,1)} %pack.1.refs_0_), channel_id=1, source_target_pairs={{0,16},{8,24},{16,0},{24,8},{1,17},{9,25},{17,1},{25,9},{2,18},{10... | collective-permute-start | bytes 1990664 | tf_op jit(solution)/shard_map/ppermute | solution.py:405
  8.9 15.9 %all-to-all-start = ((bf16[8,160,128]{2,1,0:T(8,128)(2,1)}), bf16[8,160,128]{2,1,0:T(8,128)(2,1)S(1)}, u32[]{:S(2)}, u32[]{:S(2)}) async-start(bf16[8,160,128]{2,1,0:T(8,128)(2,1)} %get-tuple-element.24), calls=%async_computation | async-start | bytes 655360 | tf_op jit(solution)/shard_map/all_to_all | solution.py:503
  14.7 10.5 %collective-permute-start.1 = (bf16[9,96,384]{2,1,0:T(8,128)(2,1)}, bf16[9,96,384]{2,1,0:T(8,128)(2,1)}, u32[]{:S(2)}, u32[]{:S(2)}) collective-permute-start(bf16[9,96,384]{2,1,0:T(8,128)(2,1)} %pack.1.refs_0_), channel_id=1, source_target_pairs={{0,8},{8,0},{16,24},{24,16},{1,9},{9,1},{17,25},{25,17},{2,10},{10... | collective-permute-start | bytes 1990664 | tf_op jit(solution)/shard_map/ppermute | solution.py:405
  24.8 3.7 %collective-permute-start.2 = (bf16[9,96,384]{2,1,0:T(8,128)(2,1)S(1)}, bf16[9,96,384]{2,1,0:T(8,128)(2,1)S(1)}, u32[]{:S(2)}, u32[]{:S(2)}) collective-permute-start(bf16[9,96,384]{2,1,0:T(8,128)(2,1)S(1)} %collective-permute-done.refs_0_), channel_id=1, source_target_pairs={{0,8},{8,0},{16,24},{24,16},{1,9},{9,1},{17,25},{25,17},{2,10},{10... | collective-permute-start | bytes 1990664 | tf_op jit(solution)/shard_map/ppermute | solution.py:405
  28.5 11.9 %copy-start = (bf16[384,1024]{1,0:T(8,128)(2,1)S(1)}, bf16[384,1024]{1,0:T(8,128)(2,1)}, u32[]{:S(2)}) copy-start(bf16[384,1024]{1,0:T(8,128)(2,1)} %patch_ref.1) | copy-start | bytes 2359300
  28.5 11.9 %copy-start.5 = (f32[1,1024]{1,0:T(1,128)S(1)}, f32[1,1024]{1,0:T(1,128)}, u32[]{:S(2)}) copy-start(f32[1,1024]{1,0:T(1,128)} %text_ref.1) | copy-start | bytes 12292
  40.4 14.9 %copy-start.2 = (bf16[512,640]{1,0:T(8,128)(2,1)S(1)}, bf16[512,640]{1,0:T(8,128)(2,1)}, u32[]{:S(2)}) copy-start(bf16[512,640]{1,0:T(8,128)(2,1)} %get-tuple-element.37.modulated_ref) | copy-start | bytes 1966084
  40.4 15.8 %copy-start.3 = (bf16[640,64]{0,1:T(8,128)(2,1)S(1)}, bf16[640,64]{0,1:T(8,128)(2,1)}, u32[]{:S(2)}) copy-start(bf16[640,64]{0,1:T(8,128)(2,1)} %param.12) | copy-start | bytes 245764
  40.4 15.8 %copy-start.6 = (f32[1,640]{1,0:T(1,128)S(1)}, f32[1,640]{1,0:T(1,128)}, u32[]{:S(2)}) copy-start(f32[1,640]{1,0:T(1,128)} %get-tuple-element.40.gain_ref) | copy-start | bytes 7684
  55.6 4.5 %collective-permute-start.4 = (bf16[64,640]{1,0:T(8,128)(2,1)S(1)}, bf16[64,640]{1,0:T(8,128)(2,1)S(1)}, u32[]{:S(2)}, u32[]{:S(2)}) collective-permute-start(bf16[64,640]{1,0:T(8,128)(2,1)S(1)} %get-tuple-element.38), channel_id=1, source_target_pairs={{0,16},{8,24},{16,0},{24,8},{1,17},{9,25},{17,1},{25,9},{2,18},{10... | collective-permute-start | bytes 245768 | tf_op jit(solution)/shard_map/ppermute | solution.py:405
  56.2 3.9 %collective-permute-start.3 = (bf16[64,640]{1,0:T(8,128)(2,1)S(1)}, bf16[64,640]{1,0:T(8,128)(2,1)S(1)}, u32[]{:S(2)}, u32[]{:S(2)}) collective-permute-start(bf16[64,640]{1,0:T(8,128)(2,1)S(1)} %get-tuple-element.38), channel_id=1, source_target_pairs={{0,8},{8,0},{16,24},{24,16},{1,9},{9,1},{17,25},{25,17},{2,10},{10... | collective-permute-start | bytes 245768 | tf_op jit(solution)/shard_map/ppermute | solution.py:405
  60.1 1.3 %collective-permute-start.5 = (bf16[64,640]{1,0:T(8,128)(2,1)S(1)}, bf16[64,640]{1,0:T(8,128)(2,1)S(1)}, u32[]{:S(2)}, u32[]{:S(2)}) collective-permute-start(bf16[64,640]{1,0:T(8,128)(2,1)S(1)} %collective-permute-done.4), channel_id=1, source_target_pairs={{0,8},{8,0},{16,24},{24,16},{1,9},{9,1},{17,25},{25,17},{2,10},{10... | collective-permute-start | bytes 245768 | tf_op jit(solution)/shard_map/ppermute | solution.py:405

commit v5 on v3

--- a/solution.py
+++ b/solution.py
@@ -23,7 +23,7 @@
 
 
 def sigmoid(value):
-    return 0.5 + 0.5 * jnp.tanh(0.5 * value)
+    return 1.0 / (1.0 + jnp.exp(-value))
 
 
 def dot(left, right):
@@ -48,40 +48,9 @@
     return pick.reshape(36 * channels, 16 * channels).astype(BF)
 
 
-def pack_kernel(taps_hbm, packed_hbm, packed, thirds, in_sems, out_sems):
-    first = taps_hbm.shape[0] - 18
-    odd = lax.axis_index("mp") % 2
-    own = pl.ds(pl.multiple_of(odd * TILE, TILE), TILE)
-    copies, results = [], []
-    for chunk in range(3):
-        pairs = pl.ds(3 * chunk, 3)
-        here = []
-        for side in range(2):
-            source = taps_hbm.at[pl.ds(first + 9 * side + 3 * chunk, 3)]
-            here.append((source.at[:, :, own], packed.at[pairs, :, pl.ds(side * TILE, TILE)]))
-            here.append((source.at[:, :, pl.ds(2 * TILE, TILE)], thirds.at[side, pairs]))
-        copies.append([pltpu.make_async_copy(*ends, in_sems.at[chunk, i]) for i, ends in enumerate(here)])
-        results.append(pltpu.make_async_copy(packed.at[pairs], packed_hbm.at[pairs], out_sems.at[chunk]))
-    for chunk in range(3):
-        for copy in copies[chunk]:
-            copy.start()
-    lane = lax.broadcasted_iota(jnp.int32, thirds.shape[2:], 1)
-    for chunk in range(3):
-        for copy in copies[chunk]:
-            copy.wait()
-        for pair in range(3 * chunk, 3 * chunk + 3):
-            left, right = thirds[0, pair].astype(F32), thirds[1, pair].astype(F32)
-            left = jnp.where(odd == 0, left, pltpu.roll(left, TILE // 2, 1))
-            right = jnp.where(odd == 0, pltpu.roll(right, TILE // 2, 1), right)
-            packed[pair, :, 2 * TILE :] = jnp.where(lane < TILE // 2, left, right).astype(BF)
-        results[chunk].start()
-    for result in results:
-        result.wait()
-
-
 def head_kernel(
-    parts, step_ref, hidden_hbm, mod_hbm, head_hbm, modulated_hbm, gain_ref, send_hbm, hidden_ref, mod_ref, head_ref,
-    modulated, blocks, in_sems, out_sems, send_sems
+    parts, step_ref, hidden_hbm, mod_hbm, head_hbm, taps_hbm, modulated_hbm, gain_ref, send_hbm, packed_hbm, hidden_ref,
+    mod_ref, head_ref, modulated, blocks, packed, thirds, in_sems, out_sems, send_sems, tap_sems, packed_sems
 ):
     n = PAIR_COLS
     half = hidden_ref.shape[0] // LT
@@ -97,8 +66,25 @@
     results = [
         pltpu.make_async_copy(modulated.at[rows], modulated_hbm.at[rows], out_sems.at[t]) for t, rows in enumerate(frames)
     ]
+    first = taps_hbm.shape[0] - 18
+    odd = lax.axis_index("mp") % 2
+    own = pl.ds(pl.multiple_of(odd * TILE, TILE), TILE)
+    tap_copies, packed_results = [], []
+    for chunk in range(3):
+        pairs = pl.ds(3 * chunk, 3)
+        ends = []
+        for side in range(2):
+            source = taps_hbm.at[pl.ds(first + 9 * side + 3 * chunk, 3)]
+            ends.append((source.at[:, :, own], packed.at[pairs, :, pl.ds(side * TILE, TILE)]))
+            ends.append((source.at[:, :, pl.ds(2 * TILE, TILE)], thirds.at[side, pairs]))
+        tap_copies.append([pltpu.make_async_copy(*pair, tap_sems.at[chunk, i]) for i, pair in enumerate(ends)])
+        packed_results.append(pltpu.make_async_copy(packed.at[pairs], packed_hbm.at[pairs], packed_sems.at[chunk]))
     for copy in small + large:
         copy.start()
+    for chunk in tap_copies:
+        for copy in chunk:
+            copy.start()
+
     for copy in small:
         copy.wait()
     mod = mod_ref[step_ref[0]].astype(F32)
@@ -126,7 +112,17 @@
             results.append(pltpu.make_async_copy(blocks.at[part // 2], send_hbm.at[i], send_sems.at[i]))
             results[-1].start()
 
-    for result in results:
+    lane = lax.broadcasted_iota(jnp.int32, thirds.shape[2:], 1)
+    for chunk in range(3):
+        for copy in tap_copies[chunk]:
+            copy.wait()
+        for pair in range(3 * chunk, 3 * chunk + 3):
+            left, right = thirds[0, pair].astype(F32), thirds[1, pair].astype(F32)
+            left = jnp.where(odd == 0, left, pltpu.roll(left, TILE // 2, 1))
+            right = jnp.where(odd == 0, pltpu.roll(right, TILE // 2, 1), right)
+            packed[pair, :, 2 * TILE :] = jnp.where(lane < TILE // 2, left, right).astype(BF)
+        packed_results[chunk].start()
+    for result in results + packed_results:
         result.wait()
 
 
@@ -157,7 +153,7 @@
     for ref in refs:
         half = ref[pair, :, 2 * TILE :]
         lane = lax.broadcasted_iota(jnp.int32, half.shape, 1)
-        half = half * jnp.where((lane < TILE // 2) == (side == 0), 1.0, 0.0).astype(BF)
+        half = jnp.where((lane < TILE // 2) == (side == 0), half, jnp.zeros_like(half))
         blocks.append(jnp.concatenate([ref[pair, :, side * TILE : (side + 1) * TILE], half], axis=1))
     filled = sum(block.shape[0] for block in blocks)
     return jnp.concatenate(blocks + [jnp.zeros((DEEP - filled, 2 * TILE), BF)], axis=0)
@@ -441,15 +437,6 @@
     return [blocks[held] for held in sorted(blocks)], unit
 
 
-def half_sum(term):
-    total, flip = term.astype(F32), 1
-    while flip < lax.axis_size("dp") // 2:
-        other = exchange(term, "dp", flip)
-        total = total + other.astype(F32)
-        term, flip = total.astype(BF), 2 * flip
-    return total
-
-
 def local_channels(weight, unit):
     count = lax.axis_size("dp") // unit
     place = lax.axis_index("dp") // unit
@@ -481,29 +468,15 @@
     rows = conv_mid.shape[0]
     far = groups // 2
 
-    packed = pl.pallas_call(
-        pack_kernel,
-        in_specs=[HBM],
-        out_specs=HBM,
-        out_shape=jax.ShapeDtypeStruct((9, rows, width), BF),
-        scratch_shapes=[
-            pltpu.VMEM((9, rows, width), BF),
-            pltpu.VMEM((2, 9, rows, TILE), BF),
-            pltpu.SemaphoreType.DMA((3, 4)),
-            pltpu.SemaphoreType.DMA((3,)),
-        ],
-        compiler_params=params(56),
-        name="pack",
-    )(taps)
-    distant = exchange(packed, "dp", far)
-    modulated, gain, send = pl.pallas_call(
+    modulated, gain, send, packed = pl.pallas_call(
         functools.partial(head_kernel, parts),
-        in_specs=[SMEM] + [HBM] * 3,
-        out_specs=[HBM, VMEM, HBM],
+        in_specs=[SMEM] + [HBM] * 4,
+        out_specs=[HBM, VMEM, HBM, HBM],
         out_shape=[
             jax.ShapeDtypeStruct((tokens, depth), BF),
             jax.ShapeDtypeStruct((1, depth), F32),
             jax.ShapeDtypeStruct((parts, 5 * n, 2 * features), BF),
+            jax.ShapeDtypeStruct((9, rows, width), BF),
         ],
         scratch_shapes=[
             pltpu.VMEM((tokens, depth), BF),
@@ -511,18 +484,21 @@
             pltpu.VMEM((features, depth), BF),
             pltpu.VMEM((tokens, depth), BF),
             pltpu.VMEM((parts // 2, 5 * n, 2 * features), BF),
+            pltpu.VMEM((9, rows, width), BF),
+            pltpu.VMEM((2, 9, rows, TILE), BF),
             pltpu.SemaphoreType.DMA((2 + LT,)),
             pltpu.SemaphoreType.DMA((LT,)),
             pltpu.SemaphoreType.DMA((parts,)),
+            pltpu.SemaphoreType.DMA((3, 4)),
+            pltpu.SemaphoreType.DMA((3,)),
         ],
         compiler_params=params(56),
         name="head",
-    )(timestep, hidden, mod_table, head_rows)
+    )(timestep, hidden, mod_table, head_rows, taps)
+    distant = exchange(packed, "dp", far)
     send, conv_in = lax.optimization_barrier((send, conv_in))
     recv = lax.all_to_all(send, "mp", 0, 0, tiled=True)
     near_blocks, unit = spread(packed)
-    recv, distant = lax.optimization_barrier((recv, distant))
-    far_blocks, _ = spread(distant)
     blocks = len(near_blocks)
     info = jnp.reshape(mp_index, (1,)).astype(jnp.int32)
     taps_in = local_channels(jnp.transpose(conv_in[:, 9:], (1, 0, 2)), unit)
@@ -542,10 +518,11 @@
             jax.ShapeDtypeStruct((2, 16 * channels, 8 * DEEP), BF),
         ],
         scratch_shapes=[pltpu.VMEM(views_shape, BF), pltpu.SemaphoreType.DMA((blocks,))],
-        cost_estimate=pl.CostEstimate(flops=4 * 10**9, bytes_accessed=10**7, transcendentals=10**6),
         compiler_params=params(20),
         name="near",
     )(info, recv, taps_in, pick, *near_blocks)
+    near_acc, distant = lax.optimization_barrier((near_acc, distant))
+    far_blocks, _ = spread(distant)
     sums, second_slope = pl.pallas_call(
         functools.partial(far_kernel, parts),
         in_specs=[SMEM] + [VMEM] * (2 + blocks),
@@ -585,7 +562,12 @@
         compiler_params=params(8),
         name="token",
     )(contributions, modulated)
-    from_far = exchange(head_term, "dp", far)
+    flip = 1
+    while flip < far:
+        other = exchange(head_term, "dp", flip)
+        head_term = (head_term.astype(F32) + other.astype(F32)).astype(BF)
+        flip *= 2
+    head_other = exchange(head_term, "dp", far)
     hidden_grad = pl.pallas_call(
         hidden_kernel,
         in_specs=[VMEM] * 3,
@@ -594,7 +576,7 @@
         compiler_params=params(8),
         name="hidden_grad",
     )(token_grad, head_rows, gain)
-    head_grad = half_sum(head_term) + half_sum(from_far)
+    head_grad = head_term.astype(F32) + head_other.astype(F32)
     return (reward, head_grad.T, hidden_grad)
 
 

time: 63.3 us -> 64.3 us (1.016)
  waiting for transfers between devices: 14.1 us -> 16.4 us
  Pallas kernels: 16.5 us -> 15 us
    pallas_call x1 -> x0, Pallas kernels: 2.24 us -> none  [body(): pl.pallas_call(pack_kernel, in_specs=[HBM], out_specs=HBM, out_shape=jax....]
    ppermute x6 -> x5, waiting for transfers between devices: 4.04 us -> 6.18 us  [exchange(): return lax.ppermute(block, axis, [(i, i ^ flip) for i in range(count)])]
    pallas_call x1, Pallas kernels: 3.07 us -> 3.88 us  [body(): pl.pallas_call(functools.partial(head_kernel, parts), in_specs=[SMEM] + [...]
    ppermute x6 -> x5, starting transfers between devices: 3.6 us -> 3.82 us  [exchange(): return lax.ppermute(block, axis, [(i, i ^ flip) for i in range(count)])]
  transfers between devices with their start and end apart: 7 -> 6, of which waited for: 3 -> 4; matrix products, arithmetic and copies ran while one was open for 1% -> 1% of each run, Pallas kernels for 12% -> 7%
where the time goes in v5:
time: 64.3 us; the launch traced here: 64 us
  blocking collectives  20.3 us (32%)
  waiting for transfers between devices  16.4 us (26%)
  Pallas kernels  15 us (23%)
  starting transfers between devices  9.65 us (15%)
  between operations  1.49 us (2%)
  other arithmetic  0.84 us (1%)
    all_to_all x1, waiting for transfers between devices, body(): recv = lax.all_to_all(send, 'mp', 0, 0, tiled=True)  10.2 us
    all_to_all x1, blocking collectives, body(): contributions = lax.all_to_all(contribution, 'mp', 0, 0, tiled=True)  10.2 us
    all_to_all x1, blocking collectives, body(): all_sums = lax.all_to_all(sums, 'mp', 0, 0, tiled=True)  10.1 us
    ppermute x5, waiting for transfers between devices, exchange(): return lax.ppermute(block, axis, [(i, i ^ flip) for i in range(count)])  6.18 us
    all_to_all x1, starting transfers between devices, body(): recv = lax.all_to_all(send, 'mp', 0, 0, tiled=True)  5.83 us
    pallas_call x1, Pallas kernels, body(): pl.pallas_call(functools.partial(backward_kernel, parts, cells), in_specs...  4.68 us
    pallas_call x1, Pallas kernels, body(): pl.pallas_call(functools.partial(head_kernel, parts), in_specs=[SMEM] + [...  3.88 us
    ppermute x5, starting transfers between devices, exchange(): return lax.ppermute(block, axis, [(i, i ^ flip) for i in range(count)])  3.82 us
  transfers between devices with their start and end apart: 6, of which 4 were waited for; matrix products, arithmetic and copies ran while one was open for 1% of the time, Pallas kernels for 7%

profile of v5, /device:TPU:0, one launch (start us, length us, event | category | flops | bytes accessed | tf_op | source)
XLA Modules:
  0.0 64.0 jit_solution(9881020881335762740)
XLA Ops:
  0.6 0.0 copy-start.7
  1.3 3.9 %head.1 = (bf16[512,640]{1,0:T(8,128)(2,1)}, f32[1,640]{1,0:T(1,128)}, bf16[8,160,128]{2,1,0:T(8,128)(2,1)}, bf16[9,96,384]{2,1,0:T(8,128)(2,1)}) custom-call(s32[1]{0:T(128)S(6)} %copy.12.step_ref, bf16[512,640]{1,0:T(8,128)(2,1)} %hidden_hbm.1, bf16[50,2,640]{2,1,0:T(2,128)(2,1)} %mod_hbm.1, bf16[64,640]{1,0:T(8,128)(2,1)} %bitcast.7, ...), custom_call_target="tpu_custom_call" | custom-call | tf_op jit(solution)/shard_map/head/pallas_call | solution.py:471
  5.2 0.0 copy-start
  5.2 0.0 copy-start.2
  5.2 0.5 collective-permute-start
  5.8 2.6 %collective-permute-start.1 = (bf16[9,96,384]{2,1,0:T(8,128)(2,1)}, bf16[9,96,384]{2,1,0:T(8,128)(2,1)S(1)}, u32[]{:S(2)}, u32[]{:S(2)}) collective-permute-start(bf16[9,96,384]{2,1,0:T(8,128)(2,1)} %get-tuple-element.25.refs_0_), channel_id=1, source_target_pairs={{0,16},{8,24},{16,0},{24,8},{1,17},{9,25},{17,1},{25,9},{2,18},{10... | collective-permute-start | bytes 1990664 | tf_op jit(solution)/shard_map/ppermute | solution.py:416
  8.3 5.8 %all-to-all-start = ((bf16[8,160,128]{2,1,0:T(8,128)(2,1)}), bf16[8,160,128]{2,1,0:T(8,128)(2,1)S(1)}, u32[]{:S(2)}, u32[]{:S(2)}) async-start(bf16[8,160,128]{2,1,0:T(8,128)(2,1)} %get-tuple-element.23), calls=%async_computation | async-start | bytes 655360 | tf_op jit(solution)/shard_map/all_to_all | solution.py:500
  14.2 0.0 copy-done.7
  14.2 0.1 broadcast_select_fusion.4
  14.4 0.2 concatenate.3.conv_ref
  14.6 10.2 %all-to-all-done.recv_ref = bf16[8,160,128]{2,1,0:T(8,128)(2,1)S(1)} async-done(((bf16[8,160,128]{2,1,0:T(8,128)(2,1)}), bf16[8,160,128]{2,1,0:T(8,128)(2,1)S(1)}, u32[]{:S(2)}, u32[]{:S(2)}) %all-to-all-start) | async-done | bytes 327712 | tf_op jit(solution)/shard_map/all_to_all | solution.py:500
  24.8 0.0 collective-permute-done.refs_1_
  24.8 0.0 copy-done
  24.8 0.0 copy-done.2
  24.8 3.3 %near.1 = (f32[768,256]{1,0:T(8,128)S(1)}, bf16[2,8,64,768]{3,2,1,0:T(8,128)(2,1)S(1)}, f32[512,512]{1,0:T(8,128)S(1)}, bf16[9,192,384]{2,1,0:T(8,128)(2,1)S(1)}, bf16[2,256,2048]{2,1,0:T(8,128)(2,1)S(1)}) custom-call(s32[1]{0:T(128)} %bitcast.info_ref, bf16[8,160,128]{2,1,0:T(8,128)(2,1)S(1)} %all-to-all-done.recv_ref, ...), custom_call_target="tpu_custom_call" | custom-call | tf_op jit(solution)/shard_map/near/pallas_call | solution.py:509
  28.0 0.0 copy-start.1
  28.1 0.0 copy-start.5
  28.1 0.0 collective-permute-done.1.refs_0_
  28.1 0.1 collective-permute-start.2
  28.2 2.1 %collective-permute-done.2.refs_1_ = bf16[9,96,384]{2,1,0:T(8,128)(2,1)S(1)} collective-permute-done((bf16[9,96,384]{2,1,0:T(8,128)(2,1)S(1)}, bf16[9,96,384]{2,1,0:T(8,128)(2,1)S(1)}, u32[]{:S(2)}, u32[]{:S(2)}) %collective-permute-start.2) | collective-permute-done | bytes 663584 | tf_op jit(solution)/shard_map/ppermute | solution.py:416
  30.3 1.8 %far.1 = (f32[8,8,128]{2,1,0:T(8,128)S(1)}, bf16[2,6,64,256]{3,2,1,0:T(8,128)(2,1)S(1)}) custom-call(s32[1]{0:T(128)} %bitcast.info_ref, f32[768,256]{1,0:T(8,128)S(1)} %get-tuple-element.27.near_ref, bf16[2,8,64,768]{3,2,1,0:T(8,128)(2,1)S(1)} %get-tuple-element.28.views, bf16[9,96,384]{2,1,0:T(8,128)(2,1)S(1)} %collective-permute-done.1.refs_0_, ...), custom_call_target="tpu_custom_call" | custom-call | tf_op jit(solution)/shard_map/far/pallas_call | solution.py:526
  32.0 10.1 %all_to_all.15.sums_ref = f32[8,8,128]{2,1,0:T(8,128)S(1)} all-to-all(f32[8,8,128]{2,1,0:T(8,128)S(1)} %get-tuple-element.30), channel_id=1, replica_groups=mesh['dp'=4,'mp'=8] {'mp'}, dimensions={0} | all-to-all | bytes 65536 | tf_op jit(solution)/shard_map/all_to_all | solution.py:538
  42.1 0.0 copy-done.1
  42.1 0.0 copy-done.5
  42.2 0.0 copy-start.3
  42.2 0.0 copy-start.4
  42.2 0.0 copy-start.6
  42.2 4.7 %backward.1 = (f32[1]{0:T(128)}, bf16[8,96,128]{2,1,0:T(8,128)(2,1)S(1)}) custom-call(s32[1]{0:T(128)} %bitcast.info_ref, f32[8,8,128]{2,1,0:T(8,128)S(1)} %all_to_all.15.sums_ref, bf16[384,1024]{1,0:T(8,128)(2,1)S(1)} %copy-done.1, f32[1,1024]{1,0:T(1,128)S(1)} %copy-done.5, bf16[2,6,64,256]{3,2,1,0:T(8,128)(2,1)S(1)} %get-tuple-element.31.second_ref, ...), custom_call_target="tpu_custom_call" | custom-call | tf_op jit(solution)/shard_map/backward/pallas_call | solution.py:540
  46.9 10.2 %all_to_all.16.recv_ref = bf16[8,96,128]{2,1,0:T(8,128)(2,1)S(1)} all-to-all(bf16[8,96,128]{2,1,0:T(8,128)(2,1)S(1)} %get-tuple-element.36), channel_id=1, replica_groups=mesh['dp'=4,'mp'=8] {'mp'}, dimensions={0} | all-to-all | bytes 393216 | tf_op jit(solution)/shard_map/all_to_all | solution.py:552
  57.0 0.0 copy-done.3
  57.0 0.3 token_.1
  57.4 0.1 collective-permute-start.3
  57.5 1.3 %collective-permute-done.3 = bf16[64,640]{1,0:T(8,128)(2,1)S(1)} collective-permute-done((bf16[64,640]{1,0:T(8,128)(2,1)S(1)}, bf16[64,640]{1,0:T(8,128)(2,1)S(1)}, u32[]{:S(2)}, u32[]{:S(2)}) %collective-permute-start.3) | collective-permute-done | bytes 81952 | tf_op jit(solution)/shard_map/ppermute | solution.py:416
  58.7 0.6 collective-permute-start.4
  59.3 0.0 copy-done.4
  59.3 0.0 copy-done.6
  59.3 1.2 %hidden_grad.1 = bf16[512,640]{1,0:T(8,128)(2,1)} custom-call(bf16[512,64]{1,0:T(8,128)(2,1)S(1)} %get-tuple-element.39.tokens_ref, bf16[64,640]{1,0:T(8,128)(2,1)S(1)} %bitcast.8, f32[1,640]{1,0:T(1,128)S(1)} %copy-done.6), custom_call_target="tpu_custom_call" | custom-call | tf_op jit(solution)/shard_map/hidden_grad/pallas_call | solution.py:571
  60.5 2.8 %collective-permute-done.4 = bf16[64,640]{1,0:T(8,128)(2,1)S(1)} collective-permute-done((bf16[64,640]{1,0:T(8,128)(2,1)S(1)}, bf16[64,640]{1,0:T(8,128)(2,1)S(1)}, u32[]{:S(2)}, u32[]{:S(2)}) %collective-permute-start.4) | collective-permute-done | bytes 81952 | tf_op jit(solution)/shard_map/ppermute | solution.py:416
  63.3 0.7 %add_bitcast_fusion = f32[640,64]{0,1:T(8,128)} fusion(bf16[64,640]{1,0:T(8,128)(2,1)S(1)} %collective-permute-done.4, bf16[64,640]{1,0:T(8,128)(2,1)S(1)} %add_convert_fusion), kind=kLoop, calls=%fused_computation.1 | loop fusion | flops 122880 | bytes 327680 | tf_op jit(solution)/shard_map/transpose | solution.py:580
  (3 shorter events, 0.1 us)
Async XLA Ops:
  0.6 13.5 %copy-start.7 = (bf16[16,27,384]{2,0,1:T(8,128)(2,1)S(1)}, bf16[16,27,384]{2,0,1:T(8,128)(2,1)}, u32[]{:S(2)}) copy-start(bf16[16,27,384]{2,0,1:T(8,128)(2,1)} %param.13) | copy-start | bytes 995332
  5.2 19.6 %copy-start = (bf16[576,256]{1,0:T(8,128)(2,1)S(1)}, bf16[576,256]{1,0:T(8,128)(2,1)}, u32[]{:S(2)}) copy-start(bf16[576,256]{1,0:T(8,128)(2,1)} %constant.56.clone.pick_ref) | copy-start | bytes 884740
  5.2 19.5 %copy-start.2 = (bf16[9,96,384]{2,1,0:T(8,128)(2,1)S(1)}, bf16[9,96,384]{2,1,0:T(8,128)(2,1)}, u32[]{:S(2)}) copy-start(bf16[9,96,384]{2,1,0:T(8,128)(2,1)} %get-tuple-element.25.refs_0_) | copy-start | bytes 1990660
  5.2 19.5 %collective-permute-start = (bf16[9,96,384]{2,1,0:T(8,128)(2,1)}, bf16[9,96,384]{2,1,0:T(8,128)(2,1)S(1)}, u32[]{:S(2)}, u32[]{:S(2)}) collective-permute-start(bf16[9,96,384]{2,1,0:T(8,128)(2,1)} %get-tuple-element.25.refs_0_), channel_id=1, source_target_pairs={{0,8},{8,0},{16,24},{24,16},{1,9},{9,1},{17,25},{25,17},{2,10},{10... | collective-permute-start | bytes 1990664 | tf_op jit(solution)/shard_map/ppermute | solution.py:416
  5.8 22.3 %collective-permute-start.1 = (bf16[9,96,384]{2,1,0:T(8,128)(2,1)}, bf16[9,96,384]{2,1,0:T(8,128)(2,1)S(1)}, u32[]{:S(2)}, u32[]{:S(2)}) collective-permute-start(bf16[9,96,384]{2,1,0:T(8,128)(2,1)} %get-tuple-element.25.refs_0_), channel_id=1, source_target_pairs={{0,16},{8,24},{16,0},{24,8},{1,17},{9,25},{17,1},{25,9},{2,18},{10... | collective-permute-start | bytes 1990664 | tf_op jit(solution)/shard_map/ppermute | solution.py:416
  8.3 16.4 %all-to-all-start = ((bf16[8,160,128]{2,1,0:T(8,128)(2,1)}), bf16[8,160,128]{2,1,0:T(8,128)(2,1)S(1)}, u32[]{:S(2)}, u32[]{:S(2)}) async-start(bf16[8,160,128]{2,1,0:T(8,128)(2,1)} %get-tuple-element.23), calls=%async_computation | async-start | bytes 655360 | tf_op jit(solution)/shard_map/all_to_all | solution.py:500
  28.0 14.1 %copy-start.1 = (bf16[384,1024]{1,0:T(8,128)(2,1)S(1)}, bf16[384,1024]{1,0:T(8,128)(2,1)}, u32[]{:S(2)}) copy-start(bf16[384,1024]{1,0:T(8,128)(2,1)} %patch_ref.1) | copy-start | bytes 2359300
  28.1 14.1 %copy-start.5 = (f32[1,1024]{1,0:T(1,128)S(1)}, f32[1,1024]{1,0:T(1,128)}, u32[]{:S(2)}) copy-start(f32[1,1024]{1,0:T(1,128)} %text_ref.1) | copy-start | bytes 12292
  28.1 2.2 %collective-permute-start.2 = (bf16[9,96,384]{2,1,0:T(8,128)(2,1)S(1)}, bf16[9,96,384]{2,1,0:T(8,128)(2,1)S(1)}, u32[]{:S(2)}, u32[]{:S(2)}) collective-permute-start(bf16[9,96,384]{2,1,0:T(8,128)(2,1)S(1)} %collective-permute-done.1.refs_0_), channel_id=1, source_target_pairs={{0,8},{8,0},{16,24},{24,16},{1,9},{9,1},{17,25},{25,17},{2,10},{10... | collective-permute-start | bytes 1990664 | tf_op jit(solution)/shard_map/ppermute | solution.py:416
  42.2 14.9 %copy-start.3 = (bf16[512,640]{1,0:T(8,128)(2,1)S(1)}, bf16[512,640]{1,0:T(8,128)(2,1)}, u32[]{:S(2)}) copy-start(bf16[512,640]{1,0:T(8,128)(2,1)} %get-tuple-element.37.modulated_ref) | copy-start | bytes 1966084
  42.2 17.2 %copy-start.4 = (bf16[640,64]{0,1:T(8,128)(2,1)S(1)}, bf16[640,64]{0,1:T(8,128)(2,1)}, u32[]{:S(2)}) copy-start(bf16[640,64]{0,1:T(8,128)(2,1)} %param.12) | copy-start | bytes 245764
  42.2 17.2 %copy-start.6 = (f32[1,640]{1,0:T(1,128)S(1)}, f32[1,640]{1,0:T(1,128)}, u32[]{:S(2)}) copy-start(f32[1,640]{1,0:T(1,128)} %get-tuple-element.40.gain_ref) | copy-start | bytes 7684
  57.4 1.3 %collective-permute-start.3 = (bf16[64,640]{1,0:T(8,128)(2,1)S(1)}, bf16[64,640]{1,0:T(8,128)(2,1)S(1)}, u32[]{:S(2)}, u32[]{:S(2)}) collective-permute-start(bf16[64,640]{1,0:T(8,128)(2,1)S(1)} %get-tuple-element.38), channel_id=1, source_target_pairs={{0,8},{8,0},{16,24},{24,16},{1,9},{9,1},{17,25},{25,17},{2,10},{10... | collective-permute-start | bytes 245768 | tf_op jit(solution)/shard_map/ppermute | solution.py:416
  58.7 4.6 %collective-permute-start.4 = (bf16[64,640]{1,0:T(8,128)(2,1)S(1)}, bf16[64,640]{1,0:T(8,128)(2,1)S(1)}, u32[]{:S(2)}, u32[]{:S(2)}) collective-permute-start(bf16[64,640]{1,0:T(8,128)(2,1)S(1)} %add_convert_fusion), channel_id=1, source_target_pairs={{0,16},{8,24},{16,0},{24,8},{1,17},{9,25},{17,1},{25,9},{2,18},{10... | collective-permute-start | bytes 245768 | tf_op jit(solution)/shard_map/ppermute | solution.py:416

commit v6 on v4

--- a/solution.py
+++ b/solution.py
@@ -48,11 +48,11 @@
     return pick.reshape(36 * channels, 16 * channels).astype(BF)
 
 
-def pack_kernel(taps_hbm, packed_hbm, packed, thirds, in_sems, out_sems):
+def pack_kernel(taps_hbm, packed, thirds, in_sems):
     first = taps_hbm.shape[0] - 18
     odd = lax.axis_index("mp") % 2
     own = pl.ds(pl.multiple_of(odd * TILE, TILE), TILE)
-    copies, results = [], []
+    copies = []
     for chunk in range(3):
         pairs = pl.ds(3 * chunk, 3)
         here = []
@@ -61,7 +61,6 @@
             here.append((source.at[:, :, own], packed.at[pairs, :, pl.ds(side * TILE, TILE)]))
             here.append((source.at[:, :, pl.ds(2 * TILE, TILE)], thirds.at[side, pairs]))
         copies.append([pltpu.make_async_copy(*ends, in_sems.at[chunk, i]) for i, ends in enumerate(here)])
-        results.append(pltpu.make_async_copy(packed.at[pairs], packed_hbm.at[pairs], out_sems.at[chunk]))
     for chunk in range(3):
         for copy in copies[chunk]:
             copy.start()
@@ -74,9 +73,6 @@
             left = jnp.where(odd == 0, left, pltpu.roll(left, TILE // 2, 1))
             right = jnp.where(odd == 0, pltpu.roll(right, TILE // 2, 1), right)
             packed[pair, :, 2 * TILE :] = jnp.where(lane < TILE // 2, left, right).astype(BF)
-        results[chunk].start()
-    for result in results:
-        result.wait()
 
 
 def head_kernel(
@@ -469,15 +465,10 @@
     packed = pl.pallas_call(
         pack_kernel,
         in_specs=[HBM],
-        out_specs=HBM,
+        out_specs=VMEM,
         out_shape=jax.ShapeDtypeStruct((9, rows, width), BF),
-        scratch_shapes=[
-            pltpu.VMEM((9, rows, width), BF),
-            pltpu.VMEM((2, 9, rows, TILE), BF),
-            pltpu.SemaphoreType.DMA((3, 4)),
-            pltpu.SemaphoreType.DMA((3,)),
-        ],
-        compiler_params=params(56),
+        scratch_shapes=[pltpu.VMEM((2, 9, rows, TILE), BF), pltpu.SemaphoreType.DMA((3, 4))],
+        compiler_params=params(53),
         name="pack",
     )(taps)
     distant = exchange(packed, "dp", far)

time: 62.4 us -> 61.7 us (0.989)
  Pallas kernels: 15.7 us -> 15 us
    pallas_call x1, Pallas kernels: 2.24 us -> 1.52 us  [body(): pl.pallas_call(pack_kernel, in_specs=[HBM], out_specs=VMEM, out_shape=jax...]
where the time goes in v6:
time: 61.7 us; the launch traced here: 61.4 us
  blocking collectives  20.3 us (33%)
  Pallas kernels  15 us (24%)
  waiting for transfers between devices  14 us (23%)
  starting transfers between devices  9.47 us (15%)
  between operations  1.49 us (2%)
  other arithmetic  0.84 us (1%)
    all_to_all x1, blocking collectives, body(): contributions = lax.all_to_all(contribution, 'mp', 0, 0, tiled=True)  10.2 us
    all_to_all x1, blocking collectives, body(): all_sums = lax.all_to_all(sums, 'mp', 0, 0, tiled=True)  10.1 us
    all_to_all x1, waiting for transfers between devices, body(): recv = lax.all_to_all(send, 'mp', 0, 0, tiled=True)  10 us
    all_to_all x1, starting transfers between devices, body(): recv = lax.all_to_all(send, 'mp', 0, 0, tiled=True)  5.84 us
    pallas_call x1, Pallas kernels, body(): pl.pallas_call(functools.partial(backward_kernel, parts, cells), in_specs...  4.67 us
    ppermute x6, waiting for transfers between devices, exchange(): return lax.ppermute(block, axis, [(i, i ^ flip) for i in range(count)])  4.01 us
    ppermute x6, starting transfers between devices, exchange(): return lax.ppermute(block, axis, [(i, i ^ flip) for i in range(count)])  3.63 us
    pallas_call x1, Pallas kernels, body(): pl.pallas_call(functools.partial(near_kernel, parts, blocks), in_specs=[S...  3.2 us
  transfers between devices with their start and end apart: 7, of which 3 were waited for; matrix products, arithmetic and copies ran while one was open for 1% of the time, Pallas kernels for 11%

profile of v6, /device:TPU:0, one launch (start us, length us, event | category | flops | bytes accessed | tf_op | source)
XLA Modules:
  0.0 61.4 jit_solution(4059679496639572713)
XLA Ops:
  0.6 0.0 copy-start.6
  0.6 1.5 %pack.1.refs_0_ = bf16[9,96,384]{2,1,0:T(8,128)(2,1)S(1)} custom-call(bf16[27,96,384]{2,1,0:T(8,128)(2,1)} %bitcast.9), custom_call_target="tpu_custom_call" | custom-call | tf_op jit(solution)/shard_map/pack/pallas_call | solution.py:465
  2.2 0.0 copy-start.3
  2.2 3.0 %collective-permute-start = (bf16[9,96,384]{2,1,0:T(8,128)(2,1)S(1)}, bf16[9,96,384]{2,1,0:T(8,128)(2,1)S(1)}, u32[]{:S(2)}, u32[]{:S(2)}) collective-permute-start(bf16[9,96,384]{2,1,0:T(8,128)(2,1)S(1)} %pack.1.refs_0_), channel_id=1, source_target_pairs={{0,16},{8,24},{16,0},{24,8},{1,17},{9,25},{17,1},{25,9},{2,18},{10... | collective-permute-start | bytes 1990664 | tf_op jit(solution)/shard_map/ppermute | solution.py:401
  5.8 2.3 %head.1 = (bf16[512,640]{1,0:T(8,128)(2,1)}, f32[1,640]{1,0:T(1,128)}, bf16[8,160,128]{2,1,0:T(8,128)(2,1)}) custom-call(s32[1]{0:T(128)S(6)} %copy.12.step_ref, bf16[512,640]{1,0:T(8,128)(2,1)} %hidden_hbm.1, bf16[50,2,640]{2,1,0:T(2,128)(2,1)} %mod_hbm.1, bf16[64,640]{1,0:T(8,128)(2,1)} %bitcast.7), custom_call_target="tpu_custom_call" | custom-call | tf_op jit(solution)/shard_map/head/pallas_call | solution.py:475
  8.2 5.8 %all-to-all-start = ((bf16[8,160,128]{2,1,0:T(8,128)(2,1)}), bf16[8,160,128]{2,1,0:T(8,128)(2,1)S(1)}, u32[]{:S(2)}, u32[]{:S(2)}) async-start(bf16[8,160,128]{2,1,0:T(8,128)(2,1)} %get-tuple-element.24), calls=%async_computation | async-start | bytes 655360 | tf_op jit(solution)/shard_map/all_to_all | solution.py:494
  14.0 0.0 collective-permute-start.1
  14.0 10.0 %all-to-all-done.recv_ref = bf16[8,160,128]{2,1,0:T(8,128)(2,1)S(1)} async-done(((bf16[8,160,128]{2,1,0:T(8,128)(2,1)}), bf16[8,160,128]{2,1,0:T(8,128)(2,1)S(1)}, u32[]{:S(2)}, u32[]{:S(2)}) %all-to-all-start) | async-done | bytes 327712 | tf_op jit(solution)/shard_map/all_to_all | solution.py:494
  24.1 0.0 collective-permute-done.refs_0_
  24.1 0.0 collective-permute-start.2
  24.1 0.0 copy-done.6
  24.2 0.1 broadcast_select_fusion.4
  24.3 0.2 concatenate.3.conv_ref
  24.5 0.0 collective-permute-done.1.refs_1_
  24.5 0.0 copy-done.3
  24.6 3.2 %near.1 = (f32[768,256]{1,0:T(8,128)S(1)}, bf16[2,8,64,768]{3,2,1,0:T(8,128)(2,1)S(1)}, f32[512,512]{1,0:T(8,128)S(1)}, bf16[9,192,384]{2,1,0:T(8,128)(2,1)S(1)}, bf16[2,256,2048]{2,1,0:T(8,128)(2,1)S(1)}) custom-call(s32[1]{0:T(128)} %bitcast.info_ref, bf16[8,160,128]{2,1,0:T(8,128)(2,1)S(1)} %all-to-all-done.recv_ref, ...), custom_call_target="tpu_custom_call" | custom-call | flops 4000000000 | bytes 10000000 | tf_op jit(solution)/shard_map/near/pallas_call | solution.py:505
  27.8 0.0 copy-start
  27.8 0.0 copy-start.4
  27.8 0.0 collective-permute-done.2.refs_1_
  27.8 1.8 %far.1 = (f32[8,8,128]{2,1,0:T(8,128)S(1)}, bf16[2,6,64,256]{3,2,1,0:T(8,128)(2,1)S(1)}) custom-call(s32[1]{0:T(128)} %bitcast.info_ref, f32[768,256]{1,0:T(8,128)S(1)} %get-tuple-element.27.near_ref, bf16[2,8,64,768]{3,2,1,0:T(8,128)(2,1)S(1)} %get-tuple-element.28.views, bf16[9,96,384]{2,1,0:T(8,128)(2,1)S(1)} %collective-permute-done.refs_0_, ...), custom_call_target="tpu_custom_call" | custom-call | tf_op jit(solution)/shard_map/far/pallas_call | solution.py:521
  29.6 10.1 %all_to_all.15.sums_ref = f32[8,8,128]{2,1,0:T(8,128)S(1)} all-to-all(f32[8,8,128]{2,1,0:T(8,128)S(1)} %get-tuple-element.30), channel_id=1, replica_groups=mesh['dp'=4,'mp'=8] {'mp'}, dimensions={0} | all-to-all | bytes 65536 | tf_op jit(solution)/shard_map/all_to_all | solution.py:533
  39.7 0.0 copy-done
  39.7 0.0 copy-done.4
  39.7 0.0 copy-start.1
  39.7 0.0 copy-start.2
  39.7 0.0 copy-start.5
  39.7 4.7 %backward.1 = (f32[1]{0:T(128)}, bf16[8,96,128]{2,1,0:T(8,128)(2,1)S(1)}) custom-call(s32[1]{0:T(128)} %bitcast.info_ref, f32[8,8,128]{2,1,0:T(8,128)S(1)} %all_to_all.15.sums_ref, bf16[384,1024]{1,0:T(8,128)(2,1)S(1)} %copy-done, f32[1,1024]{1,0:T(1,128)S(1)} %copy-done.4, bf16[2,6,64,256]{3,2,1,0:T(8,128)(2,1)S(1)} %get-tuple-element.31.second_ref, ...), custom_call_target="tpu_custom_call" | custom-call | tf_op jit(solution)/shard_map/backward/pallas_call | solution.py:535
  44.4 10.2 %all_to_all.16.recv_ref = bf16[8,96,128]{2,1,0:T(8,128)(2,1)S(1)} all-to-all(bf16[8,96,128]{2,1,0:T(8,128)(2,1)S(1)} %get-tuple-element.36), channel_id=1, replica_groups=mesh['dp'=4,'mp'=8] {'mp'}, dimensions={0} | all-to-all | bytes 393216 | tf_op jit(solution)/shard_map/all_to_all | solution.py:547
  54.6 0.0 copy-done.1
  54.6 0.3 token_.1
  54.9 0.6 collective-permute-start.4
  55.5 0.0 collective-permute-start.3
  55.5 0.0 copy-done.2
  55.5 0.0 copy-done.5
  55.5 1.2 %hidden_grad.1 = bf16[512,640]{1,0:T(8,128)(2,1)} custom-call(bf16[512,64]{1,0:T(8,128)(2,1)S(1)} %get-tuple-element.39.tokens_ref, bf16[64,640]{1,0:T(8,128)(2,1)S(1)} %bitcast.8, f32[1,640]{1,0:T(1,128)S(1)} %copy-done.5), custom_call_target="tpu_custom_call" | custom-call | tf_op jit(solution)/shard_map/hidden_grad/pallas_call | solution.py:561
  56.7 2.7 %collective-permute-done.4 = bf16[64,640]{1,0:T(8,128)(2,1)S(1)} collective-permute-done((bf16[64,640]{1,0:T(8,128)(2,1)S(1)}, bf16[64,640]{1,0:T(8,128)(2,1)S(1)}, u32[]{:S(2)}, u32[]{:S(2)}) %collective-permute-start.4) | collective-permute-done | bytes 81952 | tf_op jit(solution)/shard_map/ppermute | solution.py:401
  59.4 0.0 collective-permute-start.5
  59.4 0.0 collective-permute-done.3
  59.4 1.3 %collective-permute-done.5 = bf16[64,640]{1,0:T(8,128)(2,1)S(1)} collective-permute-done((bf16[64,640]{1,0:T(8,128)(2,1)S(1)}, bf16[64,640]{1,0:T(8,128)(2,1)S(1)}, u32[]{:S(2)}, u32[]{:S(2)}) %collective-permute-start.5) | collective-permute-done | bytes 81952 | tf_op jit(solution)/shard_map/ppermute | solution.py:401
  60.7 0.7 %add_bitcast_fusion = f32[640,64]{0,1:T(8,128)} fusion(bf16[64,640]{1,0:T(8,128)(2,1)S(1)} %collective-permute-done.5, bf16[64,640]{1,0:T(8,128)(2,1)S(1)} %collective-permute-done.4, bf16[64,640]{1,0:T(8,128)(2,1)S(1)} %collective-permute-done.3, bf16[64,640]{1,0:T(8,128)(2,1)S(1)} %get-tuple-element.38), kind=kLoop, calls=%fused_computation.1 | loop fusion | flops 286720 | bytes 491520 | tf_op jit(solution)/shard_map/transpose | solution.py:571
  (2 shorter events, 0.0 us)
Async XLA Ops:
  0.6 23.4 %copy-start.6 = (bf16[16,27,384]{2,0,1:T(8,128)(2,1)S(1)}, bf16[16,27,384]{2,0,1:T(8,128)(2,1)}, u32[]{:S(2)}) copy-start(bf16[16,27,384]{2,0,1:T(8,128)(2,1)} %param.13) | copy-start | bytes 995332
  2.2 22.4 %copy-start.3 = (bf16[576,256]{1,0:T(8,128)(2,1)S(1)}, bf16[576,256]{1,0:T(8,128)(2,1)}, u32[]{:S(2)}) copy-start(bf16[576,256]{1,0:T(8,128)(2,1)} %constant.56.clone.pick_ref) | copy-start | bytes 884740
  2.2 21.9 %collective-permute-start = (bf16[9,96,384]{2,1,0:T(8,128)(2,1)S(1)}, bf16[9,96,384]{2,1,0:T(8,128)(2,1)S(1)}, u32[]{:S(2)}, u32[]{:S(2)}) collective-permute-start(bf16[9,96,384]{2,1,0:T(8,128)(2,1)S(1)} %pack.1.refs_0_), channel_id=1, source_target_pairs={{0,16},{8,24},{16,0},{24,8},{1,17},{9,25},{17,1},{25,9},{2,18},{10... | collective-permute-start | bytes 1990664 | tf_op jit(solution)/shard_map/ppermute | solution.py:401
  8.2 15.9 %all-to-all-start = ((bf16[8,160,128]{2,1,0:T(8,128)(2,1)}), bf16[8,160,128]{2,1,0:T(8,128)(2,1)S(1)}, u32[]{:S(2)}, u32[]{:S(2)}) async-start(bf16[8,160,128]{2,1,0:T(8,128)(2,1)} %get-tuple-element.24), calls=%async_computation | async-start | bytes 655360 | tf_op jit(solution)/shard_map/all_to_all | solution.py:494
  14.0 10.5 %collective-permute-start.1 = (bf16[9,96,384]{2,1,0:T(8,128)(2,1)S(1)}, bf16[9,96,384]{2,1,0:T(8,128)(2,1)}, u32[]{:S(2)}, u32[]{:S(2)}) collective-permute-start(bf16[9,96,384]{2,1,0:T(8,128)(2,1)S(1)} %pack.1.refs_0_), channel_id=1, source_target_pairs={{0,8},{8,0},{16,24},{24,16},{1,9},{9,1},{17,25},{25,17},{2,10},{10... | collective-permute-start | bytes 1990664 | tf_op jit(solution)/shard_map/ppermute | solution.py:401
  24.1 3.7 %collective-permute-start.2 = (bf16[9,96,384]{2,1,0:T(8,128)(2,1)S(1)}, bf16[9,96,384]{2,1,0:T(8,128)(2,1)S(1)}, u32[]{:S(2)}, u32[]{:S(2)}) collective-permute-start(bf16[9,96,384]{2,1,0:T(8,128)(2,1)S(1)} %collective-permute-done.refs_0_), channel_id=1, source_target_pairs={{0,8},{8,0},{16,24},{24,16},{1,9},{9,1},{17,25},{25,17},{2,10},{10... | collective-permute-start | bytes 1990664 | tf_op jit(solution)/shard_map/ppermute | solution.py:401
  27.8 11.9 %copy-start = (bf16[384,1024]{1,0:T(8,128)(2,1)S(1)}, bf16[384,1024]{1,0:T(8,128)(2,1)}, u32[]{:S(2)}) copy-start(bf16[384,1024]{1,0:T(8,128)(2,1)} %patch_ref.1) | copy-start | bytes 2359300
  27.8 11.9 %copy-start.4 = (f32[1,1024]{1,0:T(1,128)S(1)}, f32[1,1024]{1,0:T(1,128)}, u32[]{:S(2)}) copy-start(f32[1,1024]{1,0:T(1,128)} %text_ref.1) | copy-start | bytes 12292
  39.7 14.9 %copy-start.1 = (bf16[512,640]{1,0:T(8,128)(2,1)S(1)}, bf16[512,640]{1,0:T(8,128)(2,1)}, u32[]{:S(2)}) copy-start(bf16[512,640]{1,0:T(8,128)(2,1)} %get-tuple-element.37.modulated_ref) | copy-start | bytes 1966084
  39.7 15.8 %copy-start.2 = (bf16[640,64]{0,1:T(8,128)(2,1)S(1)}, bf16[640,64]{0,1:T(8,128)(2,1)}, u32[]{:S(2)}) copy-start(bf16[640,64]{0,1:T(8,128)(2,1)} %param.12) | copy-start | bytes 245764
  39.7 15.8 %copy-start.5 = (f32[1,640]{1,0:T(1,128)S(1)}, f32[1,640]{1,0:T(1,128)}, u32[]{:S(2)}) copy-start(f32[1,640]{1,0:T(1,128)} %get-tuple-element.40.gain_ref) | copy-start | bytes 7684
  54.9 4.5 %collective-permute-start.4 = (bf16[64,640]{1,0:T(8,128)(2,1)S(1)}, bf16[64,640]{1,0:T(8,128)(2,1)S(1)}, u32[]{:S(2)}, u32[]{:S(2)}) collective-permute-start(bf16[64,640]{1,0:T(8,128)(2,1)S(1)} %get-tuple-element.38), channel_id=1, source_target_pairs={{0,16},{8,24},{16,0},{24,8},{1,17},{9,25},{17,1},{25,9},{2,18},{10... | collective-permute-start | bytes 245768 | tf_op jit(solution)/shard_map/ppermute | solution.py:401
  55.5 3.9 %collective-permute-start.3 = (bf16[64,640]{1,0:T(8,128)(2,1)S(1)}, bf16[64,640]{1,0:T(8,128)(2,1)S(1)}, u32[]{:S(2)}, u32[]{:S(2)}) collective-permute-start(bf16[64,640]{1,0:T(8,128)(2,1)S(1)} %get-tuple-element.38), channel_id=1, source_target_pairs={{0,8},{8,0},{16,24},{24,16},{1,9},{9,1},{17,25},{25,17},{2,10},{10... | collective-permute-start | bytes 245768 | tf_op jit(solution)/shard_map/ppermute | solution.py:401
  59.4 1.3 %collective-permute-start.5 = (bf16[64,640]{1,0:T(8,128)(2,1)S(1)}, bf16[64,640]{1,0:T(8,128)(2,1)S(1)}, u32[]{:S(2)}, u32[]{:S(2)}) collective-permute-start(bf16[64,640]{1,0:T(8,128)(2,1)S(1)} %collective-permute-done.4), channel_id=1, source_target_pairs={{0,8},{8,0},{16,24},{24,16},{1,9},{9,1},{17,25},{25,17},{2,10},{10... | collective-permute-start | bytes 245768 | tf_op jit(solution)/shard_map/ppermute | solution.py:401

commit v7 on v6

--- a/solution.py
+++ b/solution.py
@@ -422,15 +422,6 @@
     return [blocks[held] for held in sorted(blocks)], unit
 
 
-def half_sum(term):
-    total, flip = term.astype(F32), 1
-    while flip < lax.axis_size("dp") // 2:
-        other = exchange(term, "dp", flip)
-        total = total + other.astype(F32)
-        term, flip = total.astype(BF), 2 * flip
-    return total
-
-
 def local_channels(weight, unit):
     count = lax.axis_size("dp") // unit
     place = lax.axis_index("dp") // unit
@@ -557,7 +548,12 @@
         compiler_params=params(8),
         name="token",
     )(contributions, modulated)
-    from_far = exchange(head_term, "dp", far)
+    flip = 1
+    while flip < far:
+        other = exchange(head_term, "dp", flip)
+        head_term = (head_term.astype(F32) + other.astype(F32)).astype(BF)
+        flip *= 2
+    head_other = exchange(head_term, "dp", far)
     hidden_grad = pl.pallas_call(
         hidden_kernel,
         in_specs=[VMEM] * 3,
@@ -566,8 +562,7 @@
         compiler_params=params(8),
         name="hidden_grad",
     )(token_grad, head_rows, gain)
-    hidden_grad, from_far = lax.optimization_barrier((hidden_grad, from_far))
-    head_grad = half_sum(head_term) + half_sum(from_far)
+    head_grad = head_term.astype(F32) + head_other.astype(F32)
     return (reward, head_grad.T, hidden_grad)
 
 

time: 61.7 us -> 61.8 us (level)
    ppermute x6 -> x5, starting transfers between devices: 3.63 us -> 3.69 us  [exchange(): return lax.ppermute(block, axis, [(i, i ^ flip) for i in range(count)])]
    ppermute x6 -> x5, waiting for transfers between devices: 4.01 us -> 4.07 us  [exchange(): return lax.ppermute(block, axis, [(i, i ^ flip) for i in range(count)])]
  transfers between devices with their start and end apart: 7 -> 6, of which waited for: 3 -> 3; matrix products, arithmetic and copies ran while one was open for 1% -> 1% of each run, Pallas kernels for 11% -> 11%
where the time goes in v7:
time: 61.8 us; the launch traced here: 61.5 us
  blocking collectives  20.3 us (33%)
  Pallas kernels  15 us (24%)
  waiting for transfers between devices  14.1 us (23%)
  starting transfers between devices  9.53 us (15%)
  between operations  1.5 us (2%)
  other arithmetic  0.84 us (1%)
    all_to_all x1, blocking collectives, body(): contributions = lax.all_to_all(contribution, 'mp', 0, 0, tiled=True)  10.2 us
    all_to_all x1, blocking collectives, body(): all_sums = lax.all_to_all(sums, 'mp', 0, 0, tiled=True)  10.1 us
    all_to_all x1, waiting for transfers between devices, body(): recv = lax.all_to_all(send, 'mp', 0, 0, tiled=True)  10 us
    all_to_all x1, starting transfers between devices, body(): recv = lax.all_to_all(send, 'mp', 0, 0, tiled=True)  5.84 us
    pallas_call x1, Pallas kernels, body(): pl.pallas_call(functools.partial(backward_kernel, parts, cells), in_specs...  4.67 us
    ppermute x5, waiting for transfers between devices, exchange(): return lax.ppermute(block, axis, [(i, i ^ flip) for i in range(count)])  4.07 us
    ppermute x5, starting transfers between devices, exchange(): return lax.ppermute(block, axis, [(i, i ^ flip) for i in range(count)])  3.69 us
    pallas_call x1, Pallas kernels, body(): pl.pallas_call(functools.partial(near_kernel, parts, blocks), in_specs=[S...  3.2 us
  transfers between devices with their start and end apart: 6, of which 3 were waited for; matrix products, arithmetic and copies ran while one was open for 1% of the time, Pallas kernels for 11%

profile of v7, /device:TPU:0, one launch (start us, length us, event | category | flops | bytes accessed | tf_op | source)
XLA Modules:
  0.0 61.5 jit_solution(14166426198390956882)
XLA Ops:
  0.6 0.0 copy-start.6
  0.6 1.5 %pack.1.refs_0_ = bf16[9,96,384]{2,1,0:T(8,128)(2,1)S(1)} custom-call(bf16[27,96,384]{2,1,0:T(8,128)(2,1)} %bitcast.9), custom_call_target="tpu_custom_call" | custom-call | tf_op jit(solution)/shard_map/pack/pallas_call | solution.py:456
  2.2 0.0 copy-start.3
  2.2 3.0 %collective-permute-start = (bf16[9,96,384]{2,1,0:T(8,128)(2,1)S(1)}, bf16[9,96,384]{2,1,0:T(8,128)(2,1)S(1)}, u32[]{:S(2)}, u32[]{:S(2)}) collective-permute-start(bf16[9,96,384]{2,1,0:T(8,128)(2,1)S(1)} %pack.1.refs_0_), channel_id=1, source_target_pairs={{0,16},{8,24},{16,0},{24,8},{1,17},{9,25},{17,1},{25,9},{2,18},{10... | collective-permute-start | bytes 1990664 | tf_op jit(solution)/shard_map/ppermute | solution.py:401
  5.8 2.3 %head.1 = (bf16[512,640]{1,0:T(8,128)(2,1)}, f32[1,640]{1,0:T(1,128)}, bf16[8,160,128]{2,1,0:T(8,128)(2,1)}) custom-call(s32[1]{0:T(128)S(6)} %copy.12.step_ref, bf16[512,640]{1,0:T(8,128)(2,1)} %hidden_hbm.1, bf16[50,2,640]{2,1,0:T(2,128)(2,1)} %mod_hbm.1, bf16[64,640]{1,0:T(8,128)(2,1)} %bitcast.7), custom_call_target="tpu_custom_call" | custom-call | tf_op jit(solution)/shard_map/head/pallas_call | solution.py:466
  8.2 5.8 %all-to-all-start = ((bf16[8,160,128]{2,1,0:T(8,128)(2,1)}), bf16[8,160,128]{2,1,0:T(8,128)(2,1)S(1)}, u32[]{:S(2)}, u32[]{:S(2)}) async-start(bf16[8,160,128]{2,1,0:T(8,128)(2,1)} %get-tuple-element.22), calls=%async_computation | async-start | bytes 655360 | tf_op jit(solution)/shard_map/all_to_all | solution.py:485
  14.0 0.0 collective-permute-start.1
  14.0 10.0 %all-to-all-done.recv_ref = bf16[8,160,128]{2,1,0:T(8,128)(2,1)S(1)} async-done(((bf16[8,160,128]{2,1,0:T(8,128)(2,1)}), bf16[8,160,128]{2,1,0:T(8,128)(2,1)S(1)}, u32[]{:S(2)}, u32[]{:S(2)}) %all-to-all-start) | async-done | bytes 327712 | tf_op jit(solution)/shard_map/all_to_all | solution.py:485
  24.1 0.0 collective-permute-done.refs_0_
  24.1 0.0 collective-permute-start.2
  24.1 0.0 copy-done.6
  24.1 0.1 broadcast_select_fusion.4
  24.3 0.2 concatenate.3.conv_ref
  24.5 0.0 collective-permute-done.1.refs_1_
  24.5 0.0 copy-done.3
  24.5 3.2 %near.1 = (f32[768,256]{1,0:T(8,128)S(1)}, bf16[2,8,64,768]{3,2,1,0:T(8,128)(2,1)S(1)}, f32[512,512]{1,0:T(8,128)S(1)}, bf16[9,192,384]{2,1,0:T(8,128)(2,1)S(1)}, bf16[2,256,2048]{2,1,0:T(8,128)(2,1)S(1)}) custom-call(s32[1]{0:T(128)} %bitcast.info_ref, bf16[8,160,128]{2,1,0:T(8,128)(2,1)S(1)} %all-to-all-done.recv_ref, ...), custom_call_target="tpu_custom_call" | custom-call | flops 4000000000 | bytes 10000000 | tf_op jit(solution)/shard_map/near/pallas_call | solution.py:496
  27.7 0.0 copy-start
  27.8 0.0 copy-start.4
  27.8 0.0 collective-permute-done.2.refs_1_
  27.8 1.8 %far.1 = (f32[8,8,128]{2,1,0:T(8,128)S(1)}, bf16[2,6,64,256]{3,2,1,0:T(8,128)(2,1)S(1)}) custom-call(s32[1]{0:T(128)} %bitcast.info_ref, f32[768,256]{1,0:T(8,128)S(1)} %get-tuple-element.25.near_ref, bf16[2,8,64,768]{3,2,1,0:T(8,128)(2,1)S(1)} %get-tuple-element.26.views, bf16[9,96,384]{2,1,0:T(8,128)(2,1)S(1)} %collective-permute-done.refs_0_, ...), custom_call_target="tpu_custom_call" | custom-call | tf_op jit(solution)/shard_map/far/pallas_call | solution.py:512
  29.6 10.1 %all_to_all.15.sums_ref = f32[8,8,128]{2,1,0:T(8,128)S(1)} all-to-all(f32[8,8,128]{2,1,0:T(8,128)S(1)} %get-tuple-element.28), channel_id=1, replica_groups=mesh['dp'=4,'mp'=8] {'mp'}, dimensions={0} | all-to-all | bytes 65536 | tf_op jit(solution)/shard_map/all_to_all | solution.py:524
  39.6 0.0 copy-done
  39.7 0.0 copy-done.4
  39.7 0.0 copy-start.1
  39.7 0.0 copy-start.2
  39.7 0.0 copy-start.5
  39.7 4.7 %backward.1 = (f32[1]{0:T(128)}, bf16[8,96,128]{2,1,0:T(8,128)(2,1)S(1)}) custom-call(s32[1]{0:T(128)} %bitcast.info_ref, f32[8,8,128]{2,1,0:T(8,128)S(1)} %all_to_all.15.sums_ref, bf16[384,1024]{1,0:T(8,128)(2,1)S(1)} %copy-done, f32[1,1024]{1,0:T(1,128)S(1)} %copy-done.4, bf16[2,6,64,256]{3,2,1,0:T(8,128)(2,1)S(1)} %get-tuple-element.29.second_ref, ...), custom_call_target="tpu_custom_call" | custom-call | tf_op jit(solution)/shard_map/backward/pallas_call | solution.py:526
  44.4 10.2 %all_to_all.16.recv_ref = bf16[8,96,128]{2,1,0:T(8,128)(2,1)S(1)} all-to-all(bf16[8,96,128]{2,1,0:T(8,128)(2,1)S(1)} %get-tuple-element.34), channel_id=1, replica_groups=mesh['dp'=4,'mp'=8] {'mp'}, dimensions={0} | all-to-all | bytes 393216 | tf_op jit(solution)/shard_map/all_to_all | solution.py:538
  54.5 0.0 copy-done.1
  54.5 0.3 token_.1
  54.9 0.1 collective-permute-start.3
  55.0 1.3 %collective-permute-done.3 = bf16[64,640]{1,0:T(8,128)(2,1)S(1)} collective-permute-done((bf16[64,640]{1,0:T(8,128)(2,1)S(1)}, bf16[64,640]{1,0:T(8,128)(2,1)S(1)}, u32[]{:S(2)}, u32[]{:S(2)}) %collective-permute-start.3) | collective-permute-done | bytes 81952 | tf_op jit(solution)/shard_map/ppermute | solution.py:401
  56.2 0.6 collective-permute-start.4
  56.9 0.0 copy-done.2
  56.9 0.0 copy-done.5
  56.9 1.2 %hidden_grad.1 = bf16[512,640]{1,0:T(8,128)(2,1)} custom-call(bf16[512,64]{1,0:T(8,128)(2,1)S(1)} %get-tuple-element.37.tokens_ref, bf16[64,640]{1,0:T(8,128)(2,1)S(1)} %bitcast.8, f32[1,640]{1,0:T(1,128)S(1)} %copy-done.5), custom_call_target="tpu_custom_call" | custom-call | tf_op jit(solution)/shard_map/hidden_grad/pallas_call | solution.py:557
  58.0 2.8 %collective-permute-done.4 = bf16[64,640]{1,0:T(8,128)(2,1)S(1)} collective-permute-done((bf16[64,640]{1,0:T(8,128)(2,1)S(1)}, bf16[64,640]{1,0:T(8,128)(2,1)S(1)}, u32[]{:S(2)}, u32[]{:S(2)}) %collective-permute-start.4) | collective-permute-done | bytes 81952 | tf_op jit(solution)/shard_map/ppermute | solution.py:401
  60.8 0.7 %add_bitcast_fusion = f32[640,64]{0,1:T(8,128)} fusion(bf16[64,640]{1,0:T(8,128)(2,1)S(1)} %collective-permute-done.4, bf16[64,640]{1,0:T(8,128)(2,1)S(1)} %add_convert_fusion), kind=kLoop, calls=%fused_computation.1 | loop fusion | flops 122880 | bytes 327680 | tf_op jit(solution)/shard_map/transpose | solution.py:566
  (3 shorter events, 0.1 us)
Async XLA Ops:
  0.6 23.4 %copy-start.6 = (bf16[16,27,384]{2,0,1:T(8,128)(2,1)S(1)}, bf16[16,27,384]{2,0,1:T(8,128)(2,1)}, u32[]{:S(2)}) copy-start(bf16[16,27,384]{2,0,1:T(8,128)(2,1)} %param.13) | copy-start | bytes 995332
  2.2 22.4 %copy-start.3 = (bf16[576,256]{1,0:T(8,128)(2,1)S(1)}, bf16[576,256]{1,0:T(8,128)(2,1)}, u32[]{:S(2)}) copy-start(bf16[576,256]{1,0:T(8,128)(2,1)} %constant.56.clone.pick_ref) | copy-start | bytes 884740
  2.2 21.9 %collective-permute-start = (bf16[9,96,384]{2,1,0:T(8,128)(2,1)S(1)}, bf16[9,96,384]{2,1,0:T(8,128)(2,1)S(1)}, u32[]{:S(2)}, u32[]{:S(2)}) collective-permute-start(bf16[9,96,384]{2,1,0:T(8,128)(2,1)S(1)} %pack.1.refs_0_), channel_id=1, source_target_pairs={{0,16},{8,24},{16,0},{24,8},{1,17},{9,25},{17,1},{25,9},{2,18},{10... | collective-permute-start | bytes 1990664 | tf_op jit(solution)/shard_map/ppermute | solution.py:401
  8.2 15.9 %all-to-all-start = ((bf16[8,160,128]{2,1,0:T(8,128)(2,1)}), bf16[8,160,128]{2,1,0:T(8,128)(2,1)S(1)}, u32[]{:S(2)}, u32[]{:S(2)}) async-start(bf16[8,160,128]{2,1,0:T(8,128)(2,1)} %get-tuple-element.22), calls=%async_computation | async-start | bytes 655360 | tf_op jit(solution)/shard_map/all_to_all | solution.py:485
  14.0 10.5 %collective-permute-start.1 = (bf16[9,96,384]{2,1,0:T(8,128)(2,1)S(1)}, bf16[9,96,384]{2,1,0:T(8,128)(2,1)}, u32[]{:S(2)}, u32[]{:S(2)}) collective-permute-start(bf16[9,96,384]{2,1,0:T(8,128)(2,1)S(1)} %pack.1.refs_0_), channel_id=1, source_target_pairs={{0,8},{8,0},{16,24},{24,16},{1,9},{9,1},{17,25},{25,17},{2,10},{10... | collective-permute-start | bytes 1990664 | tf_op jit(solution)/shard_map/ppermute | solution.py:401
  24.1 3.7 %collective-permute-start.2 = (bf16[9,96,384]{2,1,0:T(8,128)(2,1)S(1)}, bf16[9,96,384]{2,1,0:T(8,128)(2,1)S(1)}, u32[]{:S(2)}, u32[]{:S(2)}) collective-permute-start(bf16[9,96,384]{2,1,0:T(8,128)(2,1)S(1)} %collective-permute-done.refs_0_), channel_id=1, source_target_pairs={{0,8},{8,0},{16,24},{24,16},{1,9},{9,1},{17,25},{25,17},{2,10},{10... | collective-permute-start | bytes 1990664 | tf_op jit(solution)/shard_map/ppermute | solution.py:401
  27.7 11.9 %copy-start = (bf16[384,1024]{1,0:T(8,128)(2,1)S(1)}, bf16[384,1024]{1,0:T(8,128)(2,1)}, u32[]{:S(2)}) copy-start(bf16[384,1024]{1,0:T(8,128)(2,1)} %patch_ref.1) | copy-start | bytes 2359300
  27.8 11.9 %copy-start.4 = (f32[1,1024]{1,0:T(1,128)S(1)}, f32[1,1024]{1,0:T(1,128)}, u32[]{:S(2)}) copy-start(f32[1,1024]{1,0:T(1,128)} %text_ref.1) | copy-start | bytes 12292
  39.7 14.9 %copy-start.1 = (bf16[512,640]{1,0:T(8,128)(2,1)S(1)}, bf16[512,640]{1,0:T(8,128)(2,1)}, u32[]{:S(2)}) copy-start(bf16[512,640]{1,0:T(8,128)(2,1)} %get-tuple-element.35.modulated_ref) | copy-start | bytes 1966084
  39.7 17.2 %copy-start.2 = (bf16[640,64]{0,1:T(8,128)(2,1)S(1)}, bf16[640,64]{0,1:T(8,128)(2,1)}, u32[]{:S(2)}) copy-start(bf16[640,64]{0,1:T(8,128)(2,1)} %param.12) | copy-start | bytes 245764
  39.7 17.2 %copy-start.5 = (f32[1,640]{1,0:T(1,128)S(1)}, f32[1,640]{1,0:T(1,128)}, u32[]{:S(2)}) copy-start(f32[1,640]{1,0:T(1,128)} %get-tuple-element.38.gain_ref) | copy-start | bytes 7684
  54.9 1.3 %collective-permute-start.3 = (bf16[64,640]{1,0:T(8,128)(2,1)S(1)}, bf16[64,640]{1,0:T(8,128)(2,1)S(1)}, u32[]{:S(2)}, u32[]{:S(2)}) collective-permute-start(bf16[64,640]{1,0:T(8,128)(2,1)S(1)} %get-tuple-element.36), channel_id=1, source_target_pairs={{0,8},{8,0},{16,24},{24,16},{1,9},{9,1},{17,25},{25,17},{2,10},{10... | collective-permute-start | bytes 245768 | tf_op jit(solution)/shard_map/ppermute | solution.py:401
  56.2 4.6 %collective-permute-start.4 = (bf16[64,640]{1,0:T(8,128)(2,1)S(1)}, bf16[64,640]{1,0:T(8,128)(2,1)S(1)}, u32[]{:S(2)}, u32[]{:S(2)}) collective-permute-start(bf16[64,640]{1,0:T(8,128)(2,1)S(1)} %add_convert_fusion), channel_id=1, source_target_pairs={{0,16},{8,24},{16,0},{24,8},{1,17},{9,25},{17,1},{25,9},{2,18},{10... | collective-permute-start | bytes 245768 | tf_op jit(solution)/shard_map/ppermute | solution.py:401

commit v8 on v6

--- a/solution.py
+++ b/solution.py
@@ -75,9 +75,12 @@
             packed[pair, :, 2 * TILE :] = jnp.where(lane < TILE // 2, left, right).astype(BF)
 
 
+def modulate(hidden, modulation):
+    return (hidden.astype(F32) * modulation[0:1] + modulation[1:2]).astype(BF)
+
+
 def head_kernel(
-    parts, step_ref, hidden_hbm, mod_hbm, head_hbm, modulated_ref, gain_ref, send_ref, hidden_ref, mod_ref, head_ref,
-    sems
+    parts, step_ref, hidden_hbm, mod_hbm, head_hbm, modulation_ref, send_ref, hidden_ref, mod_ref, head_ref, sems
 ):
     copies = [
         pltpu.make_async_copy(hidden_hbm, hidden_ref, sems.at[0]),
@@ -89,10 +92,9 @@
     for copy in copies:
         copy.wait()
     mod = mod_ref[step_ref[0]].astype(F32)
-    gain = 1.0 + mod[1:2]
-    modulated = (hidden_ref[...].astype(F32) * gain + mod[0:1]).astype(BF)
-    modulated_ref[...] = modulated
-    gain_ref[...] = gain
+    modulation = jnp.concatenate([1.0 + mod[1:2], mod[0:1]], axis=0)
+    modulation_ref[...] = modulation
+    modulated = modulate(hidden_ref[...], modulation)
     terms = dot_nt(modulated, head_ref[...])
     half = terms.shape[0] // 2
     wide = jnp.concatenate([terms[:half], terms[half:]], axis=1)
@@ -368,7 +370,7 @@
         send_ref[part] = result
 
 
-def token_kernel(parts, recv_ref, modulated_ref, tokens_ref, head_ref):
+def token_kernel(parts, recv_ref, hidden_ref, modulation_ref, tokens_ref, head_ref):
     n = PAIR_COLS
     lanes = recv_ref.shape[2]
     sums = [recv_ref[i].astype(F32) + recv_ref[i + 1].astype(F32) for i in range(0, parts, 2)]
@@ -384,11 +386,11 @@
     tokens = jnp.concatenate([wide[:, : lanes // 2], wide[:, lanes // 2 :]], axis=0)
     flipped = jnp.transpose(tokens).astype(BF)
     tokens_ref[...] = tokens.astype(BF)
-    head_ref[...] = dot(flipped, modulated_ref[...]).astype(BF)
-
-
-def hidden_kernel(tokens_ref, head_ref, gain_ref, out_ref):
-    out_ref[...] = (dot(tokens_ref[...], head_ref[...]) * gain_ref[...]).astype(BF)
+    head_ref[...] = dot(flipped, modulate(hidden_ref[...], modulation_ref[...])).astype(BF)
+
+
+def hidden_kernel(tokens_ref, head_ref, modulation_ref, out_ref):
+    out_ref[...] = (dot(tokens_ref[...], head_ref[...]) * modulation_ref[0:1]).astype(BF)
 
 
 VMEM = pl.BlockSpec(memory_space=pltpu.VMEM)
@@ -472,13 +474,12 @@
         name="pack",
     )(taps)
     distant = exchange(packed, "dp", far)
-    modulated, gain, send = pl.pallas_call(
+    modulation, send = pl.pallas_call(
         functools.partial(head_kernel, parts),
         in_specs=[SMEM] + [HBM] * 3,
-        out_specs=[VMEM] * 3,
+        out_specs=[VMEM] * 2,
         out_shape=[
-            jax.ShapeDtypeStruct((tokens, depth), BF),
-            jax.ShapeDtypeStruct((1, depth), F32),
+            jax.ShapeDtypeStruct((2, depth), F32),
             jax.ShapeDtypeStruct((parts, 5 * n, 2 * features), BF),
         ],
         scratch_shapes=[
@@ -548,7 +549,7 @@
 
     token_grad, head_term = pl.pallas_call(
         functools.partial(token_kernel, parts),
-        in_specs=[VMEM, VMEM],
+        in_specs=[VMEM] * 3,
         out_specs=[VMEM, VMEM],
         out_shape=[
             jax.ShapeDtypeStruct((tokens, features), BF),
@@ -556,7 +557,7 @@
         ],
         compiler_params=params(8),
         name="token",
-    )(contributions, modulated)
+    )(contributions, hidden, modulation)
     from_far = exchange(head_term, "dp", far)
     hidden_grad = pl.pallas_call(
         hidden_kernel,
@@ -565,7 +566,7 @@
         out_shape=jax.ShapeDtypeStruct((tokens, depth), BF),
         compiler_params=params(8),
         name="hidden_grad",
-    )(token_grad, head_rows, gain)
+    )(token_grad, head_rows, modulation)
     hidden_grad, from_far = lax.optimization_barrier((hidden_grad, from_far))
     head_grad = half_sum(head_term) + half_sum(from_far)
     return (reward, head_grad.T, hidden_grad)

time: 61.7 us -> 61.7 us (level)
  no operation moved by 1% of the time
where the time goes in v8:
time: 61.7 us; the launch traced here: 61.4 us
  blocking collectives  20.3 us (33%)
  Pallas kernels  14.9 us (24%)
  waiting for transfers between devices  14.1 us (23%)
  starting transfers between devices  9.45 us (15%)
  between operations  1.48 us (2%)
  other arithmetic  0.84 us (1%)
    all_to_all x1, blocking collectives, body(): contributions = lax.all_to_all(contribution, 'mp', 0, 0, tiled=True)  10.2 us
    all_to_all x1, blocking collectives, body(): all_sums = lax.all_to_all(sums, 'mp', 0, 0, tiled=True)  10.1 us
    all_to_all x1, waiting for transfers between devices, body(): recv = lax.all_to_all(send, 'mp', 0, 0, tiled=True)  10 us
    all_to_all x1, starting transfers between devices, body(): recv = lax.all_to_all(send, 'mp', 0, 0, tiled=True)  5.85 us
    pallas_call x1, Pallas kernels, body(): pl.pallas_call(functools.partial(backward_kernel, parts, cells), in_specs...  4.67 us
    ppermute x6, waiting for transfers between devices, exchange(): return lax.ppermute(block, axis, [(i, i ^ flip) for i in range(count)])  4.04 us
    ppermute x6, starting transfers between devices, exchange(): return lax.ppermute(block, axis, [(i, i ^ flip) for i in range(count)])  3.6 us
    pallas_call x1, Pallas kernels, body(): pl.pallas_call(functools.partial(near_kernel, parts, blocks), in_specs=[S...  3.21 us
  transfers between devices with their start and end apart: 7, of which 3 were waited for; matrix products, arithmetic and copies ran while one was open for 1% of the time, Pallas kernels for 11%

profile of v8, /device:TPU:0, one launch (start us, length us, event | category | flops | bytes accessed | tf_op | source)
XLA Modules:
  0.0 61.4 jit_solution(12411937170726982535)
XLA Ops:
  0.6 0.0 copy-start.6
  0.6 1.5 %pack.1.refs_0_ = bf16[9,96,384]{2,1,0:T(8,128)(2,1)S(1)} custom-call(bf16[27,96,384]{2,1,0:T(8,128)(2,1)} %bitcast.9), custom_call_target="tpu_custom_call" | custom-call | tf_op jit(solution)/shard_map/pack/pallas_call | solution.py:467
  2.2 0.0 copy-start.3
  2.2 3.0 %collective-permute-start = (bf16[9,96,384]{2,1,0:T(8,128)(2,1)S(1)}, bf16[9,96,384]{2,1,0:T(8,128)(2,1)S(1)}, u32[]{:S(2)}, u32[]{:S(2)}) collective-permute-start(bf16[9,96,384]{2,1,0:T(8,128)(2,1)S(1)} %pack.1.refs_0_), channel_id=1, source_target_pairs={{0,16},{8,24},{16,0},{24,8},{1,17},{9,25},{17,1},{25,9},{2,18},{10... | collective-permute-start | bytes 1990664 | tf_op jit(solution)/shard_map/ppermute | solution.py:403
  5.8 2.3 %head.1 = (f32[2,640]{1,0:T(2,128)}, bf16[8,160,128]{2,1,0:T(8,128)(2,1)}) custom-call(s32[1]{0:T(128)S(6)} %copy.12.step_ref, bf16[512,640]{1,0:T(8,128)(2,1)} %hidden_ref.1, bf16[50,2,640]{2,1,0:T(2,128)(2,1)} %mod_hbm.1, bf16[64,640]{1,0:T(8,128)(2,1)} %bitcast.7), custom_call_target="tpu_custom_call" | custom-call | tf_op jit(solution)/shard_map/head/pallas_call | solution.py:477
  8.1 5.9 %all-to-all-start = ((bf16[8,160,128]{2,1,0:T(8,128)(2,1)}), bf16[8,160,128]{2,1,0:T(8,128)(2,1)S(1)}, u32[]{:S(2)}, u32[]{:S(2)}) async-start(bf16[8,160,128]{2,1,0:T(8,128)(2,1)} %get-tuple-element.23), calls=%async_computation | async-start | bytes 655360 | tf_op jit(solution)/shard_map/all_to_all | solution.py:495
  14.0 0.0 collective-permute-start.1
  14.0 10.0 %all-to-all-done.recv_ref = bf16[8,160,128]{2,1,0:T(8,128)(2,1)S(1)} async-done(((bf16[8,160,128]{2,1,0:T(8,128)(2,1)}), bf16[8,160,128]{2,1,0:T(8,128)(2,1)S(1)}, u32[]{:S(2)}, u32[]{:S(2)}) %all-to-all-start) | async-done | bytes 327712 | tf_op jit(solution)/shard_map/all_to_all | solution.py:495
  24.0 0.0 collective-permute-done.refs_0_
  24.0 0.0 collective-permute-start.2
  24.0 0.0 copy-done.6
  24.1 0.1 broadcast_select_fusion.4
  24.3 0.2 concatenate.3.conv_ref
  24.5 0.0 collective-permute-done.1.refs_1_
  24.5 0.0 copy-done.3
  24.5 3.2 %near.1 = (f32[768,256]{1,0:T(8,128)S(1)}, bf16[2,8,64,768]{3,2,1,0:T(8,128)(2,1)S(1)}, f32[512,512]{1,0:T(8,128)S(1)}, bf16[9,192,384]{2,1,0:T(8,128)(2,1)S(1)}, bf16[2,256,2048]{2,1,0:T(8,128)(2,1)S(1)}) custom-call(s32[1]{0:T(128)} %bitcast.info_ref, bf16[8,160,128]{2,1,0:T(8,128)(2,1)S(1)} %all-to-all-done.recv_ref, ...), custom_call_target="tpu_custom_call" | custom-call | flops 4000000000 | bytes 10000000 | tf_op jit(solution)/shard_map/near/pallas_call | solution.py:506
  27.7 0.0 copy-start.1
  27.7 0.0 copy-start.5
  27.8 0.0 collective-permute-done.2.refs_1_
  27.8 1.8 %far.1 = (f32[8,8,128]{2,1,0:T(8,128)S(1)}, bf16[2,6,64,256]{3,2,1,0:T(8,128)(2,1)S(1)}) custom-call(s32[1]{0:T(128)} %bitcast.info_ref, f32[768,256]{1,0:T(8,128)S(1)} %get-tuple-element.26.near_ref, bf16[2,8,64,768]{3,2,1,0:T(8,128)(2,1)S(1)} %get-tuple-element.27.views, bf16[9,96,384]{2,1,0:T(8,128)(2,1)S(1)} %collective-permute-done.refs_0_, ...), custom_call_target="tpu_custom_call" | custom-call | tf_op jit(solution)/shard_map/far/pallas_call | solution.py:522
  29.5 10.1 %all_to_all.15.sums_ref = f32[8,8,128]{2,1,0:T(8,128)S(1)} all-to-all(f32[8,8,128]{2,1,0:T(8,128)S(1)} %get-tuple-element.29), channel_id=1, replica_groups=mesh['dp'=4,'mp'=8] {'mp'}, dimensions={0} | all-to-all | bytes 65536 | tf_op jit(solution)/shard_map/all_to_all | solution.py:534
  39.6 0.0 copy-done.1
  39.6 0.0 copy-done.5
  39.6 0.0 copy-start
  39.6 0.0 copy-start.4
  39.6 0.0 copy-start.2
  39.6 4.7 %backward.1 = (f32[1]{0:T(128)}, bf16[8,96,128]{2,1,0:T(8,128)(2,1)S(1)}) custom-call(s32[1]{0:T(128)} %bitcast.info_ref, f32[8,8,128]{2,1,0:T(8,128)S(1)} %all_to_all.15.sums_ref, bf16[384,1024]{1,0:T(8,128)(2,1)S(1)} %copy-done.1, f32[1,1024]{1,0:T(1,128)S(1)} %copy-done.5, bf16[2,6,64,256]{3,2,1,0:T(8,128)(2,1)S(1)} %get-tuple-element.30.second_ref, ...), custom_call_target="tpu_custom_call" | custom-call | tf_op jit(solution)/shard_map/backward/pallas_call | solution.py:536
  44.3 10.2 %all_to_all.16.recv_ref = bf16[8,96,128]{2,1,0:T(8,128)(2,1)S(1)} all-to-all(bf16[8,96,128]{2,1,0:T(8,128)(2,1)S(1)} %get-tuple-element.35), channel_id=1, replica_groups=mesh['dp'=4,'mp'=8] {'mp'}, dimensions={0} | all-to-all | bytes 393216 | tf_op jit(solution)/shard_map/all_to_all | solution.py:548
  54.5 0.0 copy-done
  54.5 0.0 copy-done.4
  54.5 0.3 token_.1
  54.9 0.6 collective-permute-start.4
  55.4 0.0 collective-permute-start.3
  55.4 0.0 copy-done.2
  55.5 1.2 %hidden_grad.1 = bf16[512,640]{1,0:T(8,128)(2,1)} custom-call(bf16[512,64]{1,0:T(8,128)(2,1)S(1)} %get-tuple-element.38.tokens_ref, bf16[64,640]{1,0:T(8,128)(2,1)S(1)} %bitcast.8, f32[2,640]{1,0:T(2,128)S(1)} %copy-done.4), custom_call_target="tpu_custom_call" | custom-call | tf_op jit(solution)/shard_map/hidden_grad/pallas_call | solution.py:562
  56.6 2.8 %collective-permute-done.4 = bf16[64,640]{1,0:T(8,128)(2,1)S(1)} collective-permute-done((bf16[64,640]{1,0:T(8,128)(2,1)S(1)}, bf16[64,640]{1,0:T(8,128)(2,1)S(1)}, u32[]{:S(2)}, u32[]{:S(2)}) %collective-permute-start.4) | collective-permute-done | bytes 81952 | tf_op jit(solution)/shard_map/ppermute | solution.py:403
  59.4 0.0 collective-permute-start.5
  59.4 0.0 collective-permute-done.3
  59.4 1.3 %collective-permute-done.5 = bf16[64,640]{1,0:T(8,128)(2,1)S(1)} collective-permute-done((bf16[64,640]{1,0:T(8,128)(2,1)S(1)}, bf16[64,640]{1,0:T(8,128)(2,1)S(1)}, u32[]{:S(2)}, u32[]{:S(2)}) %collective-permute-start.5) | collective-permute-done | bytes 81952 | tf_op jit(solution)/shard_map/ppermute | solution.py:403
  60.6 0.7 %add_bitcast_fusion = f32[640,64]{0,1:T(8,128)} fusion(bf16[64,640]{1,0:T(8,128)(2,1)S(1)} %collective-permute-done.5, bf16[64,640]{1,0:T(8,128)(2,1)S(1)} %collective-permute-done.4, bf16[64,640]{1,0:T(8,128)(2,1)S(1)} %collective-permute-done.3, bf16[64,640]{1,0:T(8,128)(2,1)S(1)} %get-tuple-element.37), kind=kLoop, calls=%fused_computation.1 | loop fusion | flops 286720 | bytes 491520 | tf_op jit(solution)/shard_map/transpose | solution.py:572
  (2 shorter events, 0.0 us)
Async XLA Ops:
  0.6 23.4 %copy-start.6 = (bf16[16,27,384]{2,0,1:T(8,128)(2,1)S(1)}, bf16[16,27,384]{2,0,1:T(8,128)(2,1)}, u32[]{:S(2)}) copy-start(bf16[16,27,384]{2,0,1:T(8,128)(2,1)} %param.13) | copy-start | bytes 995332
  2.2 22.3 %copy-start.3 = (bf16[576,256]{1,0:T(8,128)(2,1)S(1)}, bf16[576,256]{1,0:T(8,128)(2,1)}, u32[]{:S(2)}) copy-start(bf16[576,256]{1,0:T(8,128)(2,1)} %constant.56.clone.pick_ref) | copy-start | bytes 884740
  2.2 21.8 %collective-permute-start = (bf16[9,96,384]{2,1,0:T(8,128)(2,1)S(1)}, bf16[9,96,384]{2,1,0:T(8,128)(2,1)S(1)}, u32[]{:S(2)}, u32[]{:S(2)}) collective-permute-start(bf16[9,96,384]{2,1,0:T(8,128)(2,1)S(1)} %pack.1.refs_0_), channel_id=1, source_target_pairs={{0,16},{8,24},{16,0},{24,8},{1,17},{9,25},{17,1},{25,9},{2,18},{10... | collective-permute-start | bytes 1990664 | tf_op jit(solution)/shard_map/ppermute | solution.py:403
  8.1 15.9 %all-to-all-start = ((bf16[8,160,128]{2,1,0:T(8,128)(2,1)}), bf16[8,160,128]{2,1,0:T(8,128)(2,1)S(1)}, u32[]{:S(2)}, u32[]{:S(2)}) async-start(bf16[8,160,128]{2,1,0:T(8,128)(2,1)} %get-tuple-element.23), calls=%async_computation | async-start | bytes 655360 | tf_op jit(solution)/shard_map/all_to_all | solution.py:495
  14.0 10.5 %collective-permute-start.1 = (bf16[9,96,384]{2,1,0:T(8,128)(2,1)S(1)}, bf16[9,96,384]{2,1,0:T(8,128)(2,1)}, u32[]{:S(2)}, u32[]{:S(2)}) collective-permute-start(bf16[9,96,384]{2,1,0:T(8,128)(2,1)S(1)} %pack.1.refs_0_), channel_id=1, source_target_pairs={{0,8},{8,0},{16,24},{24,16},{1,9},{9,1},{17,25},{25,17},{2,10},{10... | collective-permute-start | bytes 1990664 | tf_op jit(solution)/shard_map/ppermute | solution.py:403
  24.0 3.7 %collective-permute-start.2 = (bf16[9,96,384]{2,1,0:T(8,128)(2,1)S(1)}, bf16[9,96,384]{2,1,0:T(8,128)(2,1)S(1)}, u32[]{:S(2)}, u32[]{:S(2)}) collective-permute-start(bf16[9,96,384]{2,1,0:T(8,128)(2,1)S(1)} %collective-permute-done.refs_0_), channel_id=1, source_target_pairs={{0,8},{8,0},{16,24},{24,16},{1,9},{9,1},{17,25},{25,17},{2,10},{10... | collective-permute-start | bytes 1990664 | tf_op jit(solution)/shard_map/ppermute | solution.py:403
  27.7 11.9 %copy-start.1 = (bf16[384,1024]{1,0:T(8,128)(2,1)S(1)}, bf16[384,1024]{1,0:T(8,128)(2,1)}, u32[]{:S(2)}) copy-start(bf16[384,1024]{1,0:T(8,128)(2,1)} %patch_ref.1) | copy-start | bytes 2359300
  27.7 11.9 %copy-start.5 = (f32[1,1024]{1,0:T(1,128)S(1)}, f32[1,1024]{1,0:T(1,128)}, u32[]{:S(2)}) copy-start(f32[1,1024]{1,0:T(1,128)} %text_ref.1) | copy-start | bytes 12292
  39.6 14.9 %copy-start = (bf16[512,640]{1,0:T(8,128)(2,1)S(1)}, bf16[512,640]{1,0:T(8,128)(2,1)}, u32[]{:S(2)}) copy-start(bf16[512,640]{1,0:T(8,128)(2,1)} %hidden_ref.1) | copy-start | bytes 1966084
  39.6 14.9 %copy-start.4 = (f32[2,640]{1,0:T(2,128)S(1)}, f32[2,640]{1,0:T(2,128)}, u32[]{:S(2)}) copy-start(f32[2,640]{1,0:T(2,128)} %get-tuple-element.36.modulation_ref) | copy-start | bytes 15364
  39.6 15.8 %copy-start.2 = (bf16[640,64]{0,1:T(8,128)(2,1)S(1)}, bf16[640,64]{0,1:T(8,128)(2,1)}, u32[]{:S(2)}) copy-start(bf16[640,64]{0,1:T(8,128)(2,1)} %param.12) | copy-start | bytes 245764
  54.9 4.5 %collective-permute-start.4 = (bf16[64,640]{1,0:T(8,128)(2,1)S(1)}, bf16[64,640]{1,0:T(8,128)(2,1)S(1)}, u32[]{:S(2)}, u32[]{:S(2)}) collective-permute-start(bf16[64,640]{1,0:T(8,128)(2,1)S(1)} %get-tuple-element.37), channel_id=1, source_target_pairs={{0,16},{8,24},{16,0},{24,8},{1,17},{9,25},{17,1},{25,9},{2,18},{10... | collective-permute-start | bytes 245768 | tf_op jit(solution)/shard_map/ppermute | solution.py:403
  55.4 3.9 %collective-permute-start.3 = (bf16[64,640]{1,0:T(8,128)(2,1)S(1)}, bf16[64,640]{1,0:T(8,128)(2,1)S(1)}, u32[]{:S(2)}, u32[]{:S(2)}) collective-permute-start(bf16[64,640]{1,0:T(8,128)(2,1)S(1)} %get-tuple-element.37), channel_id=1, source_target_pairs={{0,8},{8,0},{16,24},{24,16},{1,9},{9,1},{17,25},{25,17},{2,10},{10... | collective-permute-start | bytes 245768 | tf_op jit(solution)/shard_map/ppermute | solution.py:403
  59.4 1.3 %collective-permute-start.5 = (bf16[64,640]{1,0:T(8,128)(2,1)S(1)}, bf16[64,640]{1,0:T(8,128)(2,1)S(1)}, u32[]{:S(2)}, u32[]{:S(2)}) collective-permute-start(bf16[64,640]{1,0:T(8,128)(2,1)S(1)} %collective-permute-done.4), channel_id=1, source_target_pairs={{0,8},{8,0},{16,24},{24,16},{1,9},{9,1},{17,25},{25,17},{2,10},{10... | collective-permute-start | bytes 245768 | tf_op jit(solution)/shard_map/ppermute | solution.py:403
